TPU v7x, 32 devices: a whole 2x2x4 slice. The times are simulated.
32 devices in a mesh: enc: 4 (over y, x), seq: 8 (over z, core).
Axes of the slice: x: 2, y: 2, z: 4, core: 2. Of those that a mesh axis runs over, the one named last changes fastest.
Arguments:
- qkv: bfloat16 [16, 512, 3840], P('enc', 'seq'), may hold values from -6 to 6
- resid: bfloat16 [16, 512, 1280], P('enc', 'seq'), may hold values from -6 to 6
- block_count: int32 [4, 8], P('enc', 'seq'), may hold values from 2 to 4, as said below
- send_count: int32 [4, 8], P('enc', 'seq'), may hold values from 0 to 1, as said below
- send_slot: int32 [4, 384], P('enc', 'seq'), may hold values from 0 to 47, as said below
- lm_row: int32 [4, 384], P('enc', 'seq'), may hold values from -1 to 47, as said below
- out_weight: bfloat16 [1280, 1280], replicated, may hold values from -0.15625 to 0.15625
- out_bias: bfloat16 [1280], replicated, may hold values from -3 to 3
- norm_gain: bfloat16 [1280], replicated, may hold values from 0.25 to 1.75
Outputs:
- lm_tokens: bfloat16 [4, 384, 5120], P('enc', 'seq')
Inputs may be any that keep to these rules, and one draw needn't show every extreme that they name: send_count is at most 1; a device's live slots come first. block_count[e, g] = 3 + send_count[e, g] - send_count[(e - 1) mod 4, g]. `send_slot`: values of one device are distinct; with o = (s - g) mod 8 and finv(o) = 2 * o for o < 4, else 2 * (o - 4) + 1, the device at seq index g uses slot s * 6 + k exactly when k * 8 + finv(o) < 48. `lm_row`: at seq index s, with o and finv as for send_slot, arriving slot g * 6 + k holds -1 exactly when k * 8 + finv((s - g) mod 8) >= 48; the other slots hold each of 0 to 47 once.
All inputs are finite; a program needn't handle non-finite values.
Results may differ from a plain program's by a relative error of at most 0.0036.
Values may be sent and summed in bfloat16 or wider, within the bound.
No kernel may reach another device: no remote copies, remote signals or barrier semaphores. Data moves between devices by JAX's collectives and lax.ppermute only.
A program may use at most 64 MiB of HBM per device.

v0:
```python
import functools
import math

import jax
import jax.numpy as jnp
from jax import lax
from jax.experimental import pallas as pl
from jax.experimental.pallas import tpu as pltpu
from jax.sharding import PartitionSpec as P

HEADS = 16
WIN = 64
LANES = 128
GROUP = 4
EPS = 1e-6
CORES = 2

NT = (((1,), (1,)), ((), ()))


def dot32(a, b):
    return jnp.dot(a, b, preferred_element_type=jnp.float32)


def one_hot(match):
    return match.astype(jnp.float32).astype(jnp.bfloat16)


def attend(q, k, v, out_ref, row0, width):
    head = width // HEADS
    rate = 1.0 / math.sqrt(head)
    totals = [None] * (width // LANES)
    sums = [None] * (width // LANES)
    first_half = lax.broadcasted_iota(jnp.int32, (WIN, 2 * WIN), 1) < WIN
    for pair in range(HEADS // 2):
        start = 2 * pair * head
        lo = start // LANES * LANES
        hi = -(-(start + 2 * head) // LANES) * LANES
        column = lax.broadcasted_iota(jnp.int32, (2 * WIN, hi - lo), 1) + lo
        row = lax.broadcasted_iota(jnp.int32, (2 * WIN, hi - lo), 0)
        begin = jnp.where(row < WIN, start, start + head)
        mask = one_hot((column >= begin) & (column < begin + head))
        kw, vw = k(lo, hi), v(lo, hi)
        keys = jnp.concatenate([kw, kw], axis=0) * mask
        values = jnp.concatenate([vw, vw], axis=0) * mask
        scores = lax.dot_general(q(lo, hi), keys, NT, preferred_element_type=jnp.float32)
        top0 = jnp.max(jnp.where(first_half, scores, -jnp.inf), axis=1, keepdims=True)
        top1 = jnp.max(jnp.where(first_half, -jnp.inf, scores), axis=1, keepdims=True)
        raised = jnp.exp((scores - jnp.where(first_half, top0, top1)) * rate).astype(jnp.bfloat16)
        part = dot32(raised, values)
        norm = dot32(raised, mask)
        for tile in range(lo // LANES, hi // LANES):
            at = slice(tile * LANES - lo, (tile + 1) * LANES - lo)
            totals[tile] = part[:, at] if totals[tile] is None else totals[tile] + part[:, at]
            sums[tile] = norm[:, at] if sums[tile] is None else sums[tile] + norm[:, at]
    for tile in range(width // LANES):
        out_ref[row0 : row0 + WIN, tile * LANES : (tile + 1) * LANES] = (totals[tile] / sums[tile]).astype(
            jnp.bfloat16
        )


def encode(
    slot, qkv_hbm, resid_hbm, weight_hbm, bias_hbm, gain_hbm, out_ref,
    qkv, resid, weight, attended, hidden, bias_ref, gain_ref, sems,
):
    blocks = qkv.shape[0]
    width = resid.shape[2]
    at = pl.ds(slot, blocks)
    pairs = [
        (qkv_hbm.at[at], qkv), (weight_hbm, weight), (resid_hbm.at[at], resid), (bias_hbm, bias_ref), (gain_hbm, gain_ref)
    ]
    copies = [pltpu.make_async_copy(a, b, sems.at[i]) for i, (a, b) in enumerate(pairs)]
    for copy in copies:
        copy.start()
    copies[0].wait()
    for b in range(blocks):
        attend(
            lambda lo, hi, b=b: qkv[b, :, lo:hi],
            lambda lo, hi, b=b: qkv[b, :, width + lo : width + hi],
            lambda lo, hi, b=b: qkv[b, :, 2 * width + lo : 2 * width + hi],
            attended, b * WIN, width,
        )
    for copy in copies[1:]:
        copy.wait()
    rows = blocks * WIN
    squares = jnp.zeros((rows, 1), jnp.float32)
    step = 2 * LANES
    for lo in range(0, width, step):
        cols = slice(lo, lo + step)
        h = dot32(attended[...], weight[:, cols])
        h = h + bias_ref[cols].astype(jnp.float32).reshape(1, step)
        h = h + resid[:, :, cols].reshape(rows, step).astype(jnp.float32)
        hidden[:, cols] = h
        squares = squares + jnp.sum(h * h, axis=1, keepdims=True)
    scale = lax.rsqrt(squares * (1.0 / width) + EPS)
    for lo in range(0, width, step):
        cols = slice(lo, lo + step)
        gain = gain_ref[cols].astype(jnp.float32).reshape(1, step)
        out_ref[:, cols] = (hidden[:, cols] * scale * gain).astype(jnp.bfloat16)


def lent_kernel(count_ref, qkv_hbm, resid_hbm, weight_hbm, bias_hbm, gain_hbm, out_ref, *scratch):
    encode(count_ref[0, 0] - 1, qkv_hbm, resid_hbm, weight_hbm, bias_hbm, gain_hbm, out_ref, *scratch)


def split_index(index, n_seq, cap):
    step = index // (GROUP * cap)
    rest = index - step * (GROUP * cap)
    patch = rest // cap
    return step, patch, rest - patch * cap


def own_kernel(
    n_seq, cap, peer, count_ref, send_ref, me_ref, slot_ref, row_ref,
    qkv_hbm, resid_hbm, weight_hbm, bias_hbm, gain_hbm,
    packed_ref, borrow_ref, place_ref, normed, *scratch,
):
    rows = normed.shape[0]
    slots = n_seq * cap
    sent = slots * GROUP
    tokens = rows // GROUP
    me = me_ref[0, 0]
    encode(0, qkv_hbm, resid_hbm, weight_hbm, bias_hbm, gain_hbm, normed, *scratch)

    step, patch, rank = split_index(lax.broadcasted_iota(jnp.int32, (sent, 1), 0), n_seq, cap)
    row_code = (peer(me, step, 1) * cap + rank) * GROUP + patch
    token = lax.broadcasted_iota(jnp.int32, (tokens, rows), 0)
    column = lax.broadcasted_iota(jnp.int32, (tokens, rows), 1)
    spread = one_hot((column >= token * GROUP) & (column < (token + 1) * GROUP))
    slot = jnp.broadcast_to(slot_ref[...].astype(jnp.float32), (16, tokens)).astype(jnp.bfloat16)
    slot = dot32(slot, spread)[:1].astype(jnp.int32)
    index = lax.broadcasted_iota(jnp.int32, (1, rows), 1)
    col_code = slot * GROUP + jnp.bitwise_and(index, GROUP - 1)
    kept = (count_ref[0, 0] - send_ref[0, 0]) * WIN
    last = rows - WIN
    own = one_hot(row_code == jnp.where(index < kept, col_code, -1))
    packed_ref[...] = dot32(own, normed[...]).astype(jnp.bfloat16)
    borrow_ref[...] = one_hot(row_code == jnp.where(kept > last, -1, col_code[:, last:]))

    step, patch, rank = split_index(lax.broadcasted_iota(jnp.int32, (1, sent), 1), n_seq, cap)
    arrive = peer(me, step, -1) * cap + rank
    pick = one_hot(lax.broadcasted_iota(jnp.int32, (slots, sent), 0) == arrive)
    target = jnp.broadcast_to(row_ref[...].astype(jnp.float32), (16, slots)).astype(jnp.bfloat16)
    target = dot32(target, pick)[:1].astype(jnp.int32)
    out_row = lax.broadcasted_iota(jnp.int32, (tokens, sent), 0)
    for j in range(GROUP):
        place_ref[j * tokens : (j + 1) * tokens, :] = one_hot((target == out_row) & (patch == j))


def encode_call(kernel, blocks, scalars, slots, qkv, resid, weight, bias, gain, out_shape, extra):
    width = resid.shape[2]
    rows = blocks * WIN
    vmem = pl.BlockSpec(memory_space=pltpu.VMEM)
    smem = pl.BlockSpec(memory_space=pltpu.SMEM)
    hbm = pl.BlockSpec(memory_space=pltpu.HBM)
    return pl.pallas_call(
        kernel,
        out_shape=out_shape,
        in_specs=[smem] * len(scalars) + [vmem] * len(slots) + [hbm] * 5,
        out_specs=jax.tree.map(lambda _: vmem, out_shape),
        scratch_shapes=extra
        + [
            pltpu.VMEM((blocks, WIN, 3 * width), jnp.bfloat16),
            pltpu.VMEM((blocks, WIN, width), jnp.bfloat16),
            pltpu.VMEM((width, width), jnp.bfloat16),
            pltpu.VMEM((rows, width), jnp.bfloat16),
            pltpu.VMEM((rows, width), jnp.float32),
            pltpu.VMEM((width,), jnp.bfloat16),
            pltpu.VMEM((width,), jnp.bfloat16),
            pltpu.SemaphoreType.DMA((5,)),
        ],
        compiler_params=pltpu.CompilerParams(vmem_limit_bytes=24 << 20),
        cost_estimate=pl.CostEstimate(
            flops=2 * rows * width * width + 8 * rows * WIN * width,
            bytes_accessed=2 * (width * width + 5 * rows * width),
            transcendentals=rows * WIN * HEADS,
        ),
    )(*scalars, *slots, *(pltpu.with_memory_space_constraint(a, pltpu.HBM) for a in (qkv, resid, weight, bias, gain)))


def pack_kernel(packed_ref, borrow_ref, borrowed_ref, *out_refs):
    total = packed_ref[...].astype(jnp.float32) + dot32(borrow_ref[...], borrowed_ref[...])
    chunk = out_refs[0].shape[0]
    for step, out_ref in enumerate(out_refs):
        out_ref[...] = total[step * chunk : (step + 1) * chunk].astype(jnp.bfloat16)


def place_kernel(place_ref, *refs):
    *in_refs, out_hbm, out, sems = refs
    tokens = out.shape[0]
    chunks = [ref[...].astype(jnp.float32) for ref in in_refs]
    arrived = chunks[0] if len(chunks) == 1 else jnp.concatenate(chunks, axis=0)
    arrived = arrived.astype(jnp.bfloat16)
    width = arrived.shape[1]
    copies = []
    for j in range(GROUP):
        cols = slice(j * width, (j + 1) * width)
        out[:, cols] = dot32(place_ref[j * tokens : (j + 1) * tokens, :], arrived).astype(jnp.bfloat16)
        copies.append(pltpu.make_async_copy(out.at[:, cols], out_hbm.at[:, cols], sems.at[j]))
        copies[-1].start()
    for copy in copies:
        copy.wait()


def exchange_steps(n_seq):
    n_z = n_seq // CORES
    steps = [(dz, dc) for dz in range(n_z) for dc in range(CORES) if (dz, dc) != (0, 0)]
    return [(0, 0)] + sorted(steps, key=lambda s: (s != (1, 0), abs(s[0] - n_z / 2), s[1], s[0]))


def chip_peer(n_seq, me, step, sign):
    n_z = n_seq // CORES
    offset = jnp.zeros_like(step)
    flip = jnp.zeros_like(step)
    for i, (dz, dc) in enumerate(exchange_steps(n_seq)):
        offset = jnp.where(step == i, dz, offset)
        flip = jnp.where(step == i, dc, flip)
    z = me // CORES + sign * offset
    z = jnp.where(z >= n_z, z - n_z, jnp.where(z < 0, z + n_z, z))
    return z * CORES + jnp.bitwise_xor(jnp.bitwise_and(me, 1), flip)


def per_device(
    qkv, resid, block_count, send_count, send_slot, lm_row, out_weight, out_bias, norm_gain
):
    width = resid.shape[2]
    row_total = send_slot.shape[1]
    tokens = WIN // GROUP
    blocks = row_total // tokens
    n_seq = lax.axis_size("seq")
    n_enc = lax.axis_size("enc")
    slots = lm_row.shape[1]
    cap = slots // n_seq
    chunk = GROUP * cap
    sent = slots * GROUP
    vmem = pl.BlockSpec(memory_space=pltpu.VMEM)
    small = pltpu.CompilerParams(vmem_limit_bytes=16 << 20)

    def rows_of(count, columns=width):
        return jax.ShapeDtypeStruct((count, columns), jnp.bfloat16)

    data = (qkv, resid, out_weight, out_bias, norm_gain)
    lent = encode_call(lent_kernel, 1, [block_count], [], *data, rows_of(WIN), [])
    borrowed = lax.ppermute(lent, "enc", [((i - 1) % n_enc, i) for i in range(n_enc)])

    by_steps = chunk % 8 == 0 and n_seq % CORES == 0
    peer = functools.partial(chip_peer, n_seq) if by_steps else lambda me, step, sign: step
    me = lax.axis_index("seq").astype(jnp.int32).reshape(1, 1)
    packed, borrow, place = encode_call(
        functools.partial(own_kernel, n_seq, cap, peer), blocks,
        [block_count, send_count, me], [send_slot, lm_row], *data,
        (rows_of(sent), rows_of(sent, WIN), rows_of(GROUP * row_total, sent)),
        [pltpu.VMEM((row_total * GROUP, width), jnp.bfloat16)],
    )
    pieces = n_seq if by_steps else 1
    outgoing = pl.pallas_call(
        pack_kernel,
        out_shape=[rows_of(sent // pieces)] * pieces,
        in_specs=[vmem] * 3,
        out_specs=[vmem] * pieces,
        compiler_params=small,
    )(packed, borrow, borrowed)

    if by_steps:
        n_z = n_seq // CORES
        arrived = [outgoing[0]]
        for part, (dz, dc) in list(zip(outgoing, exchange_steps(n_seq)))[1:]:
            route = [(i, (i // CORES + dz) % n_z * CORES + (i + dc) % CORES) for i in range(n_seq)]
            arrived.append(lax.ppermute(part, "seq", route))
    else:
        arrived = [
            lax.all_to_all(
                outgoing[0].reshape(n_seq, chunk, width), "seq", split_axis=0, concat_axis=0, tiled=True
            ).reshape(sent, width)
        ]
    placed = pl.pallas_call(
        place_kernel,
        out_shape=rows_of(row_total, GROUP * width),
        in_specs=[vmem] * (1 + pieces),
        out_specs=pl.BlockSpec(memory_space=pltpu.HBM),
        scratch_shapes=[pltpu.VMEM((row_total, GROUP * width), jnp.bfloat16), pltpu.SemaphoreType.DMA((GROUP,))],
        compiler_params=small,
    )(place, *arrived)
    return placed[None]


def solution(mesh):
    placed = (
        P("enc", "seq", None),
        P("enc", "seq", None),
        P("enc", "seq"),
        P("enc", "seq"),
        P("enc", "seq"),
        P("enc", "seq"),
        P(),
        P(),
        P(),
    )
    return jax.shard_map(
        per_device, mesh=mesh, in_specs=placed, out_specs=P("enc", "seq", None), check_vma=False
    )
```

profile of v0, /device:TPU:0, one launch (start us, length us, event | category | flops | bytes accessed | tf_op | source)
XLA Modules:
  0.0 26.4 jit_solution(1664072711327863018)
XLA Ops:
  0.0 0.0 copy-start.1
  0.0 0.0 copy-start
  0.7 3.0 %shard_map.92 = bf16[64,1280]{1,0:T(8,128)(2,1)S(1)} custom-call(s32[1,1]{1,0:T(1,128)S(6)} %copy.10.count_ref, bf16[4,64,3840]{2,1,0:T(8,128)(2,1)} %qkv_hbm.3, bf16[4,64,1280]{2,1,0:T(8,128)(2,1)} %resid_hbm.3, bf16[1280,1280]{1,0:T(8,128)(2,1)} %weight_hbm.3, bf16[1280]{0:T(1024)(128)(2,1)} %bias_hbm.3, bf16[1280]{0:T(1024)(128)(2,1)} %gain_hbm.3), custom_call_target="tpu_custom_call" | custom-call | flops 251658240 | bytes 4096000 | tf_op jit(solution)/shard_map/pallas_call | solution.py:156
  3.7 3.0 %collective-permute-start = (bf16[64,1280]{1,0:T(8,128)(2,1)S(1)}, bf16[64,1280]{1,0:T(8,128)(2,1)S(1)}, u32[]{:S(2)}, u32[]{:S(2)}) collective-permute-start(bf16[64,1280]{1,0:T(8,128)(2,1)S(1)} %shard_map.92), channel_id=1, source_target_pairs={{24,0},{0,8},{8,16},{16,24},{25,1},{1,9},{9,17},{17,25},{26,2},{2,... | collective-permute-start | bytes 491528 | tf_op jit(solution)/shard_map/ppermute | solution.py:244
  7.3 0.0 copy-done.1
  7.4 0.0 copy-done
  7.4 4.3 %shard_map.91 = (bf16[192,1280]{1,0:T(8,128)(2,1)S(1)}, bf16[192,64]{1,0:T(8,128)(2,1)S(1)}, bf16[192,192]{1,0:T(8,128)(2,1)S(1)}) custom-call(s32[1,1]{1,0:T(1,128)S(6)} %copy.10.count_ref, s32[1,1]{1,0:T(1,128)S(6)} %copy.11.send_ref, s32[1,1]{1,0:T(1,128)} %bitcast.me_ref, s32[1,48]{1,0:T(1,128)S(1)} %copy-done, s32[1,48]{1,0:T(1,128)S(1)} %copy-done.1, ...), custom_call_target="tpu_custom_call" | custom-call | flops 754974720 | bytes 5734400 | tf_op jit(solution)/shard_map/pallas_call | solution.py:156
  11.7 0.2 collective-permute-done.borrowed_ref
  11.9 0.3 shard_map.93
  12.1 1.8 %collective-permute-start.1 = (bf16[24,1280]{1,0:T(8,128)(2,1)S(1)}, bf16[24,1280]{1,0:T(8,128)(2,1)S(1)}, u32[]{:S(2)}, u32[]{:S(2)}) collective-permute-start(bf16[24,1280]{1,0:T(8,128)(2,1)S(1)} %get-tuple-element.20), channel_id=1, source_target_pairs={{0,2},{1,3},{2,4},{3,5},{4,6},{5,7},{6,0},{7,1},{8,10},{9,11},{10,... | collective-permute-start | bytes 184328 | tf_op jit(solution)/shard_map/ppermute | solution.py:269
  13.9 2.6 %collective-permute-start.2 = (bf16[24,1280]{1,0:T(8,128)(2,1)S(1)}, bf16[24,1280]{1,0:T(8,128)(2,1)S(1)}, u32[]{:S(2)}, u32[]{:S(2)}) collective-permute-start(bf16[24,1280]{1,0:T(8,128)(2,1)S(1)} %get-tuple-element.21), channel_id=1, source_target_pairs={{0,4},{1,5},{2,6},{3,7},{4,0},{5,1},{6,2},{7,3},{8,12},{9,13},{10,... | collective-permute-start | bytes 184328 | tf_op jit(solution)/shard_map/ppermute | solution.py:269
  16.5 0.0 collective-permute-start.3
  16.5 1.3 %collective-permute-start.4 = (bf16[24,1280]{1,0:T(8,128)(2,1)S(1)}, bf16[24,1280]{1,0:T(8,128)(2,1)S(1)}, u32[]{:S(2)}, u32[]{:S(2)}) collective-permute-start(bf16[24,1280]{1,0:T(8,128)(2,1)S(1)} %get-tuple-element.23), channel_id=1, source_target_pairs={{0,6},{1,7},{2,0},{3,1},{4,2},{5,3},{6,4},{7,5},{8,14},{9,15},{10,... | collective-permute-start | bytes 184328 | tf_op jit(solution)/shard_map/ppermute | solution.py:269
  17.9 0.5 %collective-permute-start.5 = (bf16[24,1280]{1,0:T(8,128)(2,1)S(1)}, bf16[24,1280]{1,0:T(8,128)(2,1)S(1)}, u32[]{:S(2)}, u32[]{:S(2)}) collective-permute-start(bf16[24,1280]{1,0:T(8,128)(2,1)S(1)} %get-tuple-element.24), channel_id=1, source_target_pairs={{0,3},{1,2},{2,5},{3,4},{4,7},{5,6},{6,1},{7,0},{8,11},{9,10},{10,... | collective-permute-start | bytes 184328 | tf_op jit(solution)/shard_map/ppermute | solution.py:269
  18.3 0.4 %collective-permute-done.1.refs_1_ = bf16[24,1280]{1,0:T(8,128)(2,1)S(1)} collective-permute-done((bf16[24,1280]{1,0:T(8,128)(2,1)S(1)}, bf16[24,1280]{1,0:T(8,128)(2,1)S(1)}, u32[]{:S(2)}, u32[]{:S(2)}) %collective-permute-start.1) | collective-permute-done | bytes 61472 | tf_op jit(solution)/shard_map/ppermute | solution.py:269
  18.7 2.7 %collective-permute-start.6 = (bf16[24,1280]{1,0:T(8,128)(2,1)S(1)}, bf16[24,1280]{1,0:T(8,128)(2,1)S(1)}, u32[]{:S(2)}, u32[]{:S(2)}) collective-permute-start(bf16[24,1280]{1,0:T(8,128)(2,1)S(1)} %get-tuple-element.25), channel_id=1, source_target_pairs={{0,7},{1,6},{2,1},{3,0},{4,3},{5,2},{6,5},{7,4},{8,15},{9,14},{10,... | collective-permute-start | bytes 184328 | tf_op jit(solution)/shard_map/ppermute | solution.py:269
  21.4 0.0 collective-permute-done.2.refs_2_
  21.4 0.9 %collective-permute-start.7 = (bf16[24,1280]{1,0:T(8,128)(2,1)S(1)}, bf16[24,1280]{1,0:T(8,128)(2,1)S(1)}, u32[]{:S(2)}, u32[]{:S(2)}) collective-permute-start(bf16[24,1280]{1,0:T(8,128)(2,1)S(1)} %get-tuple-element.26), channel_id=1, source_target_pairs={{0,1},{1,0},{2,3},{3,2},{4,5},{5,4},{6,7},{7,6},{8,9},{9,8},{10,11... | collective-permute-start | bytes 184328 | tf_op jit(solution)/shard_map/ppermute | solution.py:269
  22.4 1.2 %collective-permute-done.3.refs_3_ = bf16[24,1280]{1,0:T(8,128)(2,1)S(1)} collective-permute-done((bf16[24,1280]{1,0:T(8,128)(2,1)S(1)}, bf16[24,1280]{1,0:T(8,128)(2,1)S(1)}, u32[]{:S(2)}, u32[]{:S(2)}) %collective-permute-start.3) | collective-permute-done | bytes 61472 | tf_op jit(solution)/shard_map/ppermute | solution.py:269
  23.6 0.0 collective-permute-done.4.refs_4_
  23.6 0.0 collective-permute-done.5.refs_5_
  23.6 1.7 %collective-permute-done.6.refs_6_ = bf16[24,1280]{1,0:T(8,128)(2,1)S(1)} collective-permute-done((bf16[24,1280]{1,0:T(8,128)(2,1)S(1)}, bf16[24,1280]{1,0:T(8,128)(2,1)S(1)}, u32[]{:S(2)}, u32[]{:S(2)}) %collective-permute-start.6) | collective-permute-done | bytes 61472 | tf_op jit(solution)/shard_map/ppermute | solution.py:269
  25.2 0.0 collective-permute-done.7.refs_7_
  25.2 1.2 %shard_map.94 = bf16[48,5120]{1,0:T(8,128)(2,1)} custom-call(bf16[192,192]{1,0:T(8,128)(2,1)S(1)} %get-tuple-element.16.place_ref, bf16[24,1280]{1,0:T(8,128)(2,1)S(1)} %get-tuple-element.19.refs_0_, bf16[24,1280]{1,0:T(8,128)(2,1)S(1)} %collective-permute-done.1.refs_1_, bf16[24,1280]{1,0:T(8,128)(2,1)S(1)} %collective-permute-done.2.refs_2_, ...), custom_call_target="tpu_custom_call" | custom-call | tf_op jit(solution)/shard_map/pallas_call | solution.py:276
Async XLA Ops:
  0.0 7.3 %copy-start.1 = (s32[1,48]{1,0:T(1,128)S(1)}, s32[1,48]{1,0:T(1,128)}, u32[]{:S(2)}) copy-start(s32[1,48]{1,0:T(1,128)} %row_ref.1) | copy-start | bytes 580
  0.0 7.4 %copy-start = (s32[1,48]{1,0:T(1,128)S(1)}, s32[1,48]{1,0:T(1,128)}, u32[]{:S(2)}) copy-start(s32[1,48]{1,0:T(1,128)} %slot_ref.1) | copy-start | bytes 580
  3.7 8.1 %collective-permute-start = (bf16[64,1280]{1,0:T(8,128)(2,1)S(1)}, bf16[64,1280]{1,0:T(8,128)(2,1)S(1)}, u32[]{:S(2)}, u32[]{:S(2)}) collective-permute-start(bf16[64,1280]{1,0:T(8,128)(2,1)S(1)} %shard_map.92), channel_id=1, source_target_pairs={{24,0},{0,8},{8,16},{16,24},{25,1},{1,9},{9,17},{17,25},{26,2},{2,... | collective-permute-start | bytes 491528 | tf_op jit(solution)/shard_map/ppermute | solution.py:244
  12.1 6.6 %collective-permute-start.1 = (bf16[24,1280]{1,0:T(8,128)(2,1)S(1)}, bf16[24,1280]{1,0:T(8,128)(2,1)S(1)}, u32[]{:S(2)}, u32[]{:S(2)}) collective-permute-start(bf16[24,1280]{1,0:T(8,128)(2,1)S(1)} %get-tuple-element.20), channel_id=1, source_target_pairs={{0,2},{1,3},{2,4},{3,5},{4,6},{5,7},{6,0},{7,1},{8,10},{9,11},{10,... | collective-permute-start | bytes 184328 | tf_op jit(solution)/shard_map/ppermute | solution.py:269
  13.9 7.5 %collective-permute-start.2 = (bf16[24,1280]{1,0:T(8,128)(2,1)S(1)}, bf16[24,1280]{1,0:T(8,128)(2,1)S(1)}, u32[]{:S(2)}, u32[]{:S(2)}) collective-permute-start(bf16[24,1280]{1,0:T(8,128)(2,1)S(1)} %get-tuple-element.21), channel_id=1, source_target_pairs={{0,4},{1,5},{2,6},{3,7},{4,0},{5,1},{6,2},{7,3},{8,12},{9,13},{10,... | collective-permute-start | bytes 184328 | tf_op jit(solution)/shard_map/ppermute | solution.py:269
  16.5 7.0 %collective-permute-start.3 = (bf16[24,1280]{1,0:T(8,128)(2,1)S(1)}, bf16[24,1280]{1,0:T(8,128)(2,1)S(1)}, u32[]{:S(2)}, u32[]{:S(2)}) collective-permute-start(bf16[24,1280]{1,0:T(8,128)(2,1)S(1)} %get-tuple-element.22), channel_id=1, source_target_pairs={{0,5},{1,4},{2,7},{3,6},{4,1},{5,0},{6,3},{7,2},{8,13},{9,12},{10,... | collective-permute-start | bytes 184328 | tf_op jit(solution)/shard_map/ppermute | solution.py:269
  16.5 7.0 %collective-permute-start.4 = (bf16[24,1280]{1,0:T(8,128)(2,1)S(1)}, bf16[24,1280]{1,0:T(8,128)(2,1)S(1)}, u32[]{:S(2)}, u32[]{:S(2)}) collective-permute-start(bf16[24,1280]{1,0:T(8,128)(2,1)S(1)} %get-tuple-element.23), channel_id=1, source_target_pairs={{0,6},{1,7},{2,0},{3,1},{4,2},{5,3},{6,4},{7,5},{8,14},{9,15},{10,... | collective-permute-start | bytes 184328 | tf_op jit(solution)/shard_map/ppermute | solution.py:269
  17.9 5.7 %collective-permute-start.5 = (bf16[24,1280]{1,0:T(8,128)(2,1)S(1)}, bf16[24,1280]{1,0:T(8,128)(2,1)S(1)}, u32[]{:S(2)}, u32[]{:S(2)}) collective-permute-start(bf16[24,1280]{1,0:T(8,128)(2,1)S(1)} %get-tuple-element.24), channel_id=1, source_target_pairs={{0,3},{1,2},{2,5},{3,4},{4,7},{5,6},{6,1},{7,0},{8,11},{9,10},{10,... | collective-permute-start | bytes 184328 | tf_op jit(solution)/shard_map/ppermute | solution.py:269
  18.7 6.5 %collective-permute-start.6 = (bf16[24,1280]{1,0:T(8,128)(2,1)S(1)}, bf16[24,1280]{1,0:T(8,128)(2,1)S(1)}, u32[]{:S(2)}, u32[]{:S(2)}) collective-permute-start(bf16[24,1280]{1,0:T(8,128)(2,1)S(1)} %get-tuple-element.25), channel_id=1, source_target_pairs={{0,7},{1,6},{2,1},{3,0},{4,3},{5,2},{6,5},{7,4},{8,15},{9,14},{10,... | collective-permute-start | bytes 184328 | tf_op jit(solution)/shard_map/ppermute | solution.py:269
  21.4 3.8 %collective-permute-start.7 = (bf16[24,1280]{1,0:T(8,128)(2,1)S(1)}, bf16[24,1280]{1,0:T(8,128)(2,1)S(1)}, u32[]{:S(2)}, u32[]{:S(2)}) collective-permute-start(bf16[24,1280]{1,0:T(8,128)(2,1)S(1)} %get-tuple-element.26), channel_id=1, source_target_pairs={{0,1},{1,0},{2,3},{3,2},{4,5},{5,4},{6,7},{7,6},{8,9},{9,8},{10,11... | collective-permute-start | bytes 184328 | tf_op jit(solution)/shard_map/ppermute | solution.py:269
where the time goes:
time: 26.6 us; the launch traced here: 26.4 us
  starting transfers between devices  12.8 us (48%)
  Pallas kernels  8.73 us (33%)
  waiting for transfers between devices  3.44 us (13%)
  between operations  1.38 us (5%)
    ppermute x7, starting transfers between devices, per_device(): arrived.append(lax.ppermute(part, 'seq', route))  9.85 us
    pallas_call x2, Pallas kernels, encode_call(): pl.pallas_call(kernel, out_shape=out_shape, in_specs=[smem] * len(scalars...  7.32 us
    ppermute x7, waiting for transfers between devices, per_device(): arrived.append(lax.ppermute(part, 'seq', route))  3.27 us
    ppermute x1, starting transfers between devices, per_device(): lax.ppermute(lent, 'enc', [((i - 1) % n_enc, i) for i in range(n_enc)])  2.99 us
    pallas_call x1, Pallas kernels, per_device(): pl.pallas_call(place_kernel, out_shape=rows_of(row_total, GROUP * width),...  1.15 us
  transfers between devices with their start and end apart: 8, of which 4 were waited for; matrix products, arithmetic and copies ran while one was open for 0% of the time, Pallas kernels for 16%

commit v1 on v0

--- a/solution.py
+++ b/solution.py
@@ -180,15 +180,24 @@
 
 def pack_kernel(packed_ref, borrow_ref, borrowed_ref, *out_refs):
     total = packed_ref[...].astype(jnp.float32) + dot32(borrow_ref[...], borrowed_ref[...])
-    chunk = out_refs[0].shape[0]
-    for step, out_ref in enumerate(out_refs):
-        out_ref[...] = total[step * chunk : (step + 1) * chunk].astype(jnp.bfloat16)
+    start = 0
+    for out_ref in out_refs:
+        stop = start + out_ref.shape[0]
+        out_ref[...] = total[start:stop].astype(jnp.bfloat16)
+        start = stop
+
+
+def forward_kernel(double_ref, after_ref, out_ref):
+    rows = out_ref.shape[0]
+    out_ref[...] = double_ref[...].astype(jnp.float32)[rows:].astype(jnp.bfloat16)
 
 
 def place_kernel(place_ref, *refs):
     *in_refs, out_hbm, out, sems = refs
     tokens = out.shape[0]
     chunks = [ref[...].astype(jnp.float32) for ref in in_refs]
+    if len(chunks) > 1:
+        chunks[1] = chunks[1][: chunks[0].shape[0]]
     arrived = chunks[0] if len(chunks) == 1 else jnp.concatenate(chunks, axis=0)
     arrived = arrived.astype(jnp.bfloat16)
     width = arrived.shape[1]
@@ -205,7 +214,7 @@
 def exchange_steps(n_seq):
     n_z = n_seq // CORES
     steps = [(dz, dc) for dz in range(n_z) for dc in range(CORES) if (dz, dc) != (0, 0)]
-    return [(0, 0)] + sorted(steps, key=lambda s: (s != (1, 0), abs(s[0] - n_z / 2), s[1], s[0]))
+    return [(0, 0)] + sorted(steps, key=lambda s: (abs(s[0] - n_z / 2), s[1], s[0]))
 
 
 def chip_peer(n_seq, me, step, sign):
@@ -252,21 +261,29 @@
         (rows_of(sent), rows_of(sent, WIN), rows_of(GROUP * row_total, sent)),
         [pltpu.VMEM((row_total * GROUP, width), jnp.bfloat16)],
     )
-    pieces = n_seq if by_steps else 1
+    pieces = [chunk, CORES * chunk] + [chunk] * (n_seq - 1 - CORES) if by_steps else [sent]
     outgoing = pl.pallas_call(
         pack_kernel,
-        out_shape=[rows_of(sent // pieces)] * pieces,
+        out_shape=[rows_of(rows) for rows in pieces],
         in_specs=[vmem] * 3,
-        out_specs=[vmem] * pieces,
+        out_specs=[vmem] * len(pieces),
         compiler_params=small,
     )(packed, borrow, borrowed)
 
     if by_steps:
         n_z = n_seq // CORES
-        arrived = [outgoing[0]]
-        for part, (dz, dc) in list(zip(outgoing, exchange_steps(n_seq)))[1:]:
-            route = [(i, (i // CORES + dz) % n_z * CORES + (i + dc) % CORES) for i in range(n_seq)]
-            arrived.append(lax.ppermute(part, "seq", route))
+
+        def exchange(part, dz, dc):
+            return lax.ppermute(
+                part, "seq", [(i, (i // CORES + dz) % n_z * CORES + (i + dc) % CORES) for i in range(n_seq)]
+            )
+
+        double = exchange(outgoing[1], n_z // 2, 0)
+        rest = [exchange(part, *step) for part, step in zip(outgoing[2:], exchange_steps(n_seq)[1 + CORES :])]
+        onward = pl.pallas_call(
+            forward_kernel, out_shape=rows_of(chunk), in_specs=[vmem] * 2, out_specs=vmem, compiler_params=small
+        )(double, rest[0])
+        arrived = [outgoing[0], double, exchange(onward, 0, 1), *rest]
     else:
         arrived = [
             lax.all_to_all(
@@ -276,7 +293,7 @@
     placed = pl.pallas_call(
         place_kernel,
         out_shape=rows_of(row_total, GROUP * width),
-        in_specs=[vmem] * (1 + pieces),
+        in_specs=[vmem] * (1 + len(arrived)),
         out_specs=pl.BlockSpec(memory_space=pltpu.HBM),
         scratch_shapes=[pltpu.VMEM((row_total, GROUP * width), jnp.bfloat16), pltpu.SemaphoreType.DMA((GROUP,))],
         compiler_params=small,

time: 26.6 us -> 26.3 us (0.989)
  waiting for transfers between devices: 3.44 us -> 2.81 us
  starting transfers between devices: 12.8 us -> 13.2 us
    ppermute x7, waiting for transfers between devices: 3.27 us -> 2.64 us  [exchange(): lax.ppermute(part, 'seq', [(i, (i // CORES + dz) % n_z * CORES + (i + dc)...]
    ppermute x7, starting transfers between devices: 9.85 us -> 10.2 us  [exchange(): lax.ppermute(part, 'seq', [(i, (i // CORES + dz) % n_z * CORES + (i + dc)...]
where the time goes in v1:
time: 26.3 us; the launch traced here: 26.2 us
  starting transfers between devices  13.2 us (50%)
  Pallas kernels  8.74 us (33%)
  waiting for transfers between devices  2.81 us (11%)
  between operations  1.39 us (5%)
    ppermute x7, starting transfers between devices, exchange(): lax.ppermute(part, 'seq', [(i, (i // CORES + dz) % n_z * CORES + (i + dc)...  10.2 us
    pallas_call x2, Pallas kernels, encode_call(): pl.pallas_call(kernel, out_shape=out_shape, in_specs=[smem] * len(scalars...  7.32 us
    ppermute x1, starting transfers between devices, per_device(): lax.ppermute(lent, 'enc', [((i - 1) % n_enc, i) for i in range(n_enc)])  2.99 us
    ppermute x7, waiting for transfers between devices, exchange(): lax.ppermute(part, 'seq', [(i, (i // CORES + dz) % n_z * CORES + (i + dc)...  2.64 us
    pallas_call x1, Pallas kernels, per_device(): pl.pallas_call(place_kernel, out_shape=rows_of(row_total, GROUP * width),...  1.16 us
  transfers between devices with their start and end apart: 8, of which 4 were waited for; matrix products, arithmetic and copies ran while one was open for 0% of the time, Pallas kernels for 16%

profile of v1, /device:TPU:0, one launch (start us, length us, event | category | flops | bytes accessed | tf_op | source)
XLA Modules:
  0.0 26.2 jit_solution(15645773319884766176)
XLA Ops:
  0.0 0.0 copy-start.1
  0.0 0.0 copy-start
  0.7 3.0 %shard_map.92 = bf16[64,1280]{1,0:T(8,128)(2,1)S(1)} custom-call(s32[1,1]{1,0:T(1,128)S(6)} %copy.10.count_ref, bf16[4,64,3840]{2,1,0:T(8,128)(2,1)} %qkv_hbm.3, bf16[4,64,1280]{2,1,0:T(8,128)(2,1)} %resid_hbm.3, bf16[1280,1280]{1,0:T(8,128)(2,1)} %weight_hbm.3, bf16[1280]{0:T(1024)(128)(2,1)} %bias_hbm.3, bf16[1280]{0:T(1024)(128)(2,1)} %gain_hbm.3), custom_call_target="tpu_custom_call" | custom-call | flops 251658240 | bytes 4096000 | tf_op jit(solution)/shard_map/pallas_call | solution.py:156
  3.7 3.0 %collective-permute-start = (bf16[64,1280]{1,0:T(8,128)(2,1)S(1)}, bf16[64,1280]{1,0:T(8,128)(2,1)S(1)}, u32[]{:S(2)}, u32[]{:S(2)}) collective-permute-start(bf16[64,1280]{1,0:T(8,128)(2,1)S(1)} %shard_map.92), channel_id=1, source_target_pairs={{24,0},{0,8},{8,16},{16,24},{25,1},{1,9},{9,17},{17,25},{26,2},{2,... | collective-permute-start | bytes 491528 | tf_op jit(solution)/shard_map/ppermute | solution.py:253
  7.3 0.0 copy-done.1
  7.4 0.0 copy-done
  7.4 4.3 %shard_map.91 = (bf16[192,1280]{1,0:T(8,128)(2,1)S(1)}, bf16[192,64]{1,0:T(8,128)(2,1)S(1)}, bf16[192,192]{1,0:T(8,128)(2,1)S(1)}) custom-call(s32[1,1]{1,0:T(1,128)S(6)} %copy.10.count_ref, s32[1,1]{1,0:T(1,128)S(6)} %copy.11.send_ref, s32[1,1]{1,0:T(1,128)} %bitcast.me_ref, s32[1,48]{1,0:T(1,128)S(1)} %copy-done, s32[1,48]{1,0:T(1,128)S(1)} %copy-done.1, ...), custom_call_target="tpu_custom_call" | custom-call | flops 754974720 | bytes 5734400 | tf_op jit(solution)/shard_map/pallas_call | solution.py:156
  11.7 0.2 collective-permute-done.borrowed_ref
  11.9 0.3 shard_map.93
  12.1 2.8 %collective-permute-start.1 = (bf16[48,1280]{1,0:T(8,128)(2,1)S(1)}, bf16[48,1280]{1,0:T(8,128)(2,1)S(1)}, u32[]{:S(2)}, u32[]{:S(2)}) collective-permute-start(bf16[48,1280]{1,0:T(8,128)(2,1)S(1)} %get-tuple-element.19), channel_id=1, source_target_pairs={{0,4},{1,5},{2,6},{3,7},{4,0},{5,1},{6,2},{7,3},{8,12},{9,13},{10,... | collective-permute-start | bytes 368648 | tf_op jit(solution)/shard_map/ppermute | solution.py:277
  15.0 1.6 %collective-permute-start.2 = (bf16[24,1280]{1,0:T(8,128)(2,1)S(1)}, bf16[24,1280]{1,0:T(8,128)(2,1)S(1)}, u32[]{:S(2)}, u32[]{:S(2)}) collective-permute-start(bf16[24,1280]{1,0:T(8,128)(2,1)S(1)} %get-tuple-element.20), channel_id=1, source_target_pairs={{0,2},{1,3},{2,4},{3,5},{4,6},{5,7},{6,0},{7,1},{8,10},{9,11},{10,... | collective-permute-start | bytes 184328 | tf_op jit(solution)/shard_map/ppermute | solution.py:277
  16.6 2.2 %collective-permute-start.4 = (bf16[24,1280]{1,0:T(8,128)(2,1)S(1)}, bf16[24,1280]{1,0:T(8,128)(2,1)S(1)}, u32[]{:S(2)}, u32[]{:S(2)}) collective-permute-start(bf16[24,1280]{1,0:T(8,128)(2,1)S(1)} %get-tuple-element.21), channel_id=1, source_target_pairs={{0,6},{1,7},{2,0},{3,1},{4,2},{5,3},{6,4},{7,5},{8,14},{9,15},{10,... | collective-permute-start | bytes 184328 | tf_op jit(solution)/shard_map/ppermute | solution.py:277
  18.8 0.0 collective-permute-start.5
  18.8 3.5 %collective-permute-start.6 = (bf16[24,1280]{1,0:T(8,128)(2,1)S(1)}, bf16[24,1280]{1,0:T(8,128)(2,1)S(1)}, u32[]{:S(2)}, u32[]{:S(2)}) collective-permute-start(bf16[24,1280]{1,0:T(8,128)(2,1)S(1)} %get-tuple-element.23), channel_id=1, source_target_pairs={{0,7},{1,6},{2,1},{3,0},{4,3},{5,2},{6,5},{7,4},{8,15},{9,14},{10,... | collective-permute-start | bytes 184328 | tf_op jit(solution)/shard_map/ppermute | solution.py:277
  22.3 0.0 collective-permute-done.2.after_ref.refs_3_
  22.3 0.0 collective-permute-start.7
  22.3 1.1 %collective-permute-done.1.double_ref.refs_1_ = bf16[48,1280]{1,0:T(8,128)(2,1)S(1)} collective-permute-done((bf16[48,1280]{1,0:T(8,128)(2,1)S(1)}, bf16[48,1280]{1,0:T(8,128)(2,1)S(1)}, u32[]{:S(2)}, u32[]{:S(2)}) %collective-permute-start.1) | collective-permute-done | bytes 122912 | tf_op jit(solution)/shard_map/ppermute | solution.py:277
  23.5 0.0 collective-permute-start.3
  23.5 0.0 collective-permute-done.4.refs_4_
  23.5 0.9 %collective-permute-done.5.refs_5_ = bf16[24,1280]{1,0:T(8,128)(2,1)S(1)} collective-permute-done((bf16[24,1280]{1,0:T(8,128)(2,1)S(1)}, bf16[24,1280]{1,0:T(8,128)(2,1)S(1)}, u32[]{:S(2)}, u32[]{:S(2)}) %collective-permute-start.5) | collective-permute-done | bytes 61472 | tf_op jit(solution)/shard_map/ppermute | solution.py:277
  24.4 0.6 %collective-permute-done.6.refs_6_ = bf16[24,1280]{1,0:T(8,128)(2,1)S(1)} collective-permute-done((bf16[24,1280]{1,0:T(8,128)(2,1)S(1)}, bf16[24,1280]{1,0:T(8,128)(2,1)S(1)}, u32[]{:S(2)}, u32[]{:S(2)}) %collective-permute-start.6) | collective-permute-done | bytes 61472 | tf_op jit(solution)/shard_map/ppermute | solution.py:277
  25.0 0.0 collective-permute-done.7.refs_7_
  25.0 0.0 collective-permute-done.3.refs_2_
  25.0 1.2 %shard_map.95 = bf16[48,5120]{1,0:T(8,128)(2,1)} custom-call(bf16[192,192]{1,0:T(8,128)(2,1)S(1)} %get-tuple-element.15.place_ref, bf16[24,1280]{1,0:T(8,128)(2,1)S(1)} %get-tuple-element.18.refs_0_, bf16[48,1280]{1,0:T(8,128)(2,1)S(1)} %collective-permute-done.1.double_ref.refs_1_, bf16[24,1280]{1,0:T(8,128)(2,1)S(1)} %collective-permute-done.3.refs_2_, ...), custom_call_target="tpu_custom_call" | custom-call | tf_op jit(solution)/shard_map/pallas_call | solution.py:293
  (1 shorter events, 0.0 us)
Async XLA Ops:
  0.0 7.3 %copy-start.1 = (s32[1,48]{1,0:T(1,128)S(1)}, s32[1,48]{1,0:T(1,128)}, u32[]{:S(2)}) copy-start(s32[1,48]{1,0:T(1,128)} %row_ref.1) | copy-start | bytes 580
  0.0 7.4 %copy-start = (s32[1,48]{1,0:T(1,128)S(1)}, s32[1,48]{1,0:T(1,128)}, u32[]{:S(2)}) copy-start(s32[1,48]{1,0:T(1,128)} %slot_ref.1) | copy-start | bytes 580
  3.7 8.1 %collective-permute-start = (bf16[64,1280]{1,0:T(8,128)(2,1)S(1)}, bf16[64,1280]{1,0:T(8,128)(2,1)S(1)}, u32[]{:S(2)}, u32[]{:S(2)}) collective-permute-start(bf16[64,1280]{1,0:T(8,128)(2,1)S(1)} %shard_map.92), channel_id=1, source_target_pairs={{24,0},{0,8},{8,16},{16,24},{25,1},{1,9},{9,17},{17,25},{26,2},{2,... | collective-permute-start | bytes 491528 | tf_op jit(solution)/shard_map/ppermute | solution.py:253
  12.1 11.4 %collective-permute-start.1 = (bf16[48,1280]{1,0:T(8,128)(2,1)S(1)}, bf16[48,1280]{1,0:T(8,128)(2,1)S(1)}, u32[]{:S(2)}, u32[]{:S(2)}) collective-permute-start(bf16[48,1280]{1,0:T(8,128)(2,1)S(1)} %get-tuple-element.19), channel_id=1, source_target_pairs={{0,4},{1,5},{2,6},{3,7},{4,0},{5,1},{6,2},{7,3},{8,12},{9,13},{10,... | collective-permute-start | bytes 368648 | tf_op jit(solution)/shard_map/ppermute | solution.py:277
  15.0 7.4 %collective-permute-start.2 = (bf16[24,1280]{1,0:T(8,128)(2,1)S(1)}, bf16[24,1280]{1,0:T(8,128)(2,1)S(1)}, u32[]{:S(2)}, u32[]{:S(2)}) collective-permute-start(bf16[24,1280]{1,0:T(8,128)(2,1)S(1)} %get-tuple-element.20), channel_id=1, source_target_pairs={{0,2},{1,3},{2,4},{3,5},{4,6},{5,7},{6,0},{7,1},{8,10},{9,11},{10,... | collective-permute-start | bytes 184328 | tf_op jit(solution)/shard_map/ppermute | solution.py:277
  16.6 6.9 %collective-permute-start.4 = (bf16[24,1280]{1,0:T(8,128)(2,1)S(1)}, bf16[24,1280]{1,0:T(8,128)(2,1)S(1)}, u32[]{:S(2)}, u32[]{:S(2)}) collective-permute-start(bf16[24,1280]{1,0:T(8,128)(2,1)S(1)} %get-tuple-element.21), channel_id=1, source_target_pairs={{0,6},{1,7},{2,0},{3,1},{4,2},{5,3},{6,4},{7,5},{8,14},{9,15},{10,... | collective-permute-start | bytes 184328 | tf_op jit(solution)/shard_map/ppermute | solution.py:277
  18.8 5.6 %collective-permute-start.5 = (bf16[24,1280]{1,0:T(8,128)(2,1)S(1)}, bf16[24,1280]{1,0:T(8,128)(2,1)S(1)}, u32[]{:S(2)}, u32[]{:S(2)}) collective-permute-start(bf16[24,1280]{1,0:T(8,128)(2,1)S(1)} %get-tuple-element.22), channel_id=1, source_target_pairs={{0,3},{1,2},{2,5},{3,4},{4,7},{5,6},{6,1},{7,0},{8,11},{9,10},{10,... | collective-permute-start | bytes 184328 | tf_op jit(solution)/shard_map/ppermute | solution.py:277
  18.8 6.2 %collective-permute-start.6 = (bf16[24,1280]{1,0:T(8,128)(2,1)S(1)}, bf16[24,1280]{1,0:T(8,128)(2,1)S(1)}, u32[]{:S(2)}, u32[]{:S(2)}) collective-permute-start(bf16[24,1280]{1,0:T(8,128)(2,1)S(1)} %get-tuple-element.23), channel_id=1, source_target_pairs={{0,7},{1,6},{2,1},{3,0},{4,3},{5,2},{6,5},{7,4},{8,15},{9,14},{10,... | collective-permute-start | bytes 184328 | tf_op jit(solution)/shard_map/ppermute | solution.py:277
  22.3 2.7 %collective-permute-start.7 = (bf16[24,1280]{1,0:T(8,128)(2,1)S(1)}, bf16[24,1280]{1,0:T(8,128)(2,1)S(1)}, u32[]{:S(2)}, u32[]{:S(2)}) collective-permute-start(bf16[24,1280]{1,0:T(8,128)(2,1)S(1)} %get-tuple-element.24), channel_id=1, source_target_pairs={{0,1},{1,0},{2,3},{3,2},{4,5},{5,4},{6,7},{7,6},{8,9},{9,8},{10,11... | collective-permute-start | bytes 184328 | tf_op jit(solution)/shard_map/ppermute | solution.py:277
  23.5 1.5 %collective-permute-start.3 = (bf16[24,1280]{1,0:T(8,128)(2,1)S(1)}, bf16[24,1280]{1,0:T(8,128)(2,1)S(1)}, u32[]{:S(2)}, u32[]{:S(2)}) collective-permute-start(bf16[24,1280]{1,0:T(8,128)(2,1)S(1)} %shard_map.94), channel_id=1, source_target_pairs={{0,1},{1,0},{2,3},{3,2},{4,5},{5,4},{6,7},{7,6},{8,9},{9,8},{10,11... | collective-permute-start | bytes 184328 | tf_op jit(solution)/shard_map/ppermute | solution.py:277

commit v2 on v1

--- a/solution.py
+++ b/solution.py
@@ -192,12 +192,14 @@
     out_ref[...] = double_ref[...].astype(jnp.float32)[rows:].astype(jnp.bfloat16)
 
 
-def place_kernel(place_ref, *refs):
+def place_kernel(n_double, place_ref, *refs):
     *in_refs, out_hbm, out, sems = refs
     tokens = out.shape[0]
     chunks = [ref[...].astype(jnp.float32) for ref in in_refs]
-    if len(chunks) > 1:
-        chunks[1] = chunks[1][: chunks[0].shape[0]]
+    if n_double:
+        rows = chunks[0].shape[0]
+        for i in range(1, 1 + CORES * n_double, CORES):
+            chunks[i] = chunks[i][:rows]
     arrived = chunks[0] if len(chunks) == 1 else jnp.concatenate(chunks, axis=0)
     arrived = arrived.astype(jnp.bfloat16)
     width = arrived.shape[1]
@@ -211,10 +213,14 @@
         copy.wait()
 
 
+def double_offsets(n_seq):
+    return sorted({1, n_seq // CORES // 2})
+
+
 def exchange_steps(n_seq):
-    n_z = n_seq // CORES
-    steps = [(dz, dc) for dz in range(n_z) for dc in range(CORES) if (dz, dc) != (0, 0)]
-    return [(0, 0)] + sorted(steps, key=lambda s: (abs(s[0] - n_z / 2), s[1], s[0]))
+    doubles = double_offsets(n_seq)
+    offsets = doubles + [dz for dz in range(1, n_seq // CORES) if dz not in doubles]
+    return [(0, 0)] + [(dz, dc) for dz in offsets for dc in range(CORES)] + [(0, 1)]
 
 
 def chip_peer(n_seq, me, step, sign):
@@ -261,7 +267,10 @@
         (rows_of(sent), rows_of(sent, WIN), rows_of(GROUP * row_total, sent)),
         [pltpu.VMEM((row_total * GROUP, width), jnp.bfloat16)],
     )
-    pieces = [chunk, CORES * chunk] + [chunk] * (n_seq - 1 - CORES) if by_steps else [sent]
+    n_double = len(double_offsets(n_seq)) if by_steps else 0
+    pieces = [sent]
+    if by_steps:
+        pieces = [chunk] + [CORES * chunk] * n_double + [chunk] * (n_seq - 1 - CORES * n_double)
     outgoing = pl.pallas_call(
         pack_kernel,
         out_shape=[rows_of(rows) for rows in pieces],
@@ -278,12 +287,16 @@
                 part, "seq", [(i, (i // CORES + dz) % n_z * CORES + (i + dc) % CORES) for i in range(n_seq)]
             )
 
-        double = exchange(outgoing[1], n_z // 2, 0)
-        rest = [exchange(part, *step) for part, step in zip(outgoing[2:], exchange_steps(n_seq)[1 + CORES :])]
-        onward = pl.pallas_call(
-            forward_kernel, out_shape=rows_of(chunk), in_specs=[vmem] * 2, out_specs=vmem, compiler_params=small
-        )(double, rest[0])
-        arrived = [outgoing[0], double, exchange(onward, 0, 1), *rest]
+        doubles = [exchange(part, dz, 0) for part, dz in zip(outgoing[1:], double_offsets(n_seq))]
+        singles = exchange_steps(n_seq)[1 + CORES * n_double : -1]
+        singles = [exchange(part, *step) for part, step in zip(outgoing[1 + n_double : -1], singles)]
+        arrived = [outgoing[0]]
+        for i, double in enumerate(doubles):
+            passed = pl.pallas_call(
+                forward_kernel, out_shape=rows_of(chunk), in_specs=[vmem] * 2, out_specs=vmem, compiler_params=small
+            )(double, singles[0])
+            arrived += [double, exchange(passed, 0, 1)]
+        arrived += singles + [exchange(outgoing[-1], 0, 1)]
     else:
         arrived = [
             lax.all_to_all(
@@ -291,7 +304,7 @@
             ).reshape(sent, width)
         ]
     placed = pl.pallas_call(
-        place_kernel,
+        functools.partial(place_kernel, n_double),
         out_shape=rows_of(row_total, GROUP * width),
         in_specs=[vmem] * (1 + len(arrived)),
         out_specs=pl.BlockSpec(memory_space=pltpu.HBM),

time: 26.3 us -> 26.6 us (1.011)
  waiting for transfers between devices: 2.81 us -> 6.89 us
  starting transfers between devices: 13.2 us -> 9.39 us
    ppermute x7, waiting for transfers between devices: 2.64 us -> 6.72 us  [exchange(): lax.ppermute(part, 'seq', [(i, (i // CORES + dz) % n_z * CORES + (i + dc)...]
    ppermute x7, starting transfers between devices: 10.2 us -> 6.4 us  [exchange(): lax.ppermute(part, 'seq', [(i, (i // CORES + dz) % n_z * CORES + (i + dc)...]
  transfers between devices with their start and end apart: 8 -> 8, of which waited for: 4 -> 5; matrix products, arithmetic and copies ran while one was open for 0% -> 0% of each run, Pallas kernels for 16% -> 16%
where the time goes in v2:
time: 26.6 us; the launch traced here: 26.4 us
  starting transfers between devices  9.39 us (35%)
  Pallas kernels  8.74 us (33%)
  waiting for transfers between devices  6.89 us (26%)
  between operations  1.4 us (5%)
    pallas_call x2, Pallas kernels, encode_call(): pl.pallas_call(kernel, out_shape=out_shape, in_specs=[smem] * len(scalars...  7.32 us
    ppermute x7, waiting for transfers between devices, exchange(): lax.ppermute(part, 'seq', [(i, (i // CORES + dz) % n_z * CORES + (i + dc)...  6.72 us
    ppermute x7, starting transfers between devices, exchange(): lax.ppermute(part, 'seq', [(i, (i // CORES + dz) % n_z * CORES + (i + dc)...  6.4 us
    ppermute x1, starting transfers between devices, per_device(): lax.ppermute(lent, 'enc', [((i - 1) % n_enc, i) for i in range(n_enc)])  2.99 us
    pallas_call x1, Pallas kernels, per_device(): pl.pallas_call(functools.partial(place_kernel, n_double), out_shape=rows_...  1.16 us
  transfers between devices with their start and end apart: 8, of which 5 were waited for; matrix products, arithmetic and copies ran while one was open for 0% of the time, Pallas kernels for 16%

profile of v2, /device:TPU:0, one launch (start us, length us, event | category | flops | bytes accessed | tf_op | source)
XLA Modules:
  0.0 26.4 jit_solution(5903874361994905361)
XLA Ops:
  0.0 0.0 copy-start.1
  0.0 0.0 copy-start
  0.7 3.0 %shard_map.92 = bf16[64,1280]{1,0:T(8,128)(2,1)S(1)} custom-call(s32[1,1]{1,0:T(1,128)S(6)} %copy.10.count_ref, bf16[4,64,3840]{2,1,0:T(8,128)(2,1)} %qkv_hbm.3, bf16[4,64,1280]{2,1,0:T(8,128)(2,1)} %resid_hbm.3, bf16[1280,1280]{1,0:T(8,128)(2,1)} %weight_hbm.3, bf16[1280]{0:T(1024)(128)(2,1)} %bias_hbm.3, bf16[1280]{0:T(1024)(128)(2,1)} %gain_hbm.3), custom_call_target="tpu_custom_call" | custom-call | flops 251658240 | bytes 4096000 | tf_op jit(solution)/shard_map/pallas_call | solution.py:156
  3.7 3.0 %collective-permute-start = (bf16[64,1280]{1,0:T(8,128)(2,1)S(1)}, bf16[64,1280]{1,0:T(8,128)(2,1)S(1)}, u32[]{:S(2)}, u32[]{:S(2)}) collective-permute-start(bf16[64,1280]{1,0:T(8,128)(2,1)S(1)} %shard_map.92), channel_id=1, source_target_pairs={{24,0},{0,8},{8,16},{16,24},{25,1},{1,9},{9,17},{17,25},{26,2},{2,... | collective-permute-start | bytes 491528 | tf_op jit(solution)/shard_map/ppermute | solution.py:259
  7.3 0.0 copy-done.1
  7.4 0.0 copy-done
  7.4 4.3 %shard_map.91 = (bf16[192,1280]{1,0:T(8,128)(2,1)S(1)}, bf16[192,64]{1,0:T(8,128)(2,1)S(1)}, bf16[192,192]{1,0:T(8,128)(2,1)S(1)}) custom-call(s32[1,1]{1,0:T(1,128)S(6)} %copy.10.count_ref, s32[1,1]{1,0:T(1,128)S(6)} %copy.11.send_ref, s32[1,1]{1,0:T(1,128)} %bitcast.me_ref, s32[1,48]{1,0:T(1,128)S(1)} %copy-done, s32[1,48]{1,0:T(1,128)S(1)} %copy-done.1, ...), custom_call_target="tpu_custom_call" | custom-call | flops 754974720 | bytes 5734400 | tf_op jit(solution)/shard_map/pallas_call | solution.py:156
  11.7 0.2 collective-permute-done.borrowed_ref
  11.9 0.3 shard_map.93
  12.1 1.8 %collective-permute-start.1 = (bf16[48,1280]{1,0:T(8,128)(2,1)S(1)}, bf16[48,1280]{1,0:T(8,128)(2,1)S(1)}, u32[]{:S(2)}, u32[]{:S(2)}) collective-permute-start(bf16[48,1280]{1,0:T(8,128)(2,1)S(1)} %get-tuple-element.18), channel_id=1, source_target_pairs={{0,2},{1,3},{2,4},{3,5},{4,6},{5,7},{6,0},{7,1},{8,10},{9,11},{10,... | collective-permute-start | bytes 368648 | tf_op jit(solution)/shard_map/ppermute | solution.py:286
  13.9 2.6 %collective-permute-start.4 = (bf16[48,1280]{1,0:T(8,128)(2,1)S(1)}, bf16[48,1280]{1,0:T(8,128)(2,1)S(1)}, u32[]{:S(2)}, u32[]{:S(2)}) collective-permute-start(bf16[48,1280]{1,0:T(8,128)(2,1)S(1)} %get-tuple-element.20), channel_id=1, source_target_pairs={{0,4},{1,5},{2,6},{3,7},{4,0},{5,1},{6,2},{7,3},{8,12},{9,13},{10,... | collective-permute-start | bytes 368648 | tf_op jit(solution)/shard_map/ppermute | solution.py:286
  16.5 1.3 %collective-permute-start.2 = (bf16[24,1280]{1,0:T(8,128)(2,1)S(1)}, bf16[24,1280]{1,0:T(8,128)(2,1)S(1)}, u32[]{:S(2)}, u32[]{:S(2)}) collective-permute-start(bf16[24,1280]{1,0:T(8,128)(2,1)S(1)} %get-tuple-element.19), channel_id=1, source_target_pairs={{0,6},{1,7},{2,0},{3,1},{4,2},{5,3},{6,4},{7,5},{8,14},{9,15},{10,... | collective-permute-start | bytes 184328 | tf_op jit(solution)/shard_map/ppermute | solution.py:286
  17.9 0.0 collective-permute-start.6
  17.9 0.6 %collective-permute-start.7 = (bf16[24,1280]{1,0:T(8,128)(2,1)S(1)}, bf16[24,1280]{1,0:T(8,128)(2,1)S(1)}, u32[]{:S(2)}, u32[]{:S(2)}) collective-permute-start(bf16[24,1280]{1,0:T(8,128)(2,1)S(1)} %get-tuple-element.22), channel_id=1, source_target_pairs={{0,1},{1,0},{2,3},{3,2},{4,5},{5,4},{6,7},{7,6},{8,9},{9,8},{10,11... | collective-permute-start | bytes 184328 | tf_op jit(solution)/shard_map/ppermute | solution.py:286
  18.4 3.7 %collective-permute-done.2.after_ref.refs_5_ = bf16[24,1280]{1,0:T(8,128)(2,1)S(1)} collective-permute-done((bf16[24,1280]{1,0:T(8,128)(2,1)S(1)}, bf16[24,1280]{1,0:T(8,128)(2,1)S(1)}, u32[]{:S(2)}, u32[]{:S(2)}) %collective-permute-start.2) | collective-permute-done | bytes 61472 | tf_op jit(solution)/shard_map/ppermute | solution.py:286
  22.1 0.0 collective-permute-done.1.double_ref.refs_1_
  22.1 0.1 collective-permute-start.3
  22.2 1.8 %collective-permute-done.4.double_ref.refs_3_ = bf16[48,1280]{1,0:T(8,128)(2,1)S(1)} collective-permute-done((bf16[48,1280]{1,0:T(8,128)(2,1)S(1)}, bf16[48,1280]{1,0:T(8,128)(2,1)S(1)}, u32[]{:S(2)}, u32[]{:S(2)}) %collective-permute-start.4) | collective-permute-done | bytes 122912 | tf_op jit(solution)/shard_map/ppermute | solution.py:286
  24.0 0.0 collective-permute-start.5
  24.0 0.2 collective-permute-done.6.refs_6_
  24.3 0.0 collective-permute-done.7.refs_7_
  24.3 0.0 collective-permute-done.3.refs_2_
  24.3 1.0 %collective-permute-done.5.refs_4_ = bf16[24,1280]{1,0:T(8,128)(2,1)S(1)} collective-permute-done((bf16[24,1280]{1,0:T(8,128)(2,1)S(1)}, bf16[24,1280]{1,0:T(8,128)(2,1)S(1)}, u32[]{:S(2)}, u32[]{:S(2)}) %collective-permute-start.5) | collective-permute-done | bytes 61472 | tf_op jit(solution)/shard_map/ppermute | solution.py:286
  25.3 1.2 %shard_map.96 = bf16[48,5120]{1,0:T(8,128)(2,1)} custom-call(bf16[192,192]{1,0:T(8,128)(2,1)S(1)} %get-tuple-element.14.place_ref, bf16[24,1280]{1,0:T(8,128)(2,1)S(1)} %get-tuple-element.17.refs_0_, bf16[48,1280]{1,0:T(8,128)(2,1)S(1)} %collective-permute-done.1.double_ref.refs_1_, bf16[24,1280]{1,0:T(8,128)(2,1)S(1)} %collective-permute-done.3.refs_2_, ...), custom_call_target="tpu_custom_call" | custom-call | tf_op jit(solution)/shard_map/pallas_call | solution.py:306
  (2 shorter events, 0.0 us)
Async XLA Ops:
  0.0 7.3 %copy-start.1 = (s32[1,48]{1,0:T(1,128)S(1)}, s32[1,48]{1,0:T(1,128)}, u32[]{:S(2)}) copy-start(s32[1,48]{1,0:T(1,128)} %row_ref.1) | copy-start | bytes 580
  0.0 7.4 %copy-start = (s32[1,48]{1,0:T(1,128)S(1)}, s32[1,48]{1,0:T(1,128)}, u32[]{:S(2)}) copy-start(s32[1,48]{1,0:T(1,128)} %slot_ref.1) | copy-start | bytes 580
  3.7 8.1 %collective-permute-start = (bf16[64,1280]{1,0:T(8,128)(2,1)S(1)}, bf16[64,1280]{1,0:T(8,128)(2,1)S(1)}, u32[]{:S(2)}, u32[]{:S(2)}) collective-permute-start(bf16[64,1280]{1,0:T(8,128)(2,1)S(1)} %shard_map.92), channel_id=1, source_target_pairs={{24,0},{0,8},{8,16},{16,24},{25,1},{1,9},{9,17},{17,25},{26,2},{2,... | collective-permute-start | bytes 491528 | tf_op jit(solution)/shard_map/ppermute | solution.py:259
  12.1 10.0 %collective-permute-start.1 = (bf16[48,1280]{1,0:T(8,128)(2,1)S(1)}, bf16[48,1280]{1,0:T(8,128)(2,1)S(1)}, u32[]{:S(2)}, u32[]{:S(2)}) collective-permute-start(bf16[48,1280]{1,0:T(8,128)(2,1)S(1)} %get-tuple-element.18), channel_id=1, source_target_pairs={{0,2},{1,3},{2,4},{3,5},{4,6},{5,7},{6,0},{7,1},{8,10},{9,11},{10,... | collective-permute-start | bytes 368648 | tf_op jit(solution)/shard_map/ppermute | solution.py:286
  13.9 10.1 %collective-permute-start.4 = (bf16[48,1280]{1,0:T(8,128)(2,1)S(1)}, bf16[48,1280]{1,0:T(8,128)(2,1)S(1)}, u32[]{:S(2)}, u32[]{:S(2)}) collective-permute-start(bf16[48,1280]{1,0:T(8,128)(2,1)S(1)} %get-tuple-element.20), channel_id=1, source_target_pairs={{0,4},{1,5},{2,6},{3,7},{4,0},{5,1},{6,2},{7,3},{8,12},{9,13},{10,... | collective-permute-start | bytes 368648 | tf_op jit(solution)/shard_map/ppermute | solution.py:286
  16.5 5.6 %collective-permute-start.2 = (bf16[24,1280]{1,0:T(8,128)(2,1)S(1)}, bf16[24,1280]{1,0:T(8,128)(2,1)S(1)}, u32[]{:S(2)}, u32[]{:S(2)}) collective-permute-start(bf16[24,1280]{1,0:T(8,128)(2,1)S(1)} %get-tuple-element.19), channel_id=1, source_target_pairs={{0,6},{1,7},{2,0},{3,1},{4,2},{5,3},{6,4},{7,5},{8,14},{9,15},{10,... | collective-permute-start | bytes 184328 | tf_op jit(solution)/shard_map/ppermute | solution.py:286
  17.9 6.4 %collective-permute-start.6 = (bf16[24,1280]{1,0:T(8,128)(2,1)S(1)}, bf16[24,1280]{1,0:T(8,128)(2,1)S(1)}, u32[]{:S(2)}, u32[]{:S(2)}) collective-permute-start(bf16[24,1280]{1,0:T(8,128)(2,1)S(1)} %get-tuple-element.21), channel_id=1, source_target_pairs={{0,7},{1,6},{2,1},{3,0},{4,3},{5,2},{6,5},{7,4},{8,15},{9,14},{10,... | collective-permute-start | bytes 184328 | tf_op jit(solution)/shard_map/ppermute | solution.py:286
  17.9 6.4 %collective-permute-start.7 = (bf16[24,1280]{1,0:T(8,128)(2,1)S(1)}, bf16[24,1280]{1,0:T(8,128)(2,1)S(1)}, u32[]{:S(2)}, u32[]{:S(2)}) collective-permute-start(bf16[24,1280]{1,0:T(8,128)(2,1)S(1)} %get-tuple-element.22), channel_id=1, source_target_pairs={{0,1},{1,0},{2,3},{3,2},{4,5},{5,4},{6,7},{7,6},{8,9},{9,8},{10,11... | collective-permute-start | bytes 184328 | tf_op jit(solution)/shard_map/ppermute | solution.py:286
  22.1 2.1 %collective-permute-start.3 = (bf16[24,1280]{1,0:T(8,128)(2,1)S(1)}, bf16[24,1280]{1,0:T(8,128)(2,1)S(1)}, u32[]{:S(2)}, u32[]{:S(2)}) collective-permute-start(bf16[24,1280]{1,0:T(8,128)(2,1)S(1)} %shard_map.94), channel_id=1, source_target_pairs={{0,1},{1,0},{2,3},{3,2},{4,5},{5,4},{6,7},{7,6},{8,9},{9,8},{10,11... | collective-permute-start | bytes 184328 | tf_op jit(solution)/shard_map/ppermute | solution.py:286
  24.0 1.2 %collective-permute-start.5 = (bf16[24,1280]{1,0:T(8,128)(2,1)S(1)}, bf16[24,1280]{1,0:T(8,128)(2,1)S(1)}, u32[]{:S(2)}, u32[]{:S(2)}) collective-permute-start(bf16[24,1280]{1,0:T(8,128)(2,1)S(1)} %shard_map.95), channel_id=1, source_target_pairs={{0,1},{1,0},{2,3},{3,2},{4,5},{5,4},{6,7},{7,6},{8,9},{9,8},{10,11... | collective-permute-start | bytes 184328 | tf_op jit(solution)/shard_map/ppermute | solution.py:286

commit v3 on v1

--- a/solution.py
+++ b/solution.py
@@ -212,9 +212,7 @@
 
 
 def exchange_steps(n_seq):
-    n_z = n_seq // CORES
-    steps = [(dz, dc) for dz in range(n_z) for dc in range(CORES) if (dz, dc) != (0, 0)]
-    return [(0, 0)] + sorted(steps, key=lambda s: (abs(s[0] - n_z / 2), s[1], s[0]))
+    return [(0, 0)] + [(dz, dc) for dz in range(1, n_seq // CORES) for dc in range(CORES)] + [(0, 1)]
 
 
 def chip_peer(n_seq, me, step, sign):
@@ -278,7 +276,7 @@
                 part, "seq", [(i, (i // CORES + dz) % n_z * CORES + (i + dc) % CORES) for i in range(n_seq)]
             )
 
-        double = exchange(outgoing[1], n_z // 2, 0)
+        double = exchange(outgoing[1], 1, 0)
         rest = [exchange(part, *step) for part, step in zip(outgoing[2:], exchange_steps(n_seq)[1 + CORES :])]
         onward = pl.pallas_call(
             forward_kernel, out_shape=rows_of(chunk), in_specs=[vmem] * 2, out_specs=vmem, compiler_params=small

time: 26.3 us -> 25.8 us (0.981)
  starting transfers between devices: 13.2 us -> 11.8 us
  waiting for transfers between devices: 2.81 us -> 3.51 us
    ppermute x7, starting transfers between devices: 10.2 us -> 8.81 us  [exchange(): lax.ppermute(part, 'seq', [(i, (i // CORES + dz) % n_z * CORES + (i + dc)...]
    ppermute x7, waiting for transfers between devices: 2.64 us -> 3.34 us  [exchange(): lax.ppermute(part, 'seq', [(i, (i // CORES + dz) % n_z * CORES + (i + dc)...]
  transfers between devices with their start and end apart: 8 -> 8, of which waited for: 4 -> 5; matrix products, arithmetic and copies ran while one was open for 0% -> 0% of each run, Pallas kernels for 16% -> 17%
where the time goes in v3:
time: 25.8 us; the launch traced here: 25.4 us
  starting transfers between devices  11.8 us (46%)
  Pallas kernels  8.73 us (34%)
  waiting for transfers between devices  3.51 us (14%)
  between operations  1.38 us (5%)
    ppermute x7, starting transfers between devices, exchange(): lax.ppermute(part, 'seq', [(i, (i // CORES + dz) % n_z * CORES + (i + dc)...  8.81 us
    pallas_call x2, Pallas kernels, encode_call(): pl.pallas_call(kernel, out_shape=out_shape, in_specs=[smem] * len(scalars...  7.32 us
    ppermute x7, waiting for transfers between devices, exchange(): lax.ppermute(part, 'seq', [(i, (i // CORES + dz) % n_z * CORES + (i + dc)...  3.34 us
    ppermute x1, starting transfers between devices, per_device(): lax.ppermute(lent, 'enc', [((i - 1) % n_enc, i) for i in range(n_enc)])  2.99 us
    pallas_call x1, Pallas kernels, per_device(): pl.pallas_call(place_kernel, out_shape=rows_of(row_total, GROUP * width),...  1.15 us
  transfers between devices with their start and end apart: 8, of which 5 were waited for; matrix products, arithmetic and copies ran while one was open for 0% of the time, Pallas kernels for 17%

profile of v3, /device:TPU:0, one launch (start us, length us, event | category | flops | bytes accessed | tf_op | source)
XLA Modules:
  0.0 25.4 jit_solution(11498121810074848899)
XLA Ops:
  0.0 0.0 copy-start.1
  0.0 0.0 copy-start
  0.7 3.0 %shard_map.92 = bf16[64,1280]{1,0:T(8,128)(2,1)S(1)} custom-call(s32[1,1]{1,0:T(1,128)S(6)} %copy.10.count_ref, bf16[4,64,3840]{2,1,0:T(8,128)(2,1)} %qkv_hbm.3, bf16[4,64,1280]{2,1,0:T(8,128)(2,1)} %resid_hbm.3, bf16[1280,1280]{1,0:T(8,128)(2,1)} %weight_hbm.3, bf16[1280]{0:T(1024)(128)(2,1)} %bias_hbm.3, bf16[1280]{0:T(1024)(128)(2,1)} %gain_hbm.3), custom_call_target="tpu_custom_call" | custom-call | flops 251658240 | bytes 4096000 | tf_op jit(solution)/shard_map/pallas_call | solution.py:156
  3.7 3.0 %collective-permute-start = (bf16[64,1280]{1,0:T(8,128)(2,1)S(1)}, bf16[64,1280]{1,0:T(8,128)(2,1)S(1)}, u32[]{:S(2)}, u32[]{:S(2)}) collective-permute-start(bf16[64,1280]{1,0:T(8,128)(2,1)S(1)} %shard_map.92), channel_id=1, source_target_pairs={{24,0},{0,8},{8,16},{16,24},{25,1},{1,9},{9,17},{17,25},{26,2},{2,... | collective-permute-start | bytes 491528 | tf_op jit(solution)/shard_map/ppermute | solution.py:251
  7.3 0.0 copy-done.1
  7.4 0.0 copy-done
  7.4 4.3 %shard_map.91 = (bf16[192,1280]{1,0:T(8,128)(2,1)S(1)}, bf16[192,64]{1,0:T(8,128)(2,1)S(1)}, bf16[192,192]{1,0:T(8,128)(2,1)S(1)}) custom-call(s32[1,1]{1,0:T(1,128)S(6)} %copy.10.count_ref, s32[1,1]{1,0:T(1,128)S(6)} %copy.11.send_ref, s32[1,1]{1,0:T(1,128)} %bitcast.me_ref, s32[1,48]{1,0:T(1,128)S(1)} %copy-done, s32[1,48]{1,0:T(1,128)S(1)} %copy-done.1, ...), custom_call_target="tpu_custom_call" | custom-call | flops 754974720 | bytes 5734400 | tf_op jit(solution)/shard_map/pallas_call | solution.py:156
  11.7 0.2 collective-permute-done.borrowed_ref
  11.9 0.3 %shard_map.93 = (bf16[24,1280]{1,0:T(8,128)(2,1)S(1)}, bf16[48,1280]{1,0:T(8,128)(2,1)S(1)}, bf16[24,1280]{1,0:T(8,128)(2,1)S(1)}, bf16[24,1280]{1,0:T(8,128)(2,...) custom-call(bf16[192,1280]{1,0:T(8,128)(2,1)S(1)} %get-tuple-element.16.packed_ref,, ...), custom_call_target="tpu_custom_call" | custom-call | tf_op jit(solution)/shard_map/pallas_call | solution.py:263
  12.1 1.8 %collective-permute-start.1 = (bf16[48,1280]{1,0:T(8,128)(2,1)S(1)}, bf16[48,1280]{1,0:T(8,128)(2,1)S(1)}, u32[]{:S(2)}, u32[]{:S(2)}) collective-permute-start(bf16[48,1280]{1,0:T(8,128)(2,1)S(1)} %get-tuple-element.19), channel_id=1, source_target_pairs={{0,2},{1,3},{2,4},{3,5},{4,6},{5,7},{6,0},{7,1},{8,10},{9,11},{10,... | collective-permute-start | bytes 368648 | tf_op jit(solution)/shard_map/ppermute | solution.py:275
  13.9 2.6 %collective-permute-start.2 = (bf16[24,1280]{1,0:T(8,128)(2,1)S(1)}, bf16[24,1280]{1,0:T(8,128)(2,1)S(1)}, u32[]{:S(2)}, u32[]{:S(2)}) collective-permute-start(bf16[24,1280]{1,0:T(8,128)(2,1)S(1)} %get-tuple-element.20), channel_id=1, source_target_pairs={{0,4},{1,5},{2,6},{3,7},{4,0},{5,1},{6,2},{7,3},{8,12},{9,13},{10,... | collective-permute-start | bytes 184328 | tf_op jit(solution)/shard_map/ppermute | solution.py:275
  16.5 0.0 collective-permute-start.4
  16.5 1.3 %collective-permute-start.5 = (bf16[24,1280]{1,0:T(8,128)(2,1)S(1)}, bf16[24,1280]{1,0:T(8,128)(2,1)S(1)}, u32[]{:S(2)}, u32[]{:S(2)}) collective-permute-start(bf16[24,1280]{1,0:T(8,128)(2,1)S(1)} %get-tuple-element.22), channel_id=1, source_target_pairs={{0,6},{1,7},{2,0},{3,1},{4,2},{5,3},{6,4},{7,5},{8,14},{9,15},{10,... | collective-permute-start | bytes 184328 | tf_op jit(solution)/shard_map/ppermute | solution.py:275
  17.9 2.5 %collective-permute-start.6 = (bf16[24,1280]{1,0:T(8,128)(2,1)S(1)}, bf16[24,1280]{1,0:T(8,128)(2,1)S(1)}, u32[]{:S(2)}, u32[]{:S(2)}) collective-permute-start(bf16[24,1280]{1,0:T(8,128)(2,1)S(1)} %get-tuple-element.23), channel_id=1, source_target_pairs={{0,7},{1,6},{2,1},{3,0},{4,3},{5,2},{6,5},{7,4},{8,15},{9,14},{10,... | collective-permute-start | bytes 184328 | tf_op jit(solution)/shard_map/ppermute | solution.py:275
  20.4 2.4 %collective-permute-done.2.after_ref.refs_3_ = bf16[24,1280]{1,0:T(8,128)(2,1)S(1)} collective-permute-done((bf16[24,1280]{1,0:T(8,128)(2,1)S(1)}, bf16[24,1280]{1,0:T(8,128)(2,1)S(1)}, u32[]{:S(2)}, u32[]{:S(2)}) %collective-permute-start.2) | collective-permute-done | bytes 61472 | tf_op jit(solution)/shard_map/ppermute | solution.py:275
  22.8 0.0 collective-permute-start.7
  22.8 0.0 collective-permute-done.1.double_ref.refs_1_
  22.8 0.6 %collective-permute-start.3 = (bf16[24,1280]{1,0:T(8,128)(2,1)S(1)}, bf16[24,1280]{1,0:T(8,128)(2,1)S(1)}, u32[]{:S(2)}, u32[]{:S(2)}) collective-permute-start(bf16[24,1280]{1,0:T(8,128)(2,1)S(1)} %shard_map.94), channel_id=1, source_target_pairs={{0,1},{1,0},{2,3},{3,2},{4,5},{5,4},{6,7},{7,6},{8,9},{9,8},{10,11... | collective-permute-start | bytes 184328 | tf_op jit(solution)/shard_map/ppermute | solution.py:275
  23.4 0.5 %collective-permute-done.4.refs_4_ = bf16[24,1280]{1,0:T(8,128)(2,1)S(1)} collective-permute-done((bf16[24,1280]{1,0:T(8,128)(2,1)S(1)}, bf16[24,1280]{1,0:T(8,128)(2,1)S(1)}, u32[]{:S(2)}, u32[]{:S(2)}) %collective-permute-start.4) | collective-permute-done | bytes 61472 | tf_op jit(solution)/shard_map/ppermute | solution.py:275
  23.9 0.0 collective-permute-done.5.refs_5_
  23.9 0.2 collective-permute-done.6.refs_6_
  24.1 0.0 collective-permute-done.7.refs_7_
  24.1 0.2 collective-permute-done.3.refs_2_
  24.3 1.2 %shard_map.95 = bf16[48,5120]{1,0:T(8,128)(2,1)} custom-call(bf16[192,192]{1,0:T(8,128)(2,1)S(1)} %get-tuple-element.15.place_ref, bf16[24,1280]{1,0:T(8,128)(2,1)S(1)} %get-tuple-element.18.refs_0_, bf16[48,1280]{1,0:T(8,128)(2,1)S(1)} %collective-permute-done.1.double_ref.refs_1_, bf16[24,1280]{1,0:T(8,128)(2,1)S(1)} %collective-permute-done.3.refs_2_, ...), custom_call_target="tpu_custom_call" | custom-call | tf_op jit(solution)/shard_map/pallas_call | solution.py:291
  (1 shorter events, 0.0 us)
Async XLA Ops:
  0.0 7.3 %copy-start.1 = (s32[1,48]{1,0:T(1,128)S(1)}, s32[1,48]{1,0:T(1,128)}, u32[]{:S(2)}) copy-start(s32[1,48]{1,0:T(1,128)} %row_ref.1) | copy-start | bytes 580
  0.0 7.4 %copy-start = (s32[1,48]{1,0:T(1,128)S(1)}, s32[1,48]{1,0:T(1,128)}, u32[]{:S(2)}) copy-start(s32[1,48]{1,0:T(1,128)} %slot_ref.1) | copy-start | bytes 580
  3.7 8.1 %collective-permute-start = (bf16[64,1280]{1,0:T(8,128)(2,1)S(1)}, bf16[64,1280]{1,0:T(8,128)(2,1)S(1)}, u32[]{:S(2)}, u32[]{:S(2)}) collective-permute-start(bf16[64,1280]{1,0:T(8,128)(2,1)S(1)} %shard_map.92), channel_id=1, source_target_pairs={{24,0},{0,8},{8,16},{16,24},{25,1},{1,9},{9,17},{17,25},{26,2},{2,... | collective-permute-start | bytes 491528 | tf_op jit(solution)/shard_map/ppermute | solution.py:251
  12.1 10.7 %collective-permute-start.1 = (bf16[48,1280]{1,0:T(8,128)(2,1)S(1)}, bf16[48,1280]{1,0:T(8,128)(2,1)S(1)}, u32[]{:S(2)}, u32[]{:S(2)}) collective-permute-start(bf16[48,1280]{1,0:T(8,128)(2,1)S(1)} %get-tuple-element.19), channel_id=1, source_target_pairs={{0,2},{1,3},{2,4},{3,5},{4,6},{5,7},{6,0},{7,1},{8,10},{9,11},{10,... | collective-permute-start | bytes 368648 | tf_op jit(solution)/shard_map/ppermute | solution.py:275
  13.9 8.9 %collective-permute-start.2 = (bf16[24,1280]{1,0:T(8,128)(2,1)S(1)}, bf16[24,1280]{1,0:T(8,128)(2,1)S(1)}, u32[]{:S(2)}, u32[]{:S(2)}) collective-permute-start(bf16[24,1280]{1,0:T(8,128)(2,1)S(1)} %get-tuple-element.20), channel_id=1, source_target_pairs={{0,4},{1,5},{2,6},{3,7},{4,0},{5,1},{6,2},{7,3},{8,12},{9,13},{10,... | collective-permute-start | bytes 184328 | tf_op jit(solution)/shard_map/ppermute | solution.py:275
  16.5 7.4 %collective-permute-start.4 = (bf16[24,1280]{1,0:T(8,128)(2,1)S(1)}, bf16[24,1280]{1,0:T(8,128)(2,1)S(1)}, u32[]{:S(2)}, u32[]{:S(2)}) collective-permute-start(bf16[24,1280]{1,0:T(8,128)(2,1)S(1)} %get-tuple-element.21), channel_id=1, source_target_pairs={{0,5},{1,4},{2,7},{3,6},{4,1},{5,0},{6,3},{7,2},{8,13},{9,12},{10,... | collective-permute-start | bytes 184328 | tf_op jit(solution)/shard_map/ppermute | solution.py:275
  16.5 7.4 %collective-permute-start.5 = (bf16[24,1280]{1,0:T(8,128)(2,1)S(1)}, bf16[24,1280]{1,0:T(8,128)(2,1)S(1)}, u32[]{:S(2)}, u32[]{:S(2)}) collective-permute-start(bf16[24,1280]{1,0:T(8,128)(2,1)S(1)} %get-tuple-element.22), channel_id=1, source_target_pairs={{0,6},{1,7},{2,0},{3,1},{4,2},{5,3},{6,4},{7,5},{8,14},{9,15},{10,... | collective-permute-start | bytes 184328 | tf_op jit(solution)/shard_map/ppermute | solution.py:275
  17.9 6.2 %collective-permute-start.6 = (bf16[24,1280]{1,0:T(8,128)(2,1)S(1)}, bf16[24,1280]{1,0:T(8,128)(2,1)S(1)}, u32[]{:S(2)}, u32[]{:S(2)}) collective-permute-start(bf16[24,1280]{1,0:T(8,128)(2,1)S(1)} %get-tuple-element.23), channel_id=1, source_target_pairs={{0,7},{1,6},{2,1},{3,0},{4,3},{5,2},{6,5},{7,4},{8,15},{9,14},{10,... | collective-permute-start | bytes 184328 | tf_op jit(solution)/shard_map/ppermute | solution.py:275
  22.8 1.3 %collective-permute-start.7 = (bf16[24,1280]{1,0:T(8,128)(2,1)S(1)}, bf16[24,1280]{1,0:T(8,128)(2,1)S(1)}, u32[]{:S(2)}, u32[]{:S(2)}) collective-permute-start(bf16[24,1280]{1,0:T(8,128)(2,1)S(1)} %get-tuple-element.24), channel_id=1, source_target_pairs={{0,1},{1,0},{2,3},{3,2},{4,5},{5,4},{6,7},{7,6},{8,9},{9,8},{10,11... | collective-permute-start | bytes 184328 | tf_op jit(solution)/shard_map/ppermute | solution.py:275
  22.8 1.5 %collective-permute-start.3 = (bf16[24,1280]{1,0:T(8,128)(2,1)S(1)}, bf16[24,1280]{1,0:T(8,128)(2,1)S(1)}, u32[]{:S(2)}, u32[]{:S(2)}) collective-permute-start(bf16[24,1280]{1,0:T(8,128)(2,1)S(1)} %shard_map.94), channel_id=1, source_target_pairs={{0,1},{1,0},{2,3},{3,2},{4,5},{5,4},{6,7},{7,6},{8,9},{9,8},{10,11... | collective-permute-start | bytes 184328 | tf_op jit(solution)/shard_map/ppermute | solution.py:275

commit v4 on v3

--- a/solution.py
+++ b/solution.py
@@ -61,7 +61,7 @@
 
 def encode(
     slot, qkv_hbm, resid_hbm, weight_hbm, bias_hbm, gain_hbm, out_ref,
-    qkv, resid, weight, attended, hidden, bias_ref, gain_ref, sems,
+    qkv, resid, weight, attended, hidden, bias_ref, gain_ref, sems, while_copying=lambda: None,
 ):
     blocks = qkv.shape[0]
     width = resid.shape[2]
@@ -72,6 +72,7 @@
     copies = [pltpu.make_async_copy(a, b, sems.at[i]) for i, (a, b) in enumerate(pairs)]
     for copy in copies:
         copy.start()
+    while_copying()
     copies[0].wait()
     for b in range(blocks):
         attend(
@@ -113,38 +114,40 @@
 def own_kernel(
     n_seq, cap, peer, count_ref, send_ref, me_ref, slot_ref, row_ref,
     qkv_hbm, resid_hbm, weight_hbm, bias_hbm, gain_hbm,
-    packed_ref, borrow_ref, place_ref, normed, *scratch,
+    packed_ref, borrow_ref, place_ref, normed, own_ref, *scratch,
 ):
     rows = normed.shape[0]
     slots = n_seq * cap
     sent = slots * GROUP
     tokens = rows // GROUP
     me = me_ref[0, 0]
-    encode(0, qkv_hbm, resid_hbm, weight_hbm, bias_hbm, gain_hbm, normed, *scratch)
-
-    step, patch, rank = split_index(lax.broadcasted_iota(jnp.int32, (sent, 1), 0), n_seq, cap)
-    row_code = (peer(me, step, 1) * cap + rank) * GROUP + patch
-    token = lax.broadcasted_iota(jnp.int32, (tokens, rows), 0)
-    column = lax.broadcasted_iota(jnp.int32, (tokens, rows), 1)
-    spread = one_hot((column >= token * GROUP) & (column < (token + 1) * GROUP))
-    slot = jnp.broadcast_to(slot_ref[...].astype(jnp.float32), (16, tokens)).astype(jnp.bfloat16)
-    slot = dot32(slot, spread)[:1].astype(jnp.int32)
-    index = lax.broadcasted_iota(jnp.int32, (1, rows), 1)
-    col_code = slot * GROUP + jnp.bitwise_and(index, GROUP - 1)
-    kept = (count_ref[0, 0] - send_ref[0, 0]) * WIN
-    last = rows - WIN
-    own = one_hot(row_code == jnp.where(index < kept, col_code, -1))
-    packed_ref[...] = dot32(own, normed[...]).astype(jnp.bfloat16)
-    borrow_ref[...] = one_hot(row_code == jnp.where(kept > last, -1, col_code[:, last:]))
-
-    step, patch, rank = split_index(lax.broadcasted_iota(jnp.int32, (1, sent), 1), n_seq, cap)
-    arrive = peer(me, step, -1) * cap + rank
-    pick = one_hot(lax.broadcasted_iota(jnp.int32, (slots, sent), 0) == arrive)
-    target = jnp.broadcast_to(row_ref[...].astype(jnp.float32), (16, slots)).astype(jnp.bfloat16)
-    target = dot32(target, pick)[:1].astype(jnp.int32)
-    out_row = lax.broadcasted_iota(jnp.int32, (tokens, sent), 0)
-    for j in range(GROUP):
-        place_ref[j * tokens : (j + 1) * tokens, :] = one_hot((target == out_row) & (patch == j))
+
+    def make_one_hots():
+        step, patch, rank = split_index(lax.broadcasted_iota(jnp.int32, (sent, 1), 0), n_seq, cap)
+        row_code = (peer(me, step, 1) * cap + rank) * GROUP + patch
+        token = lax.broadcasted_iota(jnp.int32, (tokens, rows), 0)
+        column = lax.broadcasted_iota(jnp.int32, (tokens, rows), 1)
+        spread = one_hot((column >= token * GROUP) & (column < (token + 1) * GROUP))
+        slot = jnp.broadcast_to(slot_ref[...].astype(jnp.float32), (16, tokens)).astype(jnp.bfloat16)
+        slot = dot32(slot, spread)[:1].astype(jnp.int32)
+        index = lax.broadcasted_iota(jnp.int32, (1, rows), 1)
+        col_code = slot * GROUP + jnp.bitwise_and(index, GROUP - 1)
+        kept = (count_ref[0, 0] - send_ref[0, 0]) * WIN
+        last = rows - WIN
+        own_ref[...] = one_hot(row_code == jnp.where(index < kept, col_code, -1))
+        borrow_ref[...] = one_hot(row_code == jnp.where(kept > last, -1, col_code[:, last:]))
+
+        step, patch, rank = split_index(lax.broadcasted_iota(jnp.int32, (1, sent), 1), n_seq, cap)
+        arrive = peer(me, step, -1) * cap + rank
+        pick = one_hot(lax.broadcasted_iota(jnp.int32, (slots, sent), 0) == arrive)
+        target = jnp.broadcast_to(row_ref[...].astype(jnp.float32), (16, slots)).astype(jnp.bfloat16)
+        target = dot32(target, pick)[:1].astype(jnp.int32)
+        out_row = lax.broadcasted_iota(jnp.int32, (tokens, sent), 0)
+        for j in range(GROUP):
+            place_ref[j * tokens : (j + 1) * tokens, :] = one_hot((target == out_row) & (patch == j))
+
+    encode(0, qkv_hbm, resid_hbm, weight_hbm, bias_hbm, gain_hbm, normed, *scratch, while_copying=make_one_hots)
+    packed_ref[...] = dot32(own_ref[...], normed[...]).astype(jnp.bfloat16)
 
 
 def encode_call(kernel, blocks, scalars, slots, qkv, resid, weight, bias, gain, out_shape, extra):
@@ -257,7 +260,10 @@
         functools.partial(own_kernel, n_seq, cap, peer), blocks,
         [block_count, send_count, me], [send_slot, lm_row], *data,
         (rows_of(sent), rows_of(sent, WIN), rows_of(GROUP * row_total, sent)),
-        [pltpu.VMEM((row_total * GROUP, width), jnp.bfloat16)],
+        [
+            pltpu.VMEM((row_total * GROUP, width), jnp.bfloat16),
+            pltpu.VMEM((sent, row_total * GROUP), jnp.bfloat16),
+        ],
     )
     pieces = [chunk, CORES * chunk] + [chunk] * (n_seq - 1 - CORES) if by_steps else [sent]
     outgoing = pl.pallas_call(

time: 25.8 us -> 25.8 us (level)
  no operation moved by 1% of the time
where the time goes in v4:
time: 25.8 us; the launch traced here: 25.4 us
  starting transfers between devices  11.8 us (46%)
  Pallas kernels  8.72 us (34%)
  waiting for transfers between devices  3.52 us (14%)
  between operations  1.38 us (5%)
    ppermute x7, starting transfers between devices, exchange(): lax.ppermute(part, 'seq', [(i, (i // CORES + dz) % n_z * CORES + (i + dc)...  8.81 us
    pallas_call x2, Pallas kernels, encode_call(): pl.pallas_call(kernel, out_shape=out_shape, in_specs=[smem] * len(scalars...  7.31 us
    ppermute x7, waiting for transfers between devices, exchange(): lax.ppermute(part, 'seq', [(i, (i // CORES + dz) % n_z * CORES + (i + dc)...  3.33 us
    ppermute x1, starting transfers between devices, per_device(): lax.ppermute(lent, 'enc', [((i - 1) % n_enc, i) for i in range(n_enc)])  2.99 us
    pallas_call x1, Pallas kernels, per_device(): pl.pallas_call(place_kernel, out_shape=rows_of(row_total, GROUP * width),...  1.15 us
  transfers between devices with their start and end apart: 8, of which 5 were waited for; matrix products, arithmetic and copies ran while one was open for 0% of the time, Pallas kernels for 17%

profile of v4, /device:TPU:0, one launch (start us, length us, event | category | flops | bytes accessed | tf_op | source)
XLA Modules:
  0.0 25.4 jit_solution(12679009906826204412)
XLA Ops:
  0.0 0.0 copy-start.1
  0.0 0.0 copy-start
  0.7 3.0 %shard_map.92 = bf16[64,1280]{1,0:T(8,128)(2,1)S(1)} custom-call(s32[1,1]{1,0:T(1,128)S(6)} %copy.10.count_ref, bf16[4,64,3840]{2,1,0:T(8,128)(2,1)} %qkv_hbm.3, bf16[4,64,1280]{2,1,0:T(8,128)(2,1)} %resid_hbm.3, bf16[1280,1280]{1,0:T(8,128)(2,1)} %weight_hbm.3, bf16[1280]{0:T(1024)(128)(2,1)} %bias_hbm.3, bf16[1280]{0:T(1024)(128)(2,1)} %gain_hbm.3), custom_call_target="tpu_custom_call" | custom-call | flops 251658240 | bytes 4096000 | tf_op jit(solution)/shard_map/pallas_call | solution.py:159
  3.7 3.0 %collective-permute-start = (bf16[64,1280]{1,0:T(8,128)(2,1)S(1)}, bf16[64,1280]{1,0:T(8,128)(2,1)S(1)}, u32[]{:S(2)}, u32[]{:S(2)}) collective-permute-start(bf16[64,1280]{1,0:T(8,128)(2,1)S(1)} %shard_map.92), channel_id=1, source_target_pairs={{24,0},{0,8},{8,16},{16,24},{25,1},{1,9},{9,17},{17,25},{26,2},{2,... | collective-permute-start | bytes 491528 | tf_op jit(solution)/shard_map/ppermute | solution.py:254
  7.3 0.0 copy-done.1
  7.4 0.0 copy-done
  7.4 4.3 %shard_map.91 = (bf16[192,1280]{1,0:T(8,128)(2,1)S(1)}, bf16[192,64]{1,0:T(8,128)(2,1)S(1)}, bf16[192,192]{1,0:T(8,128)(2,1)S(1)}) custom-call(s32[1,1]{1,0:T(1,128)S(6)} %copy.10.count_ref, s32[1,1]{1,0:T(1,128)S(6)} %copy.11.send_ref, s32[1,1]{1,0:T(1,128)} %bitcast.me_ref, s32[1,48]{1,0:T(1,128)S(1)} %copy-done, s32[1,48]{1,0:T(1,128)S(1)} %copy-done.1, ...), custom_call_target="tpu_custom_call" | custom-call | flops 754974720 | bytes 5734400 | tf_op jit(solution)/shard_map/pallas_call | solution.py:159
  11.7 0.2 collective-permute-done.borrowed_ref
  11.9 0.3 %shard_map.93 = (bf16[24,1280]{1,0:T(8,128)(2,1)S(1)}, bf16[48,1280]{1,0:T(8,128)(2,1)S(1)}, bf16[24,1280]{1,0:T(8,128)(2,1)S(1)}, bf16[24,1280]{1,0:T(8,128)(2,...) custom-call(bf16[192,1280]{1,0:T(8,128)(2,1)S(1)} %get-tuple-element.16.packed_ref,, ...), custom_call_target="tpu_custom_call" | custom-call | tf_op jit(solution)/shard_map/pallas_call | solution.py:269
  12.1 1.8 %collective-permute-start.1 = (bf16[48,1280]{1,0:T(8,128)(2,1)S(1)}, bf16[48,1280]{1,0:T(8,128)(2,1)S(1)}, u32[]{:S(2)}, u32[]{:S(2)}) collective-permute-start(bf16[48,1280]{1,0:T(8,128)(2,1)S(1)} %get-tuple-element.19), channel_id=1, source_target_pairs={{0,2},{1,3},{2,4},{3,5},{4,6},{5,7},{6,0},{7,1},{8,10},{9,11},{10,... | collective-permute-start | bytes 368648 | tf_op jit(solution)/shard_map/ppermute | solution.py:281
  13.9 2.6 %collective-permute-start.2 = (bf16[24,1280]{1,0:T(8,128)(2,1)S(1)}, bf16[24,1280]{1,0:T(8,128)(2,1)S(1)}, u32[]{:S(2)}, u32[]{:S(2)}) collective-permute-start(bf16[24,1280]{1,0:T(8,128)(2,1)S(1)} %get-tuple-element.20), channel_id=1, source_target_pairs={{0,4},{1,5},{2,6},{3,7},{4,0},{5,1},{6,2},{7,3},{8,12},{9,13},{10,... | collective-permute-start | bytes 184328 | tf_op jit(solution)/shard_map/ppermute | solution.py:281
  16.5 0.0 collective-permute-start.4
  16.5 1.3 %collective-permute-start.5 = (bf16[24,1280]{1,0:T(8,128)(2,1)S(1)}, bf16[24,1280]{1,0:T(8,128)(2,1)S(1)}, u32[]{:S(2)}, u32[]{:S(2)}) collective-permute-start(bf16[24,1280]{1,0:T(8,128)(2,1)S(1)} %get-tuple-element.22), channel_id=1, source_target_pairs={{0,6},{1,7},{2,0},{3,1},{4,2},{5,3},{6,4},{7,5},{8,14},{9,15},{10,... | collective-permute-start | bytes 184328 | tf_op jit(solution)/shard_map/ppermute | solution.py:281
  17.9 2.5 %collective-permute-start.6 = (bf16[24,1280]{1,0:T(8,128)(2,1)S(1)}, bf16[24,1280]{1,0:T(8,128)(2,1)S(1)}, u32[]{:S(2)}, u32[]{:S(2)}) collective-permute-start(bf16[24,1280]{1,0:T(8,128)(2,1)S(1)} %get-tuple-element.23), channel_id=1, source_target_pairs={{0,7},{1,6},{2,1},{3,0},{4,3},{5,2},{6,5},{7,4},{8,15},{9,14},{10,... | collective-permute-start | bytes 184328 | tf_op jit(solution)/shard_map/ppermute | solution.py:281
  20.4 2.4 %collective-permute-done.2.after_ref.refs_3_ = bf16[24,1280]{1,0:T(8,128)(2,1)S(1)} collective-permute-done((bf16[24,1280]{1,0:T(8,128)(2,1)S(1)}, bf16[24,1280]{1,0:T(8,128)(2,1)S(1)}, u32[]{:S(2)}, u32[]{:S(2)}) %collective-permute-start.2) | collective-permute-done | bytes 61472 | tf_op jit(solution)/shard_map/ppermute | solution.py:281
  22.8 0.0 collective-permute-start.7
  22.8 0.0 collective-permute-done.1.double_ref.refs_1_
  22.8 0.6 %collective-permute-start.3 = (bf16[24,1280]{1,0:T(8,128)(2,1)S(1)}, bf16[24,1280]{1,0:T(8,128)(2,1)S(1)}, u32[]{:S(2)}, u32[]{:S(2)}) collective-permute-start(bf16[24,1280]{1,0:T(8,128)(2,1)S(1)} %shard_map.94), channel_id=1, source_target_pairs={{0,1},{1,0},{2,3},{3,2},{4,5},{5,4},{6,7},{7,6},{8,9},{9,8},{10,11... | collective-permute-start | bytes 184328 | tf_op jit(solution)/shard_map/ppermute | solution.py:281
  23.4 0.5 %collective-permute-done.4.refs_4_ = bf16[24,1280]{1,0:T(8,128)(2,1)S(1)} collective-permute-done((bf16[24,1280]{1,0:T(8,128)(2,1)S(1)}, bf16[24,1280]{1,0:T(8,128)(2,1)S(1)}, u32[]{:S(2)}, u32[]{:S(2)}) %collective-permute-start.4) | collective-permute-done | bytes 61472 | tf_op jit(solution)/shard_map/ppermute | solution.py:281
  23.9 0.0 collective-permute-done.5.refs_5_
  23.9 0.2 collective-permute-done.6.refs_6_
  24.1 0.0 collective-permute-done.7.refs_7_
  24.1 0.2 collective-permute-done.3.refs_2_
  24.3 1.2 %shard_map.95 = bf16[48,5120]{1,0:T(8,128)(2,1)} custom-call(bf16[192,192]{1,0:T(8,128)(2,1)S(1)} %get-tuple-element.15.place_ref, bf16[24,1280]{1,0:T(8,128)(2,1)S(1)} %get-tuple-element.18.refs_0_, bf16[48,1280]{1,0:T(8,128)(2,1)S(1)} %collective-permute-done.1.double_ref.refs_1_, bf16[24,1280]{1,0:T(8,128)(2,1)S(1)} %collective-permute-done.3.refs_2_, ...), custom_call_target="tpu_custom_call" | custom-call | tf_op jit(solution)/shard_map/pallas_call | solution.py:297
  (1 shorter events, 0.0 us)
Async XLA Ops:
  0.0 7.3 %copy-start.1 = (s32[1,48]{1,0:T(1,128)S(1)}, s32[1,48]{1,0:T(1,128)}, u32[]{:S(2)}) copy-start(s32[1,48]{1,0:T(1,128)} %row_ref.1) | copy-start | bytes 580
  0.0 7.4 %copy-start = (s32[1,48]{1,0:T(1,128)S(1)}, s32[1,48]{1,0:T(1,128)}, u32[]{:S(2)}) copy-start(s32[1,48]{1,0:T(1,128)} %slot_ref.1) | copy-start | bytes 580
  3.7 8.1 %collective-permute-start = (bf16[64,1280]{1,0:T(8,128)(2,1)S(1)}, bf16[64,1280]{1,0:T(8,128)(2,1)S(1)}, u32[]{:S(2)}, u32[]{:S(2)}) collective-permute-start(bf16[64,1280]{1,0:T(8,128)(2,1)S(1)} %shard_map.92), channel_id=1, source_target_pairs={{24,0},{0,8},{8,16},{16,24},{25,1},{1,9},{9,17},{17,25},{26,2},{2,... | collective-permute-start | bytes 491528 | tf_op jit(solution)/shard_map/ppermute | solution.py:254
  12.1 10.7 %collective-permute-start.1 = (bf16[48,1280]{1,0:T(8,128)(2,1)S(1)}, bf16[48,1280]{1,0:T(8,128)(2,1)S(1)}, u32[]{:S(2)}, u32[]{:S(2)}) collective-permute-start(bf16[48,1280]{1,0:T(8,128)(2,1)S(1)} %get-tuple-element.19), channel_id=1, source_target_pairs={{0,2},{1,3},{2,4},{3,5},{4,6},{5,7},{6,0},{7,1},{8,10},{9,11},{10,... | collective-permute-start | bytes 368648 | tf_op jit(solution)/shard_map/ppermute | solution.py:281
  13.9 8.9 %collective-permute-start.2 = (bf16[24,1280]{1,0:T(8,128)(2,1)S(1)}, bf16[24,1280]{1,0:T(8,128)(2,1)S(1)}, u32[]{:S(2)}, u32[]{:S(2)}) collective-permute-start(bf16[24,1280]{1,0:T(8,128)(2,1)S(1)} %get-tuple-element.20), channel_id=1, source_target_pairs={{0,4},{1,5},{2,6},{3,7},{4,0},{5,1},{6,2},{7,3},{8,12},{9,13},{10,... | collective-permute-start | bytes 184328 | tf_op jit(solution)/shard_map/ppermute | solution.py:281
  16.5 7.4 %collective-permute-start.4 = (bf16[24,1280]{1,0:T(8,128)(2,1)S(1)}, bf16[24,1280]{1,0:T(8,128)(2,1)S(1)}, u32[]{:S(2)}, u32[]{:S(2)}) collective-permute-start(bf16[24,1280]{1,0:T(8,128)(2,1)S(1)} %get-tuple-element.21), channel_id=1, source_target_pairs={{0,5},{1,4},{2,7},{3,6},{4,1},{5,0},{6,3},{7,2},{8,13},{9,12},{10,... | collective-permute-start | bytes 184328 | tf_op jit(solution)/shard_map/ppermute | solution.py:281
  16.5 7.4 %collective-permute-start.5 = (bf16[24,1280]{1,0:T(8,128)(2,1)S(1)}, bf16[24,1280]{1,0:T(8,128)(2,1)S(1)}, u32[]{:S(2)}, u32[]{:S(2)}) collective-permute-start(bf16[24,1280]{1,0:T(8,128)(2,1)S(1)} %get-tuple-element.22), channel_id=1, source_target_pairs={{0,6},{1,7},{2,0},{3,1},{4,2},{5,3},{6,4},{7,5},{8,14},{9,15},{10,... | collective-permute-start | bytes 184328 | tf_op jit(solution)/shard_map/ppermute | solution.py:281
  17.9 6.2 %collective-permute-start.6 = (bf16[24,1280]{1,0:T(8,128)(2,1)S(1)}, bf16[24,1280]{1,0:T(8,128)(2,1)S(1)}, u32[]{:S(2)}, u32[]{:S(2)}) collective-permute-start(bf16[24,1280]{1,0:T(8,128)(2,1)S(1)} %get-tuple-element.23), channel_id=1, source_target_pairs={{0,7},{1,6},{2,1},{3,0},{4,3},{5,2},{6,5},{7,4},{8,15},{9,14},{10,... | collective-permute-start | bytes 184328 | tf_op jit(solution)/shard_map/ppermute | solution.py:281
  22.8 1.3 %collective-permute-start.7 = (bf16[24,1280]{1,0:T(8,128)(2,1)S(1)}, bf16[24,1280]{1,0:T(8,128)(2,1)S(1)}, u32[]{:S(2)}, u32[]{:S(2)}) collective-permute-start(bf16[24,1280]{1,0:T(8,128)(2,1)S(1)} %get-tuple-element.24), channel_id=1, source_target_pairs={{0,1},{1,0},{2,3},{3,2},{4,5},{5,4},{6,7},{7,6},{8,9},{9,8},{10,11... | collective-permute-start | bytes 184328 | tf_op jit(solution)/shard_map/ppermute | solution.py:281
  22.8 1.5 %collective-permute-start.3 = (bf16[24,1280]{1,0:T(8,128)(2,1)S(1)}, bf16[24,1280]{1,0:T(8,128)(2,1)S(1)}, u32[]{:S(2)}, u32[]{:S(2)}) collective-permute-start(bf16[24,1280]{1,0:T(8,128)(2,1)S(1)} %shard_map.94), channel_id=1, source_target_pairs={{0,1},{1,0},{2,3},{3,2},{4,5},{5,4},{6,7},{7,6},{8,9},{9,8},{10,11... | collective-permute-start | bytes 184328 | tf_op jit(solution)/shard_map/ppermute | solution.py:281

commit v5 on v3

--- a/solution.py
+++ b/solution.py
@@ -26,42 +26,79 @@
     return match.astype(jnp.float32).astype(jnp.bfloat16)
 
 
-def attend(q, k, v, out_ref, row0, width):
+def head_pairs(width):
     head = width // HEADS
-    rate = 1.0 / math.sqrt(head)
-    totals = [None] * (width // LANES)
-    sums = [None] * (width // LANES)
-    first_half = lax.broadcasted_iota(jnp.int32, (WIN, 2 * WIN), 1) < WIN
-    for pair in range(HEADS // 2):
-        start = 2 * pair * head
+    spans = []
+    for start in range(0, width, 2 * head):
         lo = start // LANES * LANES
-        hi = -(-(start + 2 * head) // LANES) * LANES
-        column = lax.broadcasted_iota(jnp.int32, (2 * WIN, hi - lo), 1) + lo
-        row = lax.broadcasted_iota(jnp.int32, (2 * WIN, hi - lo), 0)
+        spans.append((start, lo, -(-(start + 2 * head) // LANES) * LANES))
+    return spans
+
+
+def mask_period(width):
+    return LANES // math.gcd(LANES, 2 * (width // HEADS))
+
+
+def mask_scratch(width):
+    return pltpu.VMEM((mask_period(width), 2 * WIN, 2 * LANES), jnp.bfloat16)
+
+
+def make_masks(masks, width):
+    head = width // HEADS
+    for i in range(masks.shape[0]):
+        start, lo, hi = head_pairs(width)[i]
+        column = lax.broadcasted_iota(jnp.int32, masks.shape[1:], 1) + lo
+        row = lax.broadcasted_iota(jnp.int32, masks.shape[1:], 0)
         begin = jnp.where(row < WIN, start, start + head)
-        mask = one_hot((column >= begin) & (column < begin + head))
-        kw, vw = k(lo, hi), v(lo, hi)
-        keys = jnp.concatenate([kw, kw], axis=0) * mask
-        values = jnp.concatenate([vw, vw], axis=0) * mask
-        scores = lax.dot_general(q(lo, hi), keys, NT, preferred_element_type=jnp.float32)
-        top0 = jnp.max(jnp.where(first_half, scores, -jnp.inf), axis=1, keepdims=True)
-        top1 = jnp.max(jnp.where(first_half, -jnp.inf, scores), axis=1, keepdims=True)
-        raised = jnp.exp((scores - jnp.where(first_half, top0, top1)) * rate).astype(jnp.bfloat16)
-        part = dot32(raised, values)
-        norm = dot32(raised, mask)
-        for tile in range(lo // LANES, hi // LANES):
-            at = slice(tile * LANES - lo, (tile + 1) * LANES - lo)
-            totals[tile] = part[:, at] if totals[tile] is None else totals[tile] + part[:, at]
-            sums[tile] = norm[:, at] if sums[tile] is None else sums[tile] + norm[:, at]
+        masks[i] = one_hot((column >= begin) & (column < begin + head))
+
+
+def attend(qkv, b, masks, attended, width):
+    rate = math.log2(math.e) / math.sqrt(width // HEADS)
+    period = masks.shape[0]
+    spans = [(lo, hi) for _, lo, hi in head_pairs(width)]
+    first = lax.broadcasted_iota(jnp.int32, (WIN, 2 * WIN), 1) < WIN
+
+    def both_heads(part, pair):
+        return jnp.concatenate([part, part], axis=0) * masks[pair % period]
+
+    scores = [
+        lax.dot_general(
+            qkv[b, :, lo:hi], both_heads(qkv[b, :, width + lo : width + hi], pair), NT, preferred_element_type=jnp.float32
+        )
+        for pair, (lo, hi) in enumerate(spans)
+    ]
+    tops = [
+        (
+            jnp.max(jnp.where(first, s, -jnp.inf), axis=1, keepdims=True),
+            jnp.max(jnp.where(first, -jnp.inf, s), axis=1, keepdims=True),
+        )
+        for s in scores
+    ]
+    raised = [
+        jnp.exp2((s - jnp.where(first, top0, top1)) * rate).astype(jnp.bfloat16) for s, (top0, top1) in zip(scores, tops)
+    ]
+    parts = [
+        dot32(raised[pair], both_heads(qkv[b, :, 2 * width + lo : 2 * width + hi], pair))
+        for pair, (lo, hi) in enumerate(spans)
+    ]
+    norms = [None] * len(spans)
+    for i in range(period):
+        same = range(i, len(spans), period)
+        norm = dot32(jnp.concatenate([raised[pair] for pair in same], axis=0), masks[i])
+        for n, pair in enumerate(same):
+            norms[pair] = norm[n * WIN : (n + 1) * WIN]
     for tile in range(width // LANES):
-        out_ref[row0 : row0 + WIN, tile * LANES : (tile + 1) * LANES] = (totals[tile] / sums[tile]).astype(
-            jnp.bfloat16
-        )
+        at = tile * LANES
+        inside = [(pair, slice(at - lo, at - lo + LANES)) for pair, (lo, hi) in enumerate(spans) if lo <= at < hi]
+        total = sum(parts[pair][:, cols] for pair, cols in inside)
+        norm = sum(norms[pair][:, cols] for pair, cols in inside)
+        attended[b * WIN : (b + 1) * WIN, at : at + LANES] = (total / norm).astype(jnp.bfloat16)
 
 
 def encode(
     slot, qkv_hbm, resid_hbm, weight_hbm, bias_hbm, gain_hbm, out_ref,
-    qkv, resid, weight, attended, hidden, bias_ref, gain_ref, sems,
+    qkv, resid, weight, attended, hidden, bias_ref, gain_ref, masks, sems,
 ):
     blocks = qkv.shape[0]
     width = resid.shape[2]
@@ -72,14 +109,10 @@
     copies = [pltpu.make_async_copy(a, b, sems.at[i]) for i, (a, b) in enumerate(pairs)]
     for copy in copies:
         copy.start()
+    make_masks(masks, width)
     copies[0].wait()
     for b in range(blocks):
-        attend(
-            lambda lo, hi, b=b: qkv[b, :, lo:hi],
-            lambda lo, hi, b=b: qkv[b, :, width + lo : width + hi],
-            lambda lo, hi, b=b: qkv[b, :, 2 * width + lo : 2 * width + hi],
-            attended, b * WIN, width,
-        )
+        attend(qkv, b, masks, attended, width)
     for copy in copies[1:]:
         copy.wait()
     rows = blocks * WIN
@@ -167,6 +200,7 @@
             pltpu.VMEM((rows, width), jnp.float32),
             pltpu.VMEM((width,), jnp.bfloat16),
             pltpu.VMEM((width,), jnp.bfloat16),
+            mask_scratch(width),
             pltpu.SemaphoreType.DMA((5,)),
         ],
         compiler_params=pltpu.CompilerParams(vmem_limit_bytes=24 << 20),

time: 25.8 us -> 26 us (level)
  transfers between devices with their start and end apart: 8 -> 8, of which waited for: 5 -> 4; matrix products, arithmetic and copies ran while one was open for 0% -> 0% of each run, Pallas kernels for 17% -> 18%
where the time goes in v5:
time: 26 us; the launch traced here: 25.6 us
  starting transfers between devices  11.8 us (45%)
  Pallas kernels  8.93 us (34%)
  waiting for transfers between devices  3.53 us (14%)
  between operations  1.39 us (5%)
    ppermute x7, starting transfers between devices, exchange(): lax.ppermute(part, 'seq', [(i, (i // CORES + dz) % n_z * CORES + (i + dc)...  8.78 us
    pallas_call x2, Pallas kernels, encode_call(): pl.pallas_call(kernel, out_shape=out_shape, in_specs=[smem] * len(scalars...  7.51 us
    ppermute x7, waiting for transfers between devices, exchange(): lax.ppermute(part, 'seq', [(i, (i // CORES + dz) % n_z * CORES + (i + dc)...  3.52 us
    ppermute x1, starting transfers between devices, per_device(): lax.ppermute(lent, 'enc', [((i - 1) % n_enc, i) for i in range(n_enc)])  2.99 us
    pallas_call x1, Pallas kernels, per_device(): pl.pallas_call(place_kernel, out_shape=rows_of(row_total, GROUP * width),...  1.15 us
  transfers between devices with their start and end apart: 8, of which 4 were waited for; matrix products, arithmetic and copies ran while one was open for 0% of the time, Pallas kernels for 18%

profile of v5, /device:TPU:0, one launch (start us, length us, event | category | flops | bytes accessed | tf_op | source)
XLA Modules:
  0.0 25.6 jit_solution(5445080353278485862)
XLA Ops:
  0.0 0.0 copy-start.1
  0.0 0.0 copy-start
  0.7 3.0 %shard_map.92 = bf16[64,1280]{1,0:T(8,128)(2,1)S(1)} custom-call(s32[1,1]{1,0:T(1,128)S(6)} %copy.10.count_ref, bf16[4,64,3840]{2,1,0:T(8,128)(2,1)} %qkv_hbm.3, bf16[4,64,1280]{2,1,0:T(8,128)(2,1)} %resid_hbm.3, bf16[1280,1280]{1,0:T(8,128)(2,1)} %weight_hbm.3, bf16[1280]{0:T(1024)(128)(2,1)} %bias_hbm.3, bf16[1280]{0:T(1024)(128)(2,1)} %gain_hbm.3), custom_call_target="tpu_custom_call" | custom-call | flops 251658240 | bytes 4096000 | tf_op jit(solution)/shard_map/pallas_call | solution.py:189
  3.7 3.0 %collective-permute-start = (bf16[64,1280]{1,0:T(8,128)(2,1)S(1)}, bf16[64,1280]{1,0:T(8,128)(2,1)S(1)}, u32[]{:S(2)}, u32[]{:S(2)}) collective-permute-start(bf16[64,1280]{1,0:T(8,128)(2,1)S(1)} %shard_map.92), channel_id=1, source_target_pairs={{24,0},{0,8},{8,16},{16,24},{25,1},{1,9},{9,17},{17,25},{26,2},{2,... | collective-permute-start | bytes 491528 | tf_op jit(solution)/shard_map/ppermute | solution.py:285
  7.3 0.0 copy-done.1
  7.4 0.0 copy-done
  7.4 4.5 %shard_map.91 = (bf16[192,1280]{1,0:T(8,128)(2,1)S(1)}, bf16[192,64]{1,0:T(8,128)(2,1)S(1)}, bf16[192,192]{1,0:T(8,128)(2,1)S(1)}) custom-call(s32[1,1]{1,0:T(1,128)S(6)} %copy.10.count_ref, s32[1,1]{1,0:T(1,128)S(6)} %copy.11.send_ref, s32[1,1]{1,0:T(1,128)} %bitcast.me_ref, s32[1,48]{1,0:T(1,128)S(1)} %copy-done, s32[1,48]{1,0:T(1,128)S(1)} %copy-done.1, ...), custom_call_target="tpu_custom_call" | custom-call | flops 754974720 | bytes 5734400 | tf_op jit(solution)/shard_map/pallas_call | solution.py:189
  11.9 0.0 collective-permute-done.borrowed_ref
  11.9 0.3 %shard_map.93 = (bf16[24,1280]{1,0:T(8,128)(2,1)S(1)}, bf16[48,1280]{1,0:T(8,128)(2,1)S(1)}, bf16[24,1280]{1,0:T(8,128)(2,1)S(1)}, bf16[24,1280]{1,0:T(8,128)(2,...) custom-call(bf16[192,1280]{1,0:T(8,128)(2,1)S(1)} %get-tuple-element.16.packed_ref,, ...), custom_call_target="tpu_custom_call" | custom-call | tf_op jit(solution)/shard_map/pallas_call | solution.py:297
  12.2 1.8 %collective-permute-start.1 = (bf16[48,1280]{1,0:T(8,128)(2,1)S(1)}, bf16[48,1280]{1,0:T(8,128)(2,1)S(1)}, u32[]{:S(2)}, u32[]{:S(2)}) collective-permute-start(bf16[48,1280]{1,0:T(8,128)(2,1)S(1)} %get-tuple-element.19), channel_id=1, source_target_pairs={{0,2},{1,3},{2,4},{3,5},{4,6},{5,7},{6,0},{7,1},{8,10},{9,11},{10,... | collective-permute-start | bytes 368648 | tf_op jit(solution)/shard_map/ppermute | solution.py:309
  13.9 2.6 %collective-permute-start.2 = (bf16[24,1280]{1,0:T(8,128)(2,1)S(1)}, bf16[24,1280]{1,0:T(8,128)(2,1)S(1)}, u32[]{:S(2)}, u32[]{:S(2)}) collective-permute-start(bf16[24,1280]{1,0:T(8,128)(2,1)S(1)} %get-tuple-element.20), channel_id=1, source_target_pairs={{0,4},{1,5},{2,6},{3,7},{4,0},{5,1},{6,2},{7,3},{8,12},{9,13},{10,... | collective-permute-start | bytes 184328 | tf_op jit(solution)/shard_map/ppermute | solution.py:309
  16.5 0.0 collective-permute-start.4
  16.5 1.3 %collective-permute-start.5 = (bf16[24,1280]{1,0:T(8,128)(2,1)S(1)}, bf16[24,1280]{1,0:T(8,128)(2,1)S(1)}, u32[]{:S(2)}, u32[]{:S(2)}) collective-permute-start(bf16[24,1280]{1,0:T(8,128)(2,1)S(1)} %get-tuple-element.22), channel_id=1, source_target_pairs={{0,6},{1,7},{2,0},{3,1},{4,2},{5,3},{6,4},{7,5},{8,14},{9,15},{10,... | collective-permute-start | bytes 184328 | tf_op jit(solution)/shard_map/ppermute | solution.py:309
  17.9 2.5 %collective-permute-start.6 = (bf16[24,1280]{1,0:T(8,128)(2,1)S(1)}, bf16[24,1280]{1,0:T(8,128)(2,1)S(1)}, u32[]{:S(2)}, u32[]{:S(2)}) collective-permute-start(bf16[24,1280]{1,0:T(8,128)(2,1)S(1)} %get-tuple-element.23), channel_id=1, source_target_pairs={{0,7},{1,6},{2,1},{3,0},{4,3},{5,2},{6,5},{7,4},{8,15},{9,14},{10,... | collective-permute-start | bytes 184328 | tf_op jit(solution)/shard_map/ppermute | solution.py:309
  20.4 2.6 %collective-permute-done.2.after_ref.refs_3_ = bf16[24,1280]{1,0:T(8,128)(2,1)S(1)} collective-permute-done((bf16[24,1280]{1,0:T(8,128)(2,1)S(1)}, bf16[24,1280]{1,0:T(8,128)(2,1)S(1)}, u32[]{:S(2)}, u32[]{:S(2)}) %collective-permute-start.2) | collective-permute-done | bytes 61472 | tf_op jit(solution)/shard_map/ppermute | solution.py:309
  23.0 0.0 collective-permute-start.7
  23.0 0.0 collective-permute-done.1.double_ref.refs_1_
  23.0 0.6 %collective-permute-start.3 = (bf16[24,1280]{1,0:T(8,128)(2,1)S(1)}, bf16[24,1280]{1,0:T(8,128)(2,1)S(1)}, u32[]{:S(2)}, u32[]{:S(2)}) collective-permute-start(bf16[24,1280]{1,0:T(8,128)(2,1)S(1)} %shard_map.94), channel_id=1, source_target_pairs={{0,1},{1,0},{2,3},{3,2},{4,5},{5,4},{6,7},{7,6},{8,9},{9,8},{10,11... | collective-permute-start | bytes 184328 | tf_op jit(solution)/shard_map/ppermute | solution.py:309
  23.6 0.5 %collective-permute-done.4.refs_4_ = bf16[24,1280]{1,0:T(8,128)(2,1)S(1)} collective-permute-done((bf16[24,1280]{1,0:T(8,128)(2,1)S(1)}, bf16[24,1280]{1,0:T(8,128)(2,1)S(1)}, u32[]{:S(2)}, u32[]{:S(2)}) %collective-permute-start.4) | collective-permute-done | bytes 61472 | tf_op jit(solution)/shard_map/ppermute | solution.py:309
  24.1 0.0 collective-permute-done.5.refs_5_
  24.1 0.0 collective-permute-done.6.refs_6_
  24.1 0.1 collective-permute-done.7.refs_7_
  24.2 0.2 collective-permute-done.3.refs_2_
  24.5 1.2 %shard_map.95 = bf16[48,5120]{1,0:T(8,128)(2,1)} custom-call(bf16[192,192]{1,0:T(8,128)(2,1)S(1)} %get-tuple-element.15.place_ref, bf16[24,1280]{1,0:T(8,128)(2,1)S(1)} %get-tuple-element.18.refs_0_, bf16[48,1280]{1,0:T(8,128)(2,1)S(1)} %collective-permute-done.1.double_ref.refs_1_, bf16[24,1280]{1,0:T(8,128)(2,1)S(1)} %collective-permute-done.3.refs_2_, ...), custom_call_target="tpu_custom_call" | custom-call | tf_op jit(solution)/shard_map/pallas_call | solution.py:325
  (1 shorter events, 0.0 us)
Async XLA Ops:
  0.0 7.4 %copy-start.1 = (s32[1,48]{1,0:T(1,128)S(1)}, s32[1,48]{1,0:T(1,128)}, u32[]{:S(2)}) copy-start(s32[1,48]{1,0:T(1,128)} %row_ref.1) | copy-start | bytes 580
  0.0 7.4 %copy-start = (s32[1,48]{1,0:T(1,128)S(1)}, s32[1,48]{1,0:T(1,128)}, u32[]{:S(2)}) copy-start(s32[1,48]{1,0:T(1,128)} %slot_ref.1) | copy-start | bytes 580
  3.7 8.2 %collective-permute-start = (bf16[64,1280]{1,0:T(8,128)(2,1)S(1)}, bf16[64,1280]{1,0:T(8,128)(2,1)S(1)}, u32[]{:S(2)}, u32[]{:S(2)}) collective-permute-start(bf16[64,1280]{1,0:T(8,128)(2,1)S(1)} %shard_map.92), channel_id=1, source_target_pairs={{24,0},{0,8},{8,16},{16,24},{25,1},{1,9},{9,17},{17,25},{26,2},{2,... | collective-permute-start | bytes 491528 | tf_op jit(solution)/shard_map/ppermute | solution.py:285
  12.2 10.8 %collective-permute-start.1 = (bf16[48,1280]{1,0:T(8,128)(2,1)S(1)}, bf16[48,1280]{1,0:T(8,128)(2,1)S(1)}, u32[]{:S(2)}, u32[]{:S(2)}) collective-permute-start(bf16[48,1280]{1,0:T(8,128)(2,1)S(1)} %get-tuple-element.19), channel_id=1, source_target_pairs={{0,2},{1,3},{2,4},{3,5},{4,6},{5,7},{6,0},{7,1},{8,10},{9,11},{10,... | collective-permute-start | bytes 368648 | tf_op jit(solution)/shard_map/ppermute | solution.py:309
  13.9 9.1 %collective-permute-start.2 = (bf16[24,1280]{1,0:T(8,128)(2,1)S(1)}, bf16[24,1280]{1,0:T(8,128)(2,1)S(1)}, u32[]{:S(2)}, u32[]{:S(2)}) collective-permute-start(bf16[24,1280]{1,0:T(8,128)(2,1)S(1)} %get-tuple-element.20), channel_id=1, source_target_pairs={{0,4},{1,5},{2,6},{3,7},{4,0},{5,1},{6,2},{7,3},{8,12},{9,13},{10,... | collective-permute-start | bytes 184328 | tf_op jit(solution)/shard_map/ppermute | solution.py:309
  16.5 7.6 %collective-permute-start.4 = (bf16[24,1280]{1,0:T(8,128)(2,1)S(1)}, bf16[24,1280]{1,0:T(8,128)(2,1)S(1)}, u32[]{:S(2)}, u32[]{:S(2)}) collective-permute-start(bf16[24,1280]{1,0:T(8,128)(2,1)S(1)} %get-tuple-element.21), channel_id=1, source_target_pairs={{0,5},{1,4},{2,7},{3,6},{4,1},{5,0},{6,3},{7,2},{8,13},{9,12},{10,... | collective-permute-start | bytes 184328 | tf_op jit(solution)/shard_map/ppermute | solution.py:309
  16.5 7.6 %collective-permute-start.5 = (bf16[24,1280]{1,0:T(8,128)(2,1)S(1)}, bf16[24,1280]{1,0:T(8,128)(2,1)S(1)}, u32[]{:S(2)}, u32[]{:S(2)}) collective-permute-start(bf16[24,1280]{1,0:T(8,128)(2,1)S(1)} %get-tuple-element.22), channel_id=1, source_target_pairs={{0,6},{1,7},{2,0},{3,1},{4,2},{5,3},{6,4},{7,5},{8,14},{9,15},{10,... | collective-permute-start | bytes 184328 | tf_op jit(solution)/shard_map/ppermute | solution.py:309
  17.9 6.2 %collective-permute-start.6 = (bf16[24,1280]{1,0:T(8,128)(2,1)S(1)}, bf16[24,1280]{1,0:T(8,128)(2,1)S(1)}, u32[]{:S(2)}, u32[]{:S(2)}) collective-permute-start(bf16[24,1280]{1,0:T(8,128)(2,1)S(1)} %get-tuple-element.23), channel_id=1, source_target_pairs={{0,7},{1,6},{2,1},{3,0},{4,3},{5,2},{6,5},{7,4},{8,15},{9,14},{10,... | collective-permute-start | bytes 184328 | tf_op jit(solution)/shard_map/ppermute | solution.py:309
  23.0 1.2 %collective-permute-start.7 = (bf16[24,1280]{1,0:T(8,128)(2,1)S(1)}, bf16[24,1280]{1,0:T(8,128)(2,1)S(1)}, u32[]{:S(2)}, u32[]{:S(2)}) collective-permute-start(bf16[24,1280]{1,0:T(8,128)(2,1)S(1)} %get-tuple-element.24), channel_id=1, source_target_pairs={{0,1},{1,0},{2,3},{3,2},{4,5},{5,4},{6,7},{7,6},{8,9},{9,8},{10,11... | collective-permute-start | bytes 184328 | tf_op jit(solution)/shard_map/ppermute | solution.py:309
  23.0 1.5 %collective-permute-start.3 = (bf16[24,1280]{1,0:T(8,128)(2,1)S(1)}, bf16[24,1280]{1,0:T(8,128)(2,1)S(1)}, u32[]{:S(2)}, u32[]{:S(2)}) collective-permute-start(bf16[24,1280]{1,0:T(8,128)(2,1)S(1)} %shard_map.94), channel_id=1, source_target_pairs={{0,1},{1,0},{2,3},{3,2},{4,5},{5,4},{6,7},{7,6},{8,9},{9,8},{10,11... | collective-permute-start | bytes 184328 | tf_op jit(solution)/shard_map/ppermute | solution.py:309

commit v6 on v3

--- a/solution.py
+++ b/solution.py
@@ -61,13 +61,13 @@
 
 def encode(
     slot, qkv_hbm, resid_hbm, weight_hbm, bias_hbm, gain_hbm, out_ref,
-    qkv, resid, weight, attended, hidden, bias_ref, gain_ref, sems,
+    qkv, resid, weight, attended, hidden, bias_ref, gain_ref, gain_row, sems,
 ):
     blocks = qkv.shape[0]
     width = resid.shape[2]
     at = pl.ds(slot, blocks)
     pairs = [
-        (qkv_hbm.at[at], qkv), (weight_hbm, weight), (resid_hbm.at[at], resid), (bias_hbm, bias_ref), (gain_hbm, gain_ref)
+        (qkv_hbm.at[at], qkv), (bias_hbm, bias_ref), (gain_hbm, gain_ref), (resid_hbm.at[at], resid), (weight_hbm, weight)
     ]
     copies = [pltpu.make_async_copy(a, b, sems.at[i]) for i, (a, b) in enumerate(pairs)]
     for copy in copies:
@@ -80,23 +80,25 @@
             lambda lo, hi, b=b: qkv[b, :, 2 * width + lo : 2 * width + hi],
             attended, b * WIN, width,
         )
-    for copy in copies[1:]:
+    for copy in copies[1:-1]:
         copy.wait()
     rows = blocks * WIN
-    squares = jnp.zeros((rows, 1), jnp.float32)
     step = 2 * LANES
-    for lo in range(0, width, step):
-        cols = slice(lo, lo + step)
-        h = dot32(attended[...], weight[:, cols])
-        h = h + bias_ref[cols].astype(jnp.float32).reshape(1, step)
-        h = h + resid[:, :, cols].reshape(rows, step).astype(jnp.float32)
+    chunks = [slice(lo, lo + step) for lo in range(0, width, step)]
+    for cols in chunks:
+        bias = bias_ref[cols].astype(jnp.float32).reshape(1, step)
+        hidden[:, cols] = resid[:, :, cols].reshape(rows, step).astype(jnp.float32) + bias
+        gain_row[:, cols] = gain_ref[cols].astype(jnp.float32).reshape(1, step)
+    copies[-1].wait()
+    squares = jnp.zeros((rows, LANES), jnp.float32)
+    for cols in chunks:
+        h = hidden[:, cols] + dot32(attended[...], weight[:, cols])
         hidden[:, cols] = h
-        squares = squares + jnp.sum(h * h, axis=1, keepdims=True)
-    scale = lax.rsqrt(squares * (1.0 / width) + EPS)
-    for lo in range(0, width, step):
-        cols = slice(lo, lo + step)
-        gain = gain_ref[cols].astype(jnp.float32).reshape(1, step)
-        out_ref[:, cols] = (hidden[:, cols] * scale * gain).astype(jnp.bfloat16)
+        h = h * h
+        squares = squares + h[:, :LANES] + h[:, LANES:]
+    scale = lax.rsqrt(jnp.sum(squares, axis=1, keepdims=True) * (1.0 / width) + EPS)
+    for cols in chunks:
+        out_ref[:, cols] = (hidden[:, cols] * scale * gain_row[:, cols]).astype(jnp.bfloat16)
 
 
 def lent_kernel(count_ref, qkv_hbm, resid_hbm, weight_hbm, bias_hbm, gain_hbm, out_ref, *scratch):
@@ -167,6 +169,7 @@
             pltpu.VMEM((rows, width), jnp.float32),
             pltpu.VMEM((width,), jnp.bfloat16),
             pltpu.VMEM((width,), jnp.bfloat16),
+            pltpu.VMEM((1, width), jnp.float32),
             pltpu.SemaphoreType.DMA((5,)),
         ],
         compiler_params=pltpu.CompilerParams(vmem_limit_bytes=24 << 20),

time: 25.8 us -> 26 us (level)
  no operation moved by 1% of the time
where the time goes in v6:
time: 26 us; the launch traced here: 25.6 us
  starting transfers between devices  11.8 us (45%)
  Pallas kernels  8.91 us (34%)
  waiting for transfers between devices  3.51 us (14%)
  between operations  1.38 us (5%)
    ppermute x7, starting transfers between devices, exchange(): lax.ppermute(part, 'seq', [(i, (i // CORES + dz) % n_z * CORES + (i + dc)...  8.82 us
    pallas_call x2, Pallas kernels, encode_call(): pl.pallas_call(kernel, out_shape=out_shape, in_specs=[smem] * len(scalars...  7.49 us
    ppermute x7, waiting for transfers between devices, exchange(): lax.ppermute(part, 'seq', [(i, (i // CORES + dz) % n_z * CORES + (i + dc)...  3.41 us
    ppermute x1, starting transfers between devices, per_device(): lax.ppermute(lent, 'enc', [((i - 1) % n_enc, i) for i in range(n_enc)])  2.99 us
    pallas_call x1, Pallas kernels, per_device(): pl.pallas_call(place_kernel, out_shape=rows_of(row_total, GROUP * width),...  1.15 us
  transfers between devices with their start and end apart: 8, of which 5 were waited for; matrix products, arithmetic and copies ran while one was open for 0% of the time, Pallas kernels for 17%

profile of v6, /device:TPU:0, one launch (start us, length us, event | category | flops | bytes accessed | tf_op | source)
XLA Modules:
  0.0 25.6 jit_solution(4796872771936690583)
XLA Ops:
  0.0 0.0 copy-start.1
  0.0 0.0 copy-start
  0.7 3.1 %shard_map.92 = bf16[64,1280]{1,0:T(8,128)(2,1)S(1)} custom-call(s32[1,1]{1,0:T(1,128)S(6)} %copy.10.count_ref, bf16[4,64,3840]{2,1,0:T(8,128)(2,1)} %qkv_hbm.3, bf16[4,64,1280]{2,1,0:T(8,128)(2,1)} %resid_hbm.3, bf16[1280,1280]{1,0:T(8,128)(2,1)} %weight_hbm.3, bf16[1280]{0:T(1024)(128)(2,1)} %bias_hbm.3, bf16[1280]{0:T(1024)(128)(2,1)} %gain_hbm.3), custom_call_target="tpu_custom_call" | custom-call | flops 251658240 | bytes 4096000 | tf_op jit(solution)/shard_map/pallas_call | solution.py:158
  3.8 3.0 %collective-permute-start = (bf16[64,1280]{1,0:T(8,128)(2,1)S(1)}, bf16[64,1280]{1,0:T(8,128)(2,1)S(1)}, u32[]{:S(2)}, u32[]{:S(2)}) collective-permute-start(bf16[64,1280]{1,0:T(8,128)(2,1)S(1)} %shard_map.92), channel_id=1, source_target_pairs={{24,0},{0,8},{8,16},{16,24},{25,1},{1,9},{9,17},{17,25},{26,2},{2,... | collective-permute-start | bytes 491528 | tf_op jit(solution)/shard_map/ppermute | solution.py:254
  7.4 0.0 copy-done.1
  7.5 0.0 copy-done
  7.5 4.4 %shard_map.91 = (bf16[192,1280]{1,0:T(8,128)(2,1)S(1)}, bf16[192,64]{1,0:T(8,128)(2,1)S(1)}, bf16[192,192]{1,0:T(8,128)(2,1)S(1)}) custom-call(s32[1,1]{1,0:T(1,128)S(6)} %copy.10.count_ref, s32[1,1]{1,0:T(1,128)S(6)} %copy.11.send_ref, s32[1,1]{1,0:T(1,128)} %bitcast.me_ref, s32[1,48]{1,0:T(1,128)S(1)} %copy-done, s32[1,48]{1,0:T(1,128)S(1)} %copy-done.1, ...), custom_call_target="tpu_custom_call" | custom-call | flops 754974720 | bytes 5734400 | tf_op jit(solution)/shard_map/pallas_call | solution.py:158
  11.9 0.1 collective-permute-done.borrowed_ref
  12.0 0.3 %shard_map.93 = (bf16[24,1280]{1,0:T(8,128)(2,1)S(1)}, bf16[48,1280]{1,0:T(8,128)(2,1)S(1)}, bf16[24,1280]{1,0:T(8,128)(2,1)S(1)}, bf16[24,1280]{1,0:T(8,128)(2,...) custom-call(bf16[192,1280]{1,0:T(8,128)(2,1)S(1)} %get-tuple-element.16.packed_ref,, ...), custom_call_target="tpu_custom_call" | custom-call | tf_op jit(solution)/shard_map/pallas_call | solution.py:266
  12.2 1.8 %collective-permute-start.1 = (bf16[48,1280]{1,0:T(8,128)(2,1)S(1)}, bf16[48,1280]{1,0:T(8,128)(2,1)S(1)}, u32[]{:S(2)}, u32[]{:S(2)}) collective-permute-start(bf16[48,1280]{1,0:T(8,128)(2,1)S(1)} %get-tuple-element.19), channel_id=1, source_target_pairs={{0,2},{1,3},{2,4},{3,5},{4,6},{5,7},{6,0},{7,1},{8,10},{9,11},{10,... | collective-permute-start | bytes 368648 | tf_op jit(solution)/shard_map/ppermute | solution.py:278
  14.0 2.6 %collective-permute-start.2 = (bf16[24,1280]{1,0:T(8,128)(2,1)S(1)}, bf16[24,1280]{1,0:T(8,128)(2,1)S(1)}, u32[]{:S(2)}, u32[]{:S(2)}) collective-permute-start(bf16[24,1280]{1,0:T(8,128)(2,1)S(1)} %get-tuple-element.20), channel_id=1, source_target_pairs={{0,4},{1,5},{2,6},{3,7},{4,0},{5,1},{6,2},{7,3},{8,12},{9,13},{10,... | collective-permute-start | bytes 184328 | tf_op jit(solution)/shard_map/ppermute | solution.py:278
  16.6 0.0 collective-permute-start.4
  16.6 1.4 %collective-permute-start.5 = (bf16[24,1280]{1,0:T(8,128)(2,1)S(1)}, bf16[24,1280]{1,0:T(8,128)(2,1)S(1)}, u32[]{:S(2)}, u32[]{:S(2)}) collective-permute-start(bf16[24,1280]{1,0:T(8,128)(2,1)S(1)} %get-tuple-element.22), channel_id=1, source_target_pairs={{0,6},{1,7},{2,0},{3,1},{4,2},{5,3},{6,4},{7,5},{8,14},{9,15},{10,... | collective-permute-start | bytes 184328 | tf_op jit(solution)/shard_map/ppermute | solution.py:278
  18.0 2.5 %collective-permute-start.6 = (bf16[24,1280]{1,0:T(8,128)(2,1)S(1)}, bf16[24,1280]{1,0:T(8,128)(2,1)S(1)}, u32[]{:S(2)}, u32[]{:S(2)}) collective-permute-start(bf16[24,1280]{1,0:T(8,128)(2,1)S(1)} %get-tuple-element.23), channel_id=1, source_target_pairs={{0,7},{1,6},{2,1},{3,0},{4,3},{5,2},{6,5},{7,4},{8,15},{9,14},{10,... | collective-permute-start | bytes 184328 | tf_op jit(solution)/shard_map/ppermute | solution.py:278
  20.5 2.5 %collective-permute-done.2.after_ref.refs_3_ = bf16[24,1280]{1,0:T(8,128)(2,1)S(1)} collective-permute-done((bf16[24,1280]{1,0:T(8,128)(2,1)S(1)}, bf16[24,1280]{1,0:T(8,128)(2,1)S(1)}, u32[]{:S(2)}, u32[]{:S(2)}) %collective-permute-start.2) | collective-permute-done | bytes 61472 | tf_op jit(solution)/shard_map/ppermute | solution.py:278
  23.0 0.0 collective-permute-start.7
  23.0 0.0 collective-permute-done.1.double_ref.refs_1_
  23.0 0.6 %collective-permute-start.3 = (bf16[24,1280]{1,0:T(8,128)(2,1)S(1)}, bf16[24,1280]{1,0:T(8,128)(2,1)S(1)}, u32[]{:S(2)}, u32[]{:S(2)}) collective-permute-start(bf16[24,1280]{1,0:T(8,128)(2,1)S(1)} %shard_map.94), channel_id=1, source_target_pairs={{0,1},{1,0},{2,3},{3,2},{4,5},{5,4},{6,7},{7,6},{8,9},{9,8},{10,11... | collective-permute-start | bytes 184328 | tf_op jit(solution)/shard_map/ppermute | solution.py:278
  23.6 0.5 %collective-permute-done.4.refs_4_ = bf16[24,1280]{1,0:T(8,128)(2,1)S(1)} collective-permute-done((bf16[24,1280]{1,0:T(8,128)(2,1)S(1)}, bf16[24,1280]{1,0:T(8,128)(2,1)S(1)}, u32[]{:S(2)}, u32[]{:S(2)}) %collective-permute-start.4) | collective-permute-done | bytes 61472 | tf_op jit(solution)/shard_map/ppermute | solution.py:278
  24.1 0.0 collective-permute-done.5.refs_5_
  24.1 0.0 collective-permute-done.6.refs_6_
  24.1 0.1 collective-permute-done.7.refs_7_
  24.2 0.2 collective-permute-done.3.refs_2_
  24.5 1.2 %shard_map.95 = bf16[48,5120]{1,0:T(8,128)(2,1)} custom-call(bf16[192,192]{1,0:T(8,128)(2,1)S(1)} %get-tuple-element.15.place_ref, bf16[24,1280]{1,0:T(8,128)(2,1)S(1)} %get-tuple-element.18.refs_0_, bf16[48,1280]{1,0:T(8,128)(2,1)S(1)} %collective-permute-done.1.double_ref.refs_1_, bf16[24,1280]{1,0:T(8,128)(2,1)S(1)} %collective-permute-done.3.refs_2_, ...), custom_call_target="tpu_custom_call" | custom-call | tf_op jit(solution)/shard_map/pallas_call | solution.py:294
  (1 shorter events, 0.0 us)
Async XLA Ops:
  0.0 7.5 %copy-start.1 = (s32[1,48]{1,0:T(1,128)S(1)}, s32[1,48]{1,0:T(1,128)}, u32[]{:S(2)}) copy-start(s32[1,48]{1,0:T(1,128)} %row_ref.1) | copy-start | bytes 580
  0.0 7.5 %copy-start = (s32[1,48]{1,0:T(1,128)S(1)}, s32[1,48]{1,0:T(1,128)}, u32[]{:S(2)}) copy-start(s32[1,48]{1,0:T(1,128)} %slot_ref.1) | copy-start | bytes 580
  3.8 8.1 %collective-permute-start = (bf16[64,1280]{1,0:T(8,128)(2,1)S(1)}, bf16[64,1280]{1,0:T(8,128)(2,1)S(1)}, u32[]{:S(2)}, u32[]{:S(2)}) collective-permute-start(bf16[64,1280]{1,0:T(8,128)(2,1)S(1)} %shard_map.92), channel_id=1, source_target_pairs={{24,0},{0,8},{8,16},{16,24},{25,1},{1,9},{9,17},{17,25},{26,2},{2,... | collective-permute-start | bytes 491528 | tf_op jit(solution)/shard_map/ppermute | solution.py:254
  12.2 10.8 %collective-permute-start.1 = (bf16[48,1280]{1,0:T(8,128)(2,1)S(1)}, bf16[48,1280]{1,0:T(8,128)(2,1)S(1)}, u32[]{:S(2)}, u32[]{:S(2)}) collective-permute-start(bf16[48,1280]{1,0:T(8,128)(2,1)S(1)} %get-tuple-element.19), channel_id=1, source_target_pairs={{0,2},{1,3},{2,4},{3,5},{4,6},{5,7},{6,0},{7,1},{8,10},{9,11},{10,... | collective-permute-start | bytes 368648 | tf_op jit(solution)/shard_map/ppermute | solution.py:278
  14.0 8.9 %collective-permute-start.2 = (bf16[24,1280]{1,0:T(8,128)(2,1)S(1)}, bf16[24,1280]{1,0:T(8,128)(2,1)S(1)}, u32[]{:S(2)}, u32[]{:S(2)}) collective-permute-start(bf16[24,1280]{1,0:T(8,128)(2,1)S(1)} %get-tuple-element.20), channel_id=1, source_target_pairs={{0,4},{1,5},{2,6},{3,7},{4,0},{5,1},{6,2},{7,3},{8,12},{9,13},{10,... | collective-permute-start | bytes 184328 | tf_op jit(solution)/shard_map/ppermute | solution.py:278
  16.6 7.5 %collective-permute-start.4 = (bf16[24,1280]{1,0:T(8,128)(2,1)S(1)}, bf16[24,1280]{1,0:T(8,128)(2,1)S(1)}, u32[]{:S(2)}, u32[]{:S(2)}) collective-permute-start(bf16[24,1280]{1,0:T(8,128)(2,1)S(1)} %get-tuple-element.21), channel_id=1, source_target_pairs={{0,5},{1,4},{2,7},{3,6},{4,1},{5,0},{6,3},{7,2},{8,13},{9,12},{10,... | collective-permute-start | bytes 184328 | tf_op jit(solution)/shard_map/ppermute | solution.py:278
  16.6 7.5 %collective-permute-start.5 = (bf16[24,1280]{1,0:T(8,128)(2,1)S(1)}, bf16[24,1280]{1,0:T(8,128)(2,1)S(1)}, u32[]{:S(2)}, u32[]{:S(2)}) collective-permute-start(bf16[24,1280]{1,0:T(8,128)(2,1)S(1)} %get-tuple-element.22), channel_id=1, source_target_pairs={{0,6},{1,7},{2,0},{3,1},{4,2},{5,3},{6,4},{7,5},{8,14},{9,15},{10,... | collective-permute-start | bytes 184328 | tf_op jit(solution)/shard_map/ppermute | solution.py:278
  18.0 6.1 %collective-permute-start.6 = (bf16[24,1280]{1,0:T(8,128)(2,1)S(1)}, bf16[24,1280]{1,0:T(8,128)(2,1)S(1)}, u32[]{:S(2)}, u32[]{:S(2)}) collective-permute-start(bf16[24,1280]{1,0:T(8,128)(2,1)S(1)} %get-tuple-element.23), channel_id=1, source_target_pairs={{0,7},{1,6},{2,1},{3,0},{4,3},{5,2},{6,5},{7,4},{8,15},{9,14},{10,... | collective-permute-start | bytes 184328 | tf_op jit(solution)/shard_map/ppermute | solution.py:278
  23.0 1.2 %collective-permute-start.7 = (bf16[24,1280]{1,0:T(8,128)(2,1)S(1)}, bf16[24,1280]{1,0:T(8,128)(2,1)S(1)}, u32[]{:S(2)}, u32[]{:S(2)}) collective-permute-start(bf16[24,1280]{1,0:T(8,128)(2,1)S(1)} %get-tuple-element.24), channel_id=1, source_target_pairs={{0,1},{1,0},{2,3},{3,2},{4,5},{5,4},{6,7},{7,6},{8,9},{9,8},{10,11... | collective-permute-start | bytes 184328 | tf_op jit(solution)/shard_map/ppermute | solution.py:278
  23.0 1.5 %collective-permute-start.3 = (bf16[24,1280]{1,0:T(8,128)(2,1)S(1)}, bf16[24,1280]{1,0:T(8,128)(2,1)S(1)}, u32[]{:S(2)}, u32[]{:S(2)}) collective-permute-start(bf16[24,1280]{1,0:T(8,128)(2,1)S(1)} %shard_map.94), channel_id=1, source_target_pairs={{0,1},{1,0},{2,3},{3,2},{4,5},{5,4},{6,7},{7,6},{8,9},{9,8},{10,11... | collective-permute-start | bytes 184328 | tf_op jit(solution)/shard_map/ppermute | solution.py:278

commit v7 on v3

--- a/solution.py
+++ b/solution.py
@@ -187,7 +187,7 @@
         start = stop
 
 
-def forward_kernel(double_ref, after_ref, out_ref):
+def forward_kernel(double_ref, out_ref):
     rows = out_ref.shape[0]
     out_ref[...] = double_ref[...].astype(jnp.float32)[rows:].astype(jnp.bfloat16)
 
@@ -211,17 +211,23 @@
         copy.wait()
 
 
-def exchange_steps(n_seq):
-    return [(0, 0)] + [(dz, dc) for dz in range(1, n_seq // CORES) for dc in range(CORES)] + [(0, 1)]
-
-
-def chip_peer(n_seq, me, step, sign):
+def exchange_steps(n_seq, enc):
     n_z = n_seq // CORES
+    steps = [(dz, dc) for dz in range(1, n_z) for dc in range(CORES)]
+    if enc % 2:
+        steps.sort(key=lambda s: (abs(s[0] - n_z / 2), s[1], s[0]))
+    return [(0, 0)] + steps + [(0, 1)]
+
+
+def chip_peer(n_seq, place, step, sign):
+    n_z = n_seq // CORES
+    odd = lax.rem(place // n_seq, 2) == 1
+    me = lax.rem(place, n_seq)
     offset = jnp.zeros_like(step)
     flip = jnp.zeros_like(step)
-    for i, (dz, dc) in enumerate(exchange_steps(n_seq)):
-        offset = jnp.where(step == i, dz, offset)
-        flip = jnp.where(step == i, dc, flip)
+    for i, (even_step, odd_step) in enumerate(zip(exchange_steps(n_seq, 0), exchange_steps(n_seq, 1))):
+        offset = jnp.where(step == i, jnp.where(odd, odd_step[0], even_step[0]), offset)
+        flip = jnp.where(step == i, jnp.where(odd, odd_step[1], even_step[1]), flip)
     z = me // CORES + sign * offset
     z = jnp.where(z >= n_z, z - n_z, jnp.where(z < 0, z + n_z, z))
     return z * CORES + jnp.bitwise_xor(jnp.bitwise_and(me, 1), flip)
@@ -252,7 +258,7 @@
 
     by_steps = chunk % 8 == 0 and n_seq % CORES == 0
     peer = functools.partial(chip_peer, n_seq) if by_steps else lambda me, step, sign: step
-    me = lax.axis_index("seq").astype(jnp.int32).reshape(1, 1)
+    me = (lax.axis_index("enc") * n_seq + lax.axis_index("seq")).astype(jnp.int32).reshape(1, 1)
     packed, borrow, place = encode_call(
         functools.partial(own_kernel, n_seq, cap, peer), blocks,
         [block_count, send_count, me], [send_slot, lm_row], *data,
@@ -270,18 +276,23 @@
 
     if by_steps:
         n_z = n_seq // CORES
-
-        def exchange(part, dz, dc):
-            return lax.ppermute(
-                part, "seq", [(i, (i // CORES + dz) % n_z * CORES + (i + dc) % CORES) for i in range(n_seq)]
-            )
-
-        double = exchange(outgoing[1], 1, 0)
-        rest = [exchange(part, *step) for part, step in zip(outgoing[2:], exchange_steps(n_seq)[1 + CORES :])]
+        steps = [exchange_steps(n_seq, enc) for enc in range(n_enc)]
+
+        def exchange(part, step, flip=True):
+            route = []
+            for enc in range(n_enc):
+                dz, dc = steps[enc][step]
+                for i in range(n_seq):
+                    to = (i // CORES + dz) % n_z * CORES + (i + (dc if flip else 0)) % CORES
+                    route.append((enc * n_seq + i, enc * n_seq + to))
+            return lax.ppermute(part, ("enc", "seq"), route)
+
+        double = exchange(outgoing[1], 1, flip=False)
+        rest = [exchange(part, 1 + CORES + i) for i, part in enumerate(outgoing[2:])]
         onward = pl.pallas_call(
-            forward_kernel, out_shape=rows_of(chunk), in_specs=[vmem] * 2, out_specs=vmem, compiler_params=small
-        )(double, rest[0])
-        arrived = [outgoing[0], double, exchange(onward, 0, 1), *rest]
+            forward_kernel, out_shape=rows_of(chunk), in_specs=[vmem], out_specs=vmem, compiler_params=small
+        )(double)
+        arrived = [outgoing[0], double, exchange(onward, n_seq - 1), *rest]
     else:
         arrived = [
             lax.all_to_all(

time: 25.8 us -> 26 us (level)
  the two profiles are of different devices: /device:TPU:0 before, /device:TPU:3 now
where the time goes in v7:
time: 26 us; the launch traced here: 25.9 us
  starting transfers between devices  14.5 us (56%)
  Pallas kernels  8.74 us (34%)
  between operations  1.41 us (5%)
  waiting for transfers between devices  1.23 us (5%)
    ppermute x7, starting transfers between devices, exchange(): return lax.ppermute(part, ('enc', 'seq'), route)  13.2 us
    pallas_call x2, Pallas kernels, encode_call(): pl.pallas_call(kernel, out_shape=out_shape, in_specs=[smem] * len(scalars...  7.31 us
    ppermute x1, starting transfers between devices, per_device(): lax.ppermute(lent, 'enc', [((i - 1) % n_enc, i) for i in range(n_enc)])  1.26 us
    ppermute x7, waiting for transfers between devices, exchange(): return lax.ppermute(part, ('enc', 'seq'), route)  1.22 us
    pallas_call x1, Pallas kernels, per_device(): pl.pallas_call(place_kernel, out_shape=rows_of(row_total, GROUP * width),...  1.16 us
  transfers between devices with their start and end apart: 8, of which 3 were waited for; matrix products, arithmetic and copies ran while one was open for 0% of the time, Pallas kernels for 17%

profile of v7, /device:TPU:3, one launch (start us, length us, event | category | flops | bytes accessed | tf_op | source)
XLA Modules:
  0.0 25.9 jit_solution(10766733904990011064)
XLA Ops:
  0.0 0.0 copy-start.1
  0.0 0.0 copy-start
  0.7 3.0 %shard_map.92 = bf16[64,1280]{1,0:T(8,128)(2,1)S(1)} custom-call(s32[1,1]{1,0:T(1,128)S(6)} %copy.10.count_ref, bf16[4,64,3840]{2,1,0:T(8,128)(2,1)} %qkv_hbm.3, bf16[4,64,1280]{2,1,0:T(8,128)(2,1)} %resid_hbm.3, bf16[1280,1280]{1,0:T(8,128)(2,1)} %weight_hbm.3, bf16[1280]{0:T(1024)(128)(2,1)} %bias_hbm.3, bf16[1280]{0:T(1024)(128)(2,1)} %gain_hbm.3), custom_call_target="tpu_custom_call" | custom-call | flops 251658240 | bytes 4096000 | tf_op jit(solution)/shard_map/pallas_call | solution.py:156
  3.7 1.3 %collective-permute-start = (bf16[64,1280]{1,0:T(8,128)(2,1)S(1)}, bf16[64,1280]{1,0:T(8,128)(2,1)S(1)}, u32[]{:S(2)}, u32[]{:S(2)}) collective-permute-start(bf16[64,1280]{1,0:T(8,128)(2,1)S(1)} %shard_map.92), channel_id=1, source_target_pairs={{24,0},{0,8},{8,16},{16,24},{25,1},{1,9},{9,17},{17,25},{26,2},{2,... | collective-permute-start | bytes 491528 | tf_op jit(solution)/shard_map/ppermute | solution.py:257
  5.6 0.0 copy-done.1
  5.6 0.0 copy-done
  5.6 4.3 %shard_map.91 = (bf16[192,1280]{1,0:T(8,128)(2,1)S(1)}, bf16[192,64]{1,0:T(8,128)(2,1)S(1)}, bf16[192,192]{1,0:T(8,128)(2,1)S(1)}) custom-call(s32[1,1]{1,0:T(1,128)S(6)} %copy.10.count_ref, s32[1,1]{1,0:T(1,128)S(6)} %copy.11.send_ref, s32[1,1]{1,0:T(1,128)} %bitcast.me_ref, s32[1,48]{1,0:T(1,128)S(1)} %copy-done, s32[1,48]{1,0:T(1,128)S(1)} %copy-done.1, ...), custom_call_target="tpu_custom_call" | custom-call | flops 754974720 | bytes 5734400 | tf_op jit(solution)/shard_map/pallas_call | solution.py:156
  9.9 0.0 collective-permute-done.borrowed_ref
  10.0 0.3 %shard_map.93 = (bf16[24,1280]{1,0:T(8,128)(2,1)S(1)}, bf16[48,1280]{1,0:T(8,128)(2,1)S(1)}, bf16[24,1280]{1,0:T(8,128)(2,1)S(1)}, bf16[24,1280]{1,0:T(8,128)(2,...) custom-call(bf16[192,1280]{1,0:T(8,128)(2,1)S(1)} %get-tuple-element.16.packed_ref,, ...), custom_call_target="tpu_custom_call" | custom-call | tf_op jit(solution)/shard_map/pallas_call | solution.py:269
  10.2 2.4 %collective-permute-start.1 = (bf16[48,1280]{1,0:T(8,128)(2,1)S(1)}, bf16[48,1280]{1,0:T(8,128)(2,1)S(1)}, u32[]{:S(2)}, u32[]{:S(2)}) collective-permute-start(bf16[48,1280]{1,0:T(8,128)(2,1)S(1)} %get-tuple-element.19), channel_id=1, source_target_pairs={{0,2},{1,3},{2,4},{3,5},{4,6},{5,7},{6,0},{7,1},{8,12},{9,13},{10,... | collective-permute-start | bytes 368648 | tf_op jit(solution)/shard_map/ppermute | solution.py:288
  12.6 1.3 %collective-permute-start.3 = (bf16[24,1280]{1,0:T(8,128)(2,1)S(1)}, bf16[24,1280]{1,0:T(8,128)(2,1)S(1)}, u32[]{:S(2)}, u32[]{:S(2)}) collective-permute-start(bf16[24,1280]{1,0:T(8,128)(2,1)S(1)} %get-tuple-element.20), channel_id=1, source_target_pairs={{0,4},{1,5},{2,6},{3,7},{4,0},{5,1},{6,2},{7,3},{8,10},{9,11},{10,... | collective-permute-start | bytes 184328 | tf_op jit(solution)/shard_map/ppermute | solution.py:288
  13.9 2.0 %collective-permute-start.4 = (bf16[24,1280]{1,0:T(8,128)(2,1)S(1)}, bf16[24,1280]{1,0:T(8,128)(2,1)S(1)}, u32[]{:S(2)}, u32[]{:S(2)}) collective-permute-start(bf16[24,1280]{1,0:T(8,128)(2,1)S(1)} %get-tuple-element.21), channel_id=1, source_target_pairs={{0,5},{1,4},{2,7},{3,6},{4,1},{5,0},{6,3},{7,2},{8,14},{9,15},{10,... | collective-permute-start | bytes 184328 | tf_op jit(solution)/shard_map/ppermute | solution.py:288
  15.9 1.2 %collective-permute-start.5 = (bf16[24,1280]{1,0:T(8,128)(2,1)S(1)}, bf16[24,1280]{1,0:T(8,128)(2,1)S(1)}, u32[]{:S(2)}, u32[]{:S(2)}) collective-permute-start(bf16[24,1280]{1,0:T(8,128)(2,1)S(1)} %get-tuple-element.22), channel_id=1, source_target_pairs={{0,6},{1,7},{2,0},{3,1},{4,2},{5,3},{6,4},{7,5},{8,11},{9,10},{10,... | collective-permute-start | bytes 184328 | tf_op jit(solution)/shard_map/ppermute | solution.py:288
  17.0 2.4 %collective-permute-start.6 = (bf16[24,1280]{1,0:T(8,128)(2,1)S(1)}, bf16[24,1280]{1,0:T(8,128)(2,1)S(1)}, u32[]{:S(2)}, u32[]{:S(2)}) collective-permute-start(bf16[24,1280]{1,0:T(8,128)(2,1)S(1)} %get-tuple-element.23), channel_id=1, source_target_pairs={{0,7},{1,6},{2,1},{3,0},{4,3},{5,2},{6,5},{7,4},{8,15},{9,14},{10,... | collective-permute-start | bytes 184328 | tf_op jit(solution)/shard_map/ppermute | solution.py:288
  19.4 0.0 collective-permute-done.1.double_ref.refs_1_
  19.4 4.0 %collective-permute-start.7 = (bf16[24,1280]{1,0:T(8,128)(2,1)S(1)}, bf16[24,1280]{1,0:T(8,128)(2,1)S(1)}, u32[]{:S(2)}, u32[]{:S(2)}) collective-permute-start(bf16[24,1280]{1,0:T(8,128)(2,1)S(1)} %get-tuple-element.24), channel_id=1, source_target_pairs={{0,1},{1,0},{2,3},{3,2},{4,5},{5,4},{6,7},{7,6},{8,9},{9,8},{10,11... | collective-permute-start | bytes 184328 | tf_op jit(solution)/shard_map/ppermute | solution.py:288
  23.4 0.0 collective-permute-done.3.refs_3_
  23.4 0.1 collective-permute-start.2
  23.5 0.0 collective-permute-done.4.refs_4_
  23.5 0.0 collective-permute-done.5.refs_5_
  23.5 0.2 collective-permute-done.6.refs_6_
  23.6 0.6 %collective-permute-done.7.refs_7_ = bf16[24,1280]{1,0:T(8,128)(2,1)S(1)} collective-permute-done((bf16[24,1280]{1,0:T(8,128)(2,1)S(1)}, bf16[24,1280]{1,0:T(8,128)(2,1)S(1)}, u32[]{:S(2)}, u32[]{:S(2)}) %collective-permute-start.7) | collective-permute-done | bytes 61472 | tf_op jit(solution)/shard_map/ppermute | solution.py:288
  24.3 0.4 %collective-permute-done.2.refs_2_ = bf16[24,1280]{1,0:T(8,128)(2,1)S(1)} collective-permute-done((bf16[24,1280]{1,0:T(8,128)(2,1)S(1)}, bf16[24,1280]{1,0:T(8,128)(2,1)S(1)}, u32[]{:S(2)}, u32[]{:S(2)}) %collective-permute-start.2) | collective-permute-done | bytes 61472 | tf_op jit(solution)/shard_map/ppermute | solution.py:288
  24.7 1.2 %shard_map.95 = bf16[48,5120]{1,0:T(8,128)(2,1)} custom-call(bf16[192,192]{1,0:T(8,128)(2,1)S(1)} %get-tuple-element.15.place_ref, bf16[24,1280]{1,0:T(8,128)(2,1)S(1)} %get-tuple-element.18.refs_0_, bf16[48,1280]{1,0:T(8,128)(2,1)S(1)} %collective-permute-done.1.double_ref.refs_1_, bf16[24,1280]{1,0:T(8,128)(2,1)S(1)} %collective-permute-done.2.refs_2_, ...), custom_call_target="tpu_custom_call" | custom-call | tf_op jit(solution)/shard_map/pallas_call | solution.py:302
  (1 shorter events, 0.0 us)
Async XLA Ops:
  0.0 5.6 %copy-start.1 = (s32[1,48]{1,0:T(1,128)S(1)}, s32[1,48]{1,0:T(1,128)}, u32[]{:S(2)}) copy-start(s32[1,48]{1,0:T(1,128)} %row_ref.1) | copy-start | bytes 580
  0.0 5.6 %copy-start = (s32[1,48]{1,0:T(1,128)S(1)}, s32[1,48]{1,0:T(1,128)}, u32[]{:S(2)}) copy-start(s32[1,48]{1,0:T(1,128)} %slot_ref.1) | copy-start | bytes 580
  3.7 6.2 %collective-permute-start = (bf16[64,1280]{1,0:T(8,128)(2,1)S(1)}, bf16[64,1280]{1,0:T(8,128)(2,1)S(1)}, u32[]{:S(2)}, u32[]{:S(2)}) collective-permute-start(bf16[64,1280]{1,0:T(8,128)(2,1)S(1)} %shard_map.92), channel_id=1, source_target_pairs={{24,0},{0,8},{8,16},{16,24},{25,1},{1,9},{9,17},{17,25},{26,2},{2,... | collective-permute-start | bytes 491528 | tf_op jit(solution)/shard_map/ppermute | solution.py:257
  10.2 9.2 %collective-permute-start.1 = (bf16[48,1280]{1,0:T(8,128)(2,1)S(1)}, bf16[48,1280]{1,0:T(8,128)(2,1)S(1)}, u32[]{:S(2)}, u32[]{:S(2)}) collective-permute-start(bf16[48,1280]{1,0:T(8,128)(2,1)S(1)} %get-tuple-element.19), channel_id=1, source_target_pairs={{0,2},{1,3},{2,4},{3,5},{4,6},{5,7},{6,0},{7,1},{8,12},{9,13},{10,... | collective-permute-start | bytes 368648 | tf_op jit(solution)/shard_map/ppermute | solution.py:288
  12.6 10.8 %collective-permute-start.3 = (bf16[24,1280]{1,0:T(8,128)(2,1)S(1)}, bf16[24,1280]{1,0:T(8,128)(2,1)S(1)}, u32[]{:S(2)}, u32[]{:S(2)}) collective-permute-start(bf16[24,1280]{1,0:T(8,128)(2,1)S(1)} %get-tuple-element.20), channel_id=1, source_target_pairs={{0,4},{1,5},{2,6},{3,7},{4,0},{5,1},{6,2},{7,3},{8,10},{9,11},{10,... | collective-permute-start | bytes 184328 | tf_op jit(solution)/shard_map/ppermute | solution.py:288
  13.9 9.6 %collective-permute-start.4 = (bf16[24,1280]{1,0:T(8,128)(2,1)S(1)}, bf16[24,1280]{1,0:T(8,128)(2,1)S(1)}, u32[]{:S(2)}, u32[]{:S(2)}) collective-permute-start(bf16[24,1280]{1,0:T(8,128)(2,1)S(1)} %get-tuple-element.21), channel_id=1, source_target_pairs={{0,5},{1,4},{2,7},{3,6},{4,1},{5,0},{6,3},{7,2},{8,14},{9,15},{10,... | collective-permute-start | bytes 184328 | tf_op jit(solution)/shard_map/ppermute | solution.py:288
  15.9 7.6 %collective-permute-start.5 = (bf16[24,1280]{1,0:T(8,128)(2,1)S(1)}, bf16[24,1280]{1,0:T(8,128)(2,1)S(1)}, u32[]{:S(2)}, u32[]{:S(2)}) collective-permute-start(bf16[24,1280]{1,0:T(8,128)(2,1)S(1)} %get-tuple-element.22), channel_id=1, source_target_pairs={{0,6},{1,7},{2,0},{3,1},{4,2},{5,3},{6,4},{7,5},{8,11},{9,10},{10,... | collective-permute-start | bytes 184328 | tf_op jit(solution)/shard_map/ppermute | solution.py:288
  17.0 6.6 %collective-permute-start.6 = (bf16[24,1280]{1,0:T(8,128)(2,1)S(1)}, bf16[24,1280]{1,0:T(8,128)(2,1)S(1)}, u32[]{:S(2)}, u32[]{:S(2)}) collective-permute-start(bf16[24,1280]{1,0:T(8,128)(2,1)S(1)} %get-tuple-element.23), channel_id=1, source_target_pairs={{0,7},{1,6},{2,1},{3,0},{4,3},{5,2},{6,5},{7,4},{8,15},{9,14},{10,... | collective-permute-start | bytes 184328 | tf_op jit(solution)/shard_map/ppermute | solution.py:288
  19.4 4.9 %collective-permute-start.7 = (bf16[24,1280]{1,0:T(8,128)(2,1)S(1)}, bf16[24,1280]{1,0:T(8,128)(2,1)S(1)}, u32[]{:S(2)}, u32[]{:S(2)}) collective-permute-start(bf16[24,1280]{1,0:T(8,128)(2,1)S(1)} %get-tuple-element.24), channel_id=1, source_target_pairs={{0,1},{1,0},{2,3},{3,2},{4,5},{5,4},{6,7},{7,6},{8,9},{9,8},{10,11... | collective-permute-start | bytes 184328 | tf_op jit(solution)/shard_map/ppermute | solution.py:288
  23.4 1.3 %collective-permute-start.2 = (bf16[24,1280]{1,0:T(8,128)(2,1)S(1)}, bf16[24,1280]{1,0:T(8,128)(2,1)S(1)}, u32[]{:S(2)}, u32[]{:S(2)}) collective-permute-start(bf16[24,1280]{1,0:T(8,128)(2,1)S(1)} %shard_map.94), channel_id=1, source_target_pairs={{0,1},{1,0},{2,3},{3,2},{4,5},{5,4},{6,7},{7,6},{8,9},{9,8},{10,11... | collective-permute-start | bytes 184328 | tf_op jit(solution)/shard_map/ppermute | solution.py:288

commit v8 on v7

--- a/solution.py
+++ b/solution.py
@@ -14,6 +14,7 @@
 GROUP = 4
 EPS = 1e-6
 CORES = 2
+CHIP_ROUTES = ((3, 2, 1, 0), (1, 3, 0, 2), (2, 0, 3, 1))
 
 NT = (((1,), (1,)), ((), ()))
 
@@ -211,26 +212,21 @@
         copy.wait()
 
 
-def exchange_steps(n_seq, enc):
-    n_z = n_seq // CORES
-    steps = [(dz, dc) for dz in range(1, n_z) for dc in range(CORES)]
-    if enc % 2:
-        steps.sort(key=lambda s: (abs(s[0] - n_z / 2), s[1], s[0]))
-    return [(0, 0)] + steps + [(0, 1)]
-
-
-def chip_peer(n_seq, place, step, sign):
-    n_z = n_seq // CORES
-    odd = lax.rem(place // n_seq, 2) == 1
-    me = lax.rem(place, n_seq)
-    offset = jnp.zeros_like(step)
-    flip = jnp.zeros_like(step)
-    for i, (even_step, odd_step) in enumerate(zip(exchange_steps(n_seq, 0), exchange_steps(n_seq, 1))):
-        offset = jnp.where(step == i, jnp.where(odd, odd_step[0], even_step[0]), offset)
-        flip = jnp.where(step == i, jnp.where(odd, odd_step[1], even_step[1]), flip)
-    z = me // CORES + sign * offset
-    z = jnp.where(z >= n_z, z - n_z, jnp.where(z < 0, z + n_z, z))
-    return z * CORES + jnp.bitwise_xor(jnp.bitwise_and(me, 1), flip)
+def exchange_steps():
+    stay = tuple(range(len(CHIP_ROUTES[0])))
+    return [(stay, 0)] + [(route, dc) for route in CHIP_ROUTES for dc in range(CORES)] + [(stay, 1)]
+
+
+def chip_peer(me, step, sign):
+    z = me // CORES
+    peer = jnp.zeros_like(step)
+    for i, (route, flip) in enumerate(exchange_steps()):
+        chip = sum(
+            jnp.where(z == here, there, 0)
+            for here, there in ((a, b) if sign > 0 else (b, a) for a, b in enumerate(route))
+        )
+        peer = jnp.where(step == i, chip * CORES + jnp.bitwise_xor(jnp.bitwise_and(me, 1), flip), peer)
+    return peer
 
 
 def per_device(
@@ -256,9 +252,9 @@
     lent = encode_call(lent_kernel, 1, [block_count], [], *data, rows_of(WIN), [])
     borrowed = lax.ppermute(lent, "enc", [((i - 1) % n_enc, i) for i in range(n_enc)])
 
-    by_steps = chunk % 8 == 0 and n_seq % CORES == 0
-    peer = functools.partial(chip_peer, n_seq) if by_steps else lambda me, step, sign: step
-    me = (lax.axis_index("enc") * n_seq + lax.axis_index("seq")).astype(jnp.int32).reshape(1, 1)
+    by_steps = chunk % 8 == 0 and n_seq == CORES * len(CHIP_ROUTES[0])
+    peer = chip_peer if by_steps else lambda me, step, sign: step
+    me = lax.axis_index("seq").astype(jnp.int32).reshape(1, 1)
     packed, borrow, place = encode_call(
         functools.partial(own_kernel, n_seq, cap, peer), blocks,
         [block_count, send_count, me], [send_slot, lm_row], *data,
@@ -275,17 +271,12 @@
     )(packed, borrow, borrowed)
 
     if by_steps:
-        n_z = n_seq // CORES
-        steps = [exchange_steps(n_seq, enc) for enc in range(n_enc)]
+        steps = exchange_steps()
 
         def exchange(part, step, flip=True):
-            route = []
-            for enc in range(n_enc):
-                dz, dc = steps[enc][step]
-                for i in range(n_seq):
-                    to = (i // CORES + dz) % n_z * CORES + (i + (dc if flip else 0)) % CORES
-                    route.append((enc * n_seq + i, enc * n_seq + to))
-            return lax.ppermute(part, ("enc", "seq"), route)
+            route, dc = steps[step]
+            to = [route[i // CORES] * CORES + (i + (dc if flip else 0)) % CORES for i in range(n_seq)]
+            return lax.ppermute(part, "seq", list(enumerate(to)))
 
         double = exchange(outgoing[1], 1, flip=False)
         rest = [exchange(part, 1 + CORES + i) for i, part in enumerate(outgoing[2:])]

time: 26 us -> 27.6 us (1.062)
  the two profiles are of different devices: /device:TPU:3 before, /device:TPU:0 now
where the time goes in v8:
time: 27.6 us; the launch traced here: 27.4 us
  starting transfers between devices  11.2 us (41%)
  Pallas kernels  8.69 us (31%)
  waiting for transfers between devices  6.07 us (22%)
  between operations  1.4 us (5%)
    ppermute x7, starting transfers between devices, exchange(): return lax.ppermute(part, 'seq', list(enumerate(to)))  8.26 us
    pallas_call x2, Pallas kernels, encode_call(): pl.pallas_call(kernel, out_shape=out_shape, in_specs=[smem] * len(scalars...  7.27 us
    ppermute x7, waiting for transfers between devices, exchange(): return lax.ppermute(part, 'seq', list(enumerate(to)))  5.85 us
    ppermute x1, starting transfers between devices, per_device(): lax.ppermute(lent, 'enc', [((i - 1) % n_enc, i) for i in range(n_enc)])  2.99 us
    pallas_call x1, Pallas kernels, per_device(): pl.pallas_call(place_kernel, out_shape=rows_of(row_total, GROUP * width),...  1.16 us
  transfers between devices with their start and end apart: 8, of which 3 were waited for; matrix products, arithmetic and copies ran while one was open for 0% of the time, Pallas kernels for 16%

profile of v8, /device:TPU:0, one launch (start us, length us, event | category | flops | bytes accessed | tf_op | source)
XLA Modules:
  0.0 27.4 jit_solution(18443471492756050847)
XLA Ops:
  0.0 0.0 copy-start.1
  0.0 0.0 copy-start
  0.7 3.0 %shard_map.92 = bf16[64,1280]{1,0:T(8,128)(2,1)S(1)} custom-call(s32[1,1]{1,0:T(1,128)S(6)} %copy.10.count_ref, bf16[4,64,3840]{2,1,0:T(8,128)(2,1)} %qkv_hbm.3, bf16[4,64,1280]{2,1,0:T(8,128)(2,1)} %resid_hbm.3, bf16[1280,1280]{1,0:T(8,128)(2,1)} %weight_hbm.3, bf16[1280]{0:T(1024)(128)(2,1)} %bias_hbm.3, bf16[1280]{0:T(1024)(128)(2,1)} %gain_hbm.3), custom_call_target="tpu_custom_call" | custom-call | flops 251658240 | bytes 4096000 | tf_op jit(solution)/shard_map/pallas_call | solution.py:157
  3.7 3.0 %collective-permute-start = (bf16[64,1280]{1,0:T(8,128)(2,1)S(1)}, bf16[64,1280]{1,0:T(8,128)(2,1)S(1)}, u32[]{:S(2)}, u32[]{:S(2)}) collective-permute-start(bf16[64,1280]{1,0:T(8,128)(2,1)S(1)} %shard_map.92), channel_id=1, source_target_pairs={{24,0},{0,8},{8,16},{16,24},{25,1},{1,9},{9,17},{17,25},{26,2},{2,... | collective-permute-start | bytes 491528 | tf_op jit(solution)/shard_map/ppermute | solution.py:253
  7.3 0.0 copy-done.1
  7.4 0.0 copy-done
  7.4 4.3 %shard_map.91 = (bf16[192,1280]{1,0:T(8,128)(2,1)S(1)}, bf16[192,64]{1,0:T(8,128)(2,1)S(1)}, bf16[192,192]{1,0:T(8,128)(2,1)S(1)}) custom-call(s32[1,1]{1,0:T(1,128)S(6)} %copy.10.count_ref, s32[1,1]{1,0:T(1,128)S(6)} %copy.11.send_ref, s32[1,1]{1,0:T(1,128)} %bitcast.me_ref, s32[1,48]{1,0:T(1,128)S(1)} %copy-done, s32[1,48]{1,0:T(1,128)S(1)} %copy-done.1, ...), custom_call_target="tpu_custom_call" | custom-call | flops 754974720 | bytes 5734400 | tf_op jit(solution)/shard_map/pallas_call | solution.py:157
  11.6 0.2 collective-permute-done.borrowed_ref
  11.9 0.3 shard_map.93
  12.1 3.9 %collective-permute-start.1 = (bf16[48,1280]{1,0:T(8,128)(2,1)S(1)}, bf16[48,1280]{1,0:T(8,128)(2,1)S(1)}, u32[]{:S(2)}, u32[]{:S(2)}) collective-permute-start(bf16[48,1280]{1,0:T(8,128)(2,1)S(1)} %get-tuple-element.19), channel_id=1, source_target_pairs={{0,6},{1,7},{2,4},{3,5},{4,2},{5,3},{6,0},{7,1},{8,14},{9,15},{10,... | collective-permute-start | bytes 368648 | tf_op jit(solution)/shard_map/ppermute | solution.py:279
  16.0 0.0 collective-permute-start.3
  16.0 0.0 collective-permute-start.4
  16.0 2.9 %collective-permute-start.5 = (bf16[24,1280]{1,0:T(8,128)(2,1)S(1)}, bf16[24,1280]{1,0:T(8,128)(2,1)S(1)}, u32[]{:S(2)}, u32[]{:S(2)}) collective-permute-start(bf16[24,1280]{1,0:T(8,128)(2,1)S(1)} %get-tuple-element.22), channel_id=1, source_target_pairs={{0,4},{1,5},{2,0},{3,1},{4,6},{5,7},{6,2},{7,3},{8,12},{9,13},{10,... | collective-permute-start | bytes 184328 | tf_op jit(solution)/shard_map/ppermute | solution.py:279
  18.9 1.5 %collective-permute-start.6 = (bf16[24,1280]{1,0:T(8,128)(2,1)S(1)}, bf16[24,1280]{1,0:T(8,128)(2,1)S(1)}, u32[]{:S(2)}, u32[]{:S(2)}) collective-permute-start(bf16[24,1280]{1,0:T(8,128)(2,1)S(1)} %get-tuple-element.23), channel_id=1, source_target_pairs={{0,5},{1,4},{2,1},{3,0},{4,7},{5,6},{6,3},{7,2},{8,13},{9,12},{10,... | collective-permute-start | bytes 184328 | tf_op jit(solution)/shard_map/ppermute | solution.py:279
  20.4 0.0 collective-permute-done.1.double_ref.refs_1_
  20.4 0.0 collective-permute-start.7
  20.4 4.6 %collective-permute-done.3.refs_3_ = bf16[24,1280]{1,0:T(8,128)(2,1)S(1)} collective-permute-done((bf16[24,1280]{1,0:T(8,128)(2,1)S(1)}, bf16[24,1280]{1,0:T(8,128)(2,1)S(1)}, u32[]{:S(2)}, u32[]{:S(2)}) %collective-permute-start.3) | collective-permute-done | bytes 61472 | tf_op jit(solution)/shard_map/ppermute | solution.py:279
  25.0 0.0 collective-permute-start.2
  25.0 0.0 collective-permute-done.4.refs_4_
  25.0 0.0 collective-permute-done.5.refs_5_
  25.0 0.0 collective-permute-done.6.refs_6_
  25.0 0.0 collective-permute-done.7.refs_7_
  25.0 1.2 %collective-permute-done.2.refs_2_ = bf16[24,1280]{1,0:T(8,128)(2,1)S(1)} collective-permute-done((bf16[24,1280]{1,0:T(8,128)(2,1)S(1)}, bf16[24,1280]{1,0:T(8,128)(2,1)S(1)}, u32[]{:S(2)}, u32[]{:S(2)}) %collective-permute-start.2) | collective-permute-done | bytes 61472 | tf_op jit(solution)/shard_map/ppermute | solution.py:279
  26.3 1.2 %shard_map.95 = bf16[48,5120]{1,0:T(8,128)(2,1)} custom-call(bf16[192,192]{1,0:T(8,128)(2,1)S(1)} %get-tuple-element.15.place_ref, bf16[24,1280]{1,0:T(8,128)(2,1)S(1)} %get-tuple-element.18.refs_0_, bf16[48,1280]{1,0:T(8,128)(2,1)S(1)} %collective-permute-done.1.double_ref.refs_1_, bf16[24,1280]{1,0:T(8,128)(2,1)S(1)} %collective-permute-done.2.refs_2_, ...), custom_call_target="tpu_custom_call" | custom-call | tf_op jit(solution)/shard_map/pallas_call | solution.py:293
  (1 shorter events, 0.0 us)
Async XLA Ops:
  0.0 7.3 %copy-start.1 = (s32[1,48]{1,0:T(1,128)S(1)}, s32[1,48]{1,0:T(1,128)}, u32[]{:S(2)}) copy-start(s32[1,48]{1,0:T(1,128)} %row_ref.1) | copy-start | bytes 580
  0.0 7.4 %copy-start = (s32[1,48]{1,0:T(1,128)S(1)}, s32[1,48]{1,0:T(1,128)}, u32[]{:S(2)}) copy-start(s32[1,48]{1,0:T(1,128)} %slot_ref.1) | copy-start | bytes 580
  3.7 8.1 %collective-permute-start = (bf16[64,1280]{1,0:T(8,128)(2,1)S(1)}, bf16[64,1280]{1,0:T(8,128)(2,1)S(1)}, u32[]{:S(2)}, u32[]{:S(2)}) collective-permute-start(bf16[64,1280]{1,0:T(8,128)(2,1)S(1)} %shard_map.92), channel_id=1, source_target_pairs={{24,0},{0,8},{8,16},{16,24},{25,1},{1,9},{9,17},{17,25},{26,2},{2,... | collective-permute-start | bytes 491528 | tf_op jit(solution)/shard_map/ppermute | solution.py:253
  12.1 8.3 %collective-permute-start.1 = (bf16[48,1280]{1,0:T(8,128)(2,1)S(1)}, bf16[48,1280]{1,0:T(8,128)(2,1)S(1)}, u32[]{:S(2)}, u32[]{:S(2)}) collective-permute-start(bf16[48,1280]{1,0:T(8,128)(2,1)S(1)} %get-tuple-element.19), channel_id=1, source_target_pairs={{0,6},{1,7},{2,4},{3,5},{4,2},{5,3},{6,0},{7,1},{8,14},{9,15},{10,... | collective-permute-start | bytes 368648 | tf_op jit(solution)/shard_map/ppermute | solution.py:279
  16.0 9.0 %collective-permute-start.3 = (bf16[24,1280]{1,0:T(8,128)(2,1)S(1)}, bf16[24,1280]{1,0:T(8,128)(2,1)S(1)}, u32[]{:S(2)}, u32[]{:S(2)}) collective-permute-start(bf16[24,1280]{1,0:T(8,128)(2,1)S(1)} %get-tuple-element.20), channel_id=1, source_target_pairs={{0,2},{1,3},{2,6},{3,7},{4,0},{5,1},{6,4},{7,5},{8,10},{9,11},{10,... | collective-permute-start | bytes 184328 | tf_op jit(solution)/shard_map/ppermute | solution.py:279
  16.0 9.0 %collective-permute-start.4 = (bf16[24,1280]{1,0:T(8,128)(2,1)S(1)}, bf16[24,1280]{1,0:T(8,128)(2,1)S(1)}, u32[]{:S(2)}, u32[]{:S(2)}) collective-permute-start(bf16[24,1280]{1,0:T(8,128)(2,1)S(1)} %get-tuple-element.21), channel_id=1, source_target_pairs={{0,3},{1,2},{2,7},{3,6},{4,1},{5,0},{6,5},{7,4},{8,11},{9,10},{10,... | collective-permute-start | bytes 184328 | tf_op jit(solution)/shard_map/ppermute | solution.py:279
  16.0 9.0 %collective-permute-start.5 = (bf16[24,1280]{1,0:T(8,128)(2,1)S(1)}, bf16[24,1280]{1,0:T(8,128)(2,1)S(1)}, u32[]{:S(2)}, u32[]{:S(2)}) collective-permute-start(bf16[24,1280]{1,0:T(8,128)(2,1)S(1)} %get-tuple-element.22), channel_id=1, source_target_pairs={{0,4},{1,5},{2,0},{3,1},{4,6},{5,7},{6,2},{7,3},{8,12},{9,13},{10,... | collective-permute-start | bytes 184328 | tf_op jit(solution)/shard_map/ppermute | solution.py:279
  18.9 6.1 %collective-permute-start.6 = (bf16[24,1280]{1,0:T(8,128)(2,1)S(1)}, bf16[24,1280]{1,0:T(8,128)(2,1)S(1)}, u32[]{:S(2)}, u32[]{:S(2)}) collective-permute-start(bf16[24,1280]{1,0:T(8,128)(2,1)S(1)} %get-tuple-element.23), channel_id=1, source_target_pairs={{0,5},{1,4},{2,1},{3,0},{4,7},{5,6},{6,3},{7,2},{8,13},{9,12},{10,... | collective-permute-start | bytes 184328 | tf_op jit(solution)/shard_map/ppermute | solution.py:279
  20.4 4.7 %collective-permute-start.7 = (bf16[24,1280]{1,0:T(8,128)(2,1)S(1)}, bf16[24,1280]{1,0:T(8,128)(2,1)S(1)}, u32[]{:S(2)}, u32[]{:S(2)}) collective-permute-start(bf16[24,1280]{1,0:T(8,128)(2,1)S(1)} %get-tuple-element.24), channel_id=1, source_target_pairs={{0,1},{1,0},{2,3},{3,2},{4,5},{5,4},{6,7},{7,6},{8,9},{9,8},{10,11... | collective-permute-start | bytes 184328 | tf_op jit(solution)/shard_map/ppermute | solution.py:279
  25.0 1.2 %collective-permute-start.2 = (bf16[24,1280]{1,0:T(8,128)(2,1)S(1)}, bf16[24,1280]{1,0:T(8,128)(2,1)S(1)}, u32[]{:S(2)}, u32[]{:S(2)}) collective-permute-start(bf16[24,1280]{1,0:T(8,128)(2,1)S(1)} %shard_map.94), channel_id=1, source_target_pairs={{0,1},{1,0},{2,3},{3,2},{4,5},{5,4},{6,7},{7,6},{8,9},{9,8},{10,11... | collective-permute-start | bytes 184328 | tf_op jit(solution)/shard_map/ppermute | solution.py:279

commit v9 on v3

--- a/solution.py
+++ b/solution.py
@@ -187,7 +187,7 @@
         start = stop
 
 
-def forward_kernel(double_ref, after_ref, out_ref):
+def forward_kernel(double_ref, out_ref):
     rows = out_ref.shape[0]
     out_ref[...] = double_ref[...].astype(jnp.float32)[rows:].astype(jnp.bfloat16)
 
@@ -212,7 +212,8 @@
 
 
 def exchange_steps(n_seq):
-    return [(0, 0)] + [(dz, dc) for dz in range(1, n_seq // CORES) for dc in range(CORES)] + [(0, 1)]
+    steps = [(dz, dc) for dz in range(1, n_seq // CORES) for dc in range(CORES)]
+    return [(0, 0)] + steps[:CORES] + [(0, 1)] + steps[CORES:]
 
 
 def chip_peer(n_seq, me, step, sign):
@@ -279,8 +280,8 @@
         double = exchange(outgoing[1], 1, 0)
         rest = [exchange(part, *step) for part, step in zip(outgoing[2:], exchange_steps(n_seq)[1 + CORES :])]
         onward = pl.pallas_call(
-            forward_kernel, out_shape=rows_of(chunk), in_specs=[vmem] * 2, out_specs=vmem, compiler_params=small
-        )(double, rest[0])
+            forward_kernel, out_shape=rows_of(chunk), in_specs=[vmem], out_specs=vmem, compiler_params=small
+        )(double)
         arrived = [outgoing[0], double, exchange(onward, 0, 1), *rest]
     else:
         arrived = [

time: 25.8 us -> 26.7 us (1.035)
  starting transfers between devices: 11.8 us -> 12.6 us
  waiting for transfers between devices: 3.51 us -> 3.88 us
    ppermute x7, starting transfers between devices: 8.81 us -> 9.58 us  [exchange(): lax.ppermute(part, 'seq', [(i, (i // CORES + dz) % n_z * CORES + (i + dc)...]
    ppermute x7, waiting for transfers between devices: 3.34 us -> 3.71 us  [exchange(): lax.ppermute(part, 'seq', [(i, (i // CORES + dz) % n_z * CORES + (i + dc)...]
  transfers between devices with their start and end apart: 8 -> 8, of which waited for: 5 -> 5; matrix products, arithmetic and copies ran while one was open for 0% -> 0% of each run, Pallas kernels for 17% -> 16%
where the time goes in v9:
time: 26.7 us; the launch traced here: 26.6 us
  starting transfers between devices  12.6 us (47%)
  Pallas kernels  8.74 us (33%)
  waiting for transfers between devices  3.88 us (15%)
  between operations  1.38 us (5%)
    ppermute x7, starting transfers between devices, exchange(): lax.ppermute(part, 'seq', [(i, (i // CORES + dz) % n_z * CORES + (i + dc)...  9.58 us
    pallas_call x2, Pallas kernels, encode_call(): pl.pallas_call(kernel, out_shape=out_shape, in_specs=[smem] * len(scalars...  7.32 us
    ppermute x7, waiting for transfers between devices, exchange(): lax.ppermute(part, 'seq', [(i, (i // CORES + dz) % n_z * CORES + (i + dc)...  3.71 us
    ppermute x1, starting transfers between devices, per_device(): lax.ppermute(lent, 'enc', [((i - 1) % n_enc, i) for i in range(n_enc)])  2.99 us
    pallas_call x1, Pallas kernels, per_device(): pl.pallas_call(place_kernel, out_shape=rows_of(row_total, GROUP * width),...  1.16 us
  transfers between devices with their start and end apart: 8, of which 5 were waited for; matrix products, arithmetic and copies ran while one was open for 0% of the time, Pallas kernels for 16%

profile of v9, /device:TPU:0, one launch (start us, length us, event | category | flops | bytes accessed | tf_op | source)
XLA Modules:
  0.0 26.6 jit_solution(14357531965628938734)
XLA Ops:
  0.0 0.0 copy-start.1
  0.0 0.0 copy-start
  0.7 3.0 %shard_map.92 = bf16[64,1280]{1,0:T(8,128)(2,1)S(1)} custom-call(s32[1,1]{1,0:T(1,128)S(6)} %copy.10.count_ref, bf16[4,64,3840]{2,1,0:T(8,128)(2,1)} %qkv_hbm.3, bf16[4,64,1280]{2,1,0:T(8,128)(2,1)} %resid_hbm.3, bf16[1280,1280]{1,0:T(8,128)(2,1)} %weight_hbm.3, bf16[1280]{0:T(1024)(128)(2,1)} %bias_hbm.3, bf16[1280]{0:T(1024)(128)(2,1)} %gain_hbm.3), custom_call_target="tpu_custom_call" | custom-call | flops 251658240 | bytes 4096000 | tf_op jit(solution)/shard_map/pallas_call | solution.py:156
  3.7 3.0 %collective-permute-start = (bf16[64,1280]{1,0:T(8,128)(2,1)S(1)}, bf16[64,1280]{1,0:T(8,128)(2,1)S(1)}, u32[]{:S(2)}, u32[]{:S(2)}) collective-permute-start(bf16[64,1280]{1,0:T(8,128)(2,1)S(1)} %shard_map.92), channel_id=1, source_target_pairs={{24,0},{0,8},{8,16},{16,24},{25,1},{1,9},{9,17},{17,25},{26,2},{2,... | collective-permute-start | bytes 491528 | tf_op jit(solution)/shard_map/ppermute | solution.py:252
  7.3 0.0 copy-done.1
  7.4 0.0 copy-done
  7.4 4.3 %shard_map.91 = (bf16[192,1280]{1,0:T(8,128)(2,1)S(1)}, bf16[192,64]{1,0:T(8,128)(2,1)S(1)}, bf16[192,192]{1,0:T(8,128)(2,1)S(1)}) custom-call(s32[1,1]{1,0:T(1,128)S(6)} %copy.10.count_ref, s32[1,1]{1,0:T(1,128)S(6)} %copy.11.send_ref, s32[1,1]{1,0:T(1,128)} %bitcast.me_ref, s32[1,48]{1,0:T(1,128)S(1)} %copy-done, s32[1,48]{1,0:T(1,128)S(1)} %copy-done.1, ...), custom_call_target="tpu_custom_call" | custom-call | flops 754974720 | bytes 5734400 | tf_op jit(solution)/shard_map/pallas_call | solution.py:156
  11.7 0.2 collective-permute-done.borrowed_ref
  11.9 0.3 shard_map.93
  12.1 1.8 %collective-permute-start.1 = (bf16[48,1280]{1,0:T(8,128)(2,1)S(1)}, bf16[48,1280]{1,0:T(8,128)(2,1)S(1)}, u32[]{:S(2)}, u32[]{:S(2)}) collective-permute-start(bf16[48,1280]{1,0:T(8,128)(2,1)S(1)} %get-tuple-element.19), channel_id=1, source_target_pairs={{0,2},{1,3},{2,4},{3,5},{4,6},{5,7},{6,0},{7,1},{8,10},{9,11},{10,... | collective-permute-start | bytes 368648 | tf_op jit(solution)/shard_map/ppermute | solution.py:276
  13.9 0.0 collective-permute-start.3
  13.9 2.6 %collective-permute-start.4 = (bf16[24,1280]{1,0:T(8,128)(2,1)S(1)}, bf16[24,1280]{1,0:T(8,128)(2,1)S(1)}, u32[]{:S(2)}, u32[]{:S(2)}) collective-permute-start(bf16[24,1280]{1,0:T(8,128)(2,1)S(1)} %get-tuple-element.21), channel_id=1, source_target_pairs={{0,4},{1,5},{2,6},{3,7},{4,0},{5,1},{6,2},{7,3},{8,12},{9,13},{10,... | collective-permute-start | bytes 184328 | tf_op jit(solution)/shard_map/ppermute | solution.py:276
  16.5 0.2 collective-permute-start.5
  16.7 2.1 %collective-permute-start.6 = (bf16[24,1280]{1,0:T(8,128)(2,1)S(1)}, bf16[24,1280]{1,0:T(8,128)(2,1)S(1)}, u32[]{:S(2)}, u32[]{:S(2)}) collective-permute-start(bf16[24,1280]{1,0:T(8,128)(2,1)S(1)} %get-tuple-element.23), channel_id=1, source_target_pairs={{0,6},{1,7},{2,0},{3,1},{4,2},{5,3},{6,4},{7,5},{8,14},{9,15},{10,... | collective-permute-start | bytes 184328 | tf_op jit(solution)/shard_map/ppermute | solution.py:276
  18.8 0.1 collective-permute-done.1.double_ref.refs_1_
  18.9 1.4 %collective-permute-start.7 = (bf16[24,1280]{1,0:T(8,128)(2,1)S(1)}, bf16[24,1280]{1,0:T(8,128)(2,1)S(1)}, u32[]{:S(2)}, u32[]{:S(2)}) collective-permute-start(bf16[24,1280]{1,0:T(8,128)(2,1)S(1)} %get-tuple-element.24), channel_id=1, source_target_pairs={{0,7},{1,6},{2,1},{3,0},{4,3},{5,2},{6,5},{7,4},{8,15},{9,14},{10,... | collective-permute-start | bytes 184328 | tf_op jit(solution)/shard_map/ppermute | solution.py:276
  20.4 0.0 collective-permute-done.3.refs_3_
  20.4 1.5 %collective-permute-start.2 = (bf16[24,1280]{1,0:T(8,128)(2,1)S(1)}, bf16[24,1280]{1,0:T(8,128)(2,1)S(1)}, u32[]{:S(2)}, u32[]{:S(2)}) collective-permute-start(bf16[24,1280]{1,0:T(8,128)(2,1)S(1)} %shard_map.94), channel_id=1, source_target_pairs={{0,1},{1,0},{2,3},{3,2},{4,5},{5,4},{6,7},{7,6},{8,9},{9,8},{10,11... | collective-permute-start | bytes 184328 | tf_op jit(solution)/shard_map/ppermute | solution.py:276
  21.8 1.1 %collective-permute-done.4.refs_4_ = bf16[24,1280]{1,0:T(8,128)(2,1)S(1)} collective-permute-done((bf16[24,1280]{1,0:T(8,128)(2,1)S(1)}, bf16[24,1280]{1,0:T(8,128)(2,1)S(1)}, u32[]{:S(2)}, u32[]{:S(2)}) %collective-permute-start.4) | collective-permute-done | bytes 61472 | tf_op jit(solution)/shard_map/ppermute | solution.py:276
  22.9 1.2 %collective-permute-done.5.refs_5_ = bf16[24,1280]{1,0:T(8,128)(2,1)S(1)} collective-permute-done((bf16[24,1280]{1,0:T(8,128)(2,1)S(1)}, bf16[24,1280]{1,0:T(8,128)(2,1)S(1)}, u32[]{:S(2)}, u32[]{:S(2)}) %collective-permute-start.5) | collective-permute-done | bytes 61472 | tf_op jit(solution)/shard_map/ppermute | solution.py:276
  24.2 0.0 collective-permute-done.6.refs_6_
  24.2 1.2 %collective-permute-done.7.refs_7_ = bf16[24,1280]{1,0:T(8,128)(2,1)S(1)} collective-permute-done((bf16[24,1280]{1,0:T(8,128)(2,1)S(1)}, bf16[24,1280]{1,0:T(8,128)(2,1)S(1)}, u32[]{:S(2)}, u32[]{:S(2)}) %collective-permute-start.7) | collective-permute-done | bytes 61472 | tf_op jit(solution)/shard_map/ppermute | solution.py:276
  25.4 0.0 collective-permute-done.2.refs_2_
  25.4 1.2 %shard_map.95 = bf16[48,5120]{1,0:T(8,128)(2,1)} custom-call(bf16[192,192]{1,0:T(8,128)(2,1)S(1)} %get-tuple-element.15.place_ref, bf16[24,1280]{1,0:T(8,128)(2,1)S(1)} %get-tuple-element.18.refs_0_, bf16[48,1280]{1,0:T(8,128)(2,1)S(1)} %collective-permute-done.1.double_ref.refs_1_, bf16[24,1280]{1,0:T(8,128)(2,1)S(1)} %collective-permute-done.2.refs_2_, ...), custom_call_target="tpu_custom_call" | custom-call | tf_op jit(solution)/shard_map/pallas_call | solution.py:292
  (1 shorter events, 0.0 us)
Async XLA Ops:
  0.0 7.3 %copy-start.1 = (s32[1,48]{1,0:T(1,128)S(1)}, s32[1,48]{1,0:T(1,128)}, u32[]{:S(2)}) copy-start(s32[1,48]{1,0:T(1,128)} %row_ref.1) | copy-start | bytes 580
  0.0 7.4 %copy-start = (s32[1,48]{1,0:T(1,128)S(1)}, s32[1,48]{1,0:T(1,128)}, u32[]{:S(2)}) copy-start(s32[1,48]{1,0:T(1,128)} %slot_ref.1) | copy-start | bytes 580
  3.7 8.1 %collective-permute-start = (bf16[64,1280]{1,0:T(8,128)(2,1)S(1)}, bf16[64,1280]{1,0:T(8,128)(2,1)S(1)}, u32[]{:S(2)}, u32[]{:S(2)}) collective-permute-start(bf16[64,1280]{1,0:T(8,128)(2,1)S(1)} %shard_map.92), channel_id=1, source_target_pairs={{24,0},{0,8},{8,16},{16,24},{25,1},{1,9},{9,17},{17,25},{26,2},{2,... | collective-permute-start | bytes 491528 | tf_op jit(solution)/shard_map/ppermute | solution.py:252
  12.1 6.8 %collective-permute-start.1 = (bf16[48,1280]{1,0:T(8,128)(2,1)S(1)}, bf16[48,1280]{1,0:T(8,128)(2,1)S(1)}, u32[]{:S(2)}, u32[]{:S(2)}) collective-permute-start(bf16[48,1280]{1,0:T(8,128)(2,1)S(1)} %get-tuple-element.19), channel_id=1, source_target_pairs={{0,2},{1,3},{2,4},{3,5},{4,6},{5,7},{6,0},{7,1},{8,10},{9,11},{10,... | collective-permute-start | bytes 368648 | tf_op jit(solution)/shard_map/ppermute | solution.py:276
  13.9 6.4 %collective-permute-start.3 = (bf16[24,1280]{1,0:T(8,128)(2,1)S(1)}, bf16[24,1280]{1,0:T(8,128)(2,1)S(1)}, u32[]{:S(2)}, u32[]{:S(2)}) collective-permute-start(bf16[24,1280]{1,0:T(8,128)(2,1)S(1)} %get-tuple-element.20), channel_id=1, source_target_pairs={{0,1},{1,0},{2,3},{3,2},{4,5},{5,4},{6,7},{7,6},{8,9},{9,8},{10,11... | collective-permute-start | bytes 184328 | tf_op jit(solution)/shard_map/ppermute | solution.py:276
  13.9 9.0 %collective-permute-start.4 = (bf16[24,1280]{1,0:T(8,128)(2,1)S(1)}, bf16[24,1280]{1,0:T(8,128)(2,1)S(1)}, u32[]{:S(2)}, u32[]{:S(2)}) collective-permute-start(bf16[24,1280]{1,0:T(8,128)(2,1)S(1)} %get-tuple-element.21), channel_id=1, source_target_pairs={{0,4},{1,5},{2,6},{3,7},{4,0},{5,1},{6,2},{7,3},{8,12},{9,13},{10,... | collective-permute-start | bytes 184328 | tf_op jit(solution)/shard_map/ppermute | solution.py:276
  16.5 7.6 %collective-permute-start.5 = (bf16[24,1280]{1,0:T(8,128)(2,1)S(1)}, bf16[24,1280]{1,0:T(8,128)(2,1)S(1)}, u32[]{:S(2)}, u32[]{:S(2)}) collective-permute-start(bf16[24,1280]{1,0:T(8,128)(2,1)S(1)} %get-tuple-element.22), channel_id=1, source_target_pairs={{0,5},{1,4},{2,7},{3,6},{4,1},{5,0},{6,3},{7,2},{8,13},{9,12},{10,... | collective-permute-start | bytes 184328 | tf_op jit(solution)/shard_map/ppermute | solution.py:276
  16.7 7.5 %collective-permute-start.6 = (bf16[24,1280]{1,0:T(8,128)(2,1)S(1)}, bf16[24,1280]{1,0:T(8,128)(2,1)S(1)}, u32[]{:S(2)}, u32[]{:S(2)}) collective-permute-start(bf16[24,1280]{1,0:T(8,128)(2,1)S(1)} %get-tuple-element.23), channel_id=1, source_target_pairs={{0,6},{1,7},{2,0},{3,1},{4,2},{5,3},{6,4},{7,5},{8,14},{9,15},{10,... | collective-permute-start | bytes 184328 | tf_op jit(solution)/shard_map/ppermute | solution.py:276
  18.9 6.5 %collective-permute-start.7 = (bf16[24,1280]{1,0:T(8,128)(2,1)S(1)}, bf16[24,1280]{1,0:T(8,128)(2,1)S(1)}, u32[]{:S(2)}, u32[]{:S(2)}) collective-permute-start(bf16[24,1280]{1,0:T(8,128)(2,1)S(1)} %get-tuple-element.24), channel_id=1, source_target_pairs={{0,7},{1,6},{2,1},{3,0},{4,3},{5,2},{6,5},{7,4},{8,15},{9,14},{10,... | collective-permute-start | bytes 184328 | tf_op jit(solution)/shard_map/ppermute | solution.py:276
  20.4 5.0 %collective-permute-start.2 = (bf16[24,1280]{1,0:T(8,128)(2,1)S(1)}, bf16[24,1280]{1,0:T(8,128)(2,1)S(1)}, u32[]{:S(2)}, u32[]{:S(2)}) collective-permute-start(bf16[24,1280]{1,0:T(8,128)(2,1)S(1)} %shard_map.94), channel_id=1, source_target_pairs={{0,1},{1,0},{2,3},{3,2},{4,5},{5,4},{6,7},{7,6},{8,9},{9,8},{10,11... | collective-permute-start | bytes 184328 | tf_op jit(solution)/shard_map/ppermute | solution.py:276

commit v10 on v9

--- a/solution.py
+++ b/solution.py
@@ -197,7 +197,8 @@
     tokens = out.shape[0]
     chunks = [ref[...].astype(jnp.float32) for ref in in_refs]
     if len(chunks) > 1:
-        chunks[1] = chunks[1][: chunks[0].shape[0]]
+        own, double, passed, partner, *singles = chunks
+        chunks = [own, double[: own.shape[0]], passed, *singles, partner]
     arrived = chunks[0] if len(chunks) == 1 else jnp.concatenate(chunks, axis=0)
     arrived = arrived.astype(jnp.bfloat16)
     width = arrived.shape[1]
@@ -212,8 +213,9 @@
 
 
 def exchange_steps(n_seq):
-    steps = [(dz, dc) for dz in range(1, n_seq // CORES) for dc in range(CORES)]
-    return [(0, 0)] + steps[:CORES] + [(0, 1)] + steps[CORES:]
+    n_z = n_seq // CORES
+    offsets = sorted(range(1, n_z), key=lambda dz: (dz != n_z // 2, dz))
+    return [(0, 0)] + [(dz, dc) for dz in offsets for dc in range(CORES)] + [(0, 1)]
 
 
 def chip_peer(n_seq, me, step, sign):
@@ -277,12 +279,12 @@
                 part, "seq", [(i, (i // CORES + dz) % n_z * CORES + (i + dc) % CORES) for i in range(n_seq)]
             )
 
-        double = exchange(outgoing[1], 1, 0)
+        double = exchange(outgoing[1], n_z // 2, 0)
         rest = [exchange(part, *step) for part, step in zip(outgoing[2:], exchange_steps(n_seq)[1 + CORES :])]
         onward = pl.pallas_call(
             forward_kernel, out_shape=rows_of(chunk), in_specs=[vmem], out_specs=vmem, compiler_params=small
         )(double)
-        arrived = [outgoing[0], double, exchange(onward, 0, 1), *rest]
+        arrived = [outgoing[0], double, exchange(onward, 0, 1), rest[-1], *rest[:-1]]
     else:
         arrived = [
             lax.all_to_all(

time: 26.7 us -> 28.3 us (1.060)
  waiting for transfers between devices: 3.88 us -> 5.66 us
  starting transfers between devices: 12.6 us -> 12.3 us
    ppermute x7, waiting for transfers between devices: 3.71 us -> 5.49 us  [exchange(): lax.ppermute(part, 'seq', [(i, (i // CORES + dz) % n_z * CORES + (i + dc)...]
  transfers between devices with their start and end apart: 8 -> 8, of which waited for: 5 -> 3; matrix products, arithmetic and copies ran while one was open for 0% -> 0% of each run, Pallas kernels for 16% -> 15%
where the time goes in v10:
time: 28.3 us; the launch traced here: 28.1 us
  starting transfers between devices  12.3 us (43%)
  Pallas kernels  8.74 us (31%)
  waiting for transfers between devices  5.66 us (20%)
  between operations  1.39 us (5%)
    ppermute x7, starting transfers between devices, exchange(): lax.ppermute(part, 'seq', [(i, (i // CORES + dz) % n_z * CORES + (i + dc)...  9.33 us
    pallas_call x2, Pallas kernels, encode_call(): pl.pallas_call(kernel, out_shape=out_shape, in_specs=[smem] * len(scalars...  7.32 us
    ppermute x7, waiting for transfers between devices, exchange(): lax.ppermute(part, 'seq', [(i, (i // CORES + dz) % n_z * CORES + (i + dc)...  5.49 us
    ppermute x1, starting transfers between devices, per_device(): lax.ppermute(lent, 'enc', [((i - 1) % n_enc, i) for i in range(n_enc)])  2.99 us
    pallas_call x1, Pallas kernels, per_device(): pl.pallas_call(place_kernel, out_shape=rows_of(row_total, GROUP * width),...  1.16 us
  transfers between devices with their start and end apart: 8, of which 3 were waited for; matrix products, arithmetic and copies ran while one was open for 0% of the time, Pallas kernels for 15%

profile of v10, /device:TPU:0, one launch (start us, length us, event | category | flops | bytes accessed | tf_op | source)
XLA Modules:
  0.0 28.1 jit_solution(16655709514982667884)
XLA Ops:
  0.0 0.0 copy-start.1
  0.0 0.0 copy-start
  0.7 3.0 %shard_map.92 = bf16[64,1280]{1,0:T(8,128)(2,1)S(1)} custom-call(s32[1,1]{1,0:T(1,128)S(6)} %copy.10.count_ref, bf16[4,64,3840]{2,1,0:T(8,128)(2,1)} %qkv_hbm.3, bf16[4,64,1280]{2,1,0:T(8,128)(2,1)} %resid_hbm.3, bf16[1280,1280]{1,0:T(8,128)(2,1)} %weight_hbm.3, bf16[1280]{0:T(1024)(128)(2,1)} %bias_hbm.3, bf16[1280]{0:T(1024)(128)(2,1)} %gain_hbm.3), custom_call_target="tpu_custom_call" | custom-call | flops 251658240 | bytes 4096000 | tf_op jit(solution)/shard_map/pallas_call | solution.py:156
  3.7 3.0 %collective-permute-start = (bf16[64,1280]{1,0:T(8,128)(2,1)S(1)}, bf16[64,1280]{1,0:T(8,128)(2,1)S(1)}, u32[]{:S(2)}, u32[]{:S(2)}) collective-permute-start(bf16[64,1280]{1,0:T(8,128)(2,1)S(1)} %shard_map.92), channel_id=1, source_target_pairs={{24,0},{0,8},{8,16},{16,24},{25,1},{1,9},{9,17},{17,25},{26,2},{2,... | collective-permute-start | bytes 491528 | tf_op jit(solution)/shard_map/ppermute | solution.py:254
  7.3 0.0 copy-done.1
  7.4 0.0 copy-done
  7.4 4.3 %shard_map.91 = (bf16[192,1280]{1,0:T(8,128)(2,1)S(1)}, bf16[192,64]{1,0:T(8,128)(2,1)S(1)}, bf16[192,192]{1,0:T(8,128)(2,1)S(1)}) custom-call(s32[1,1]{1,0:T(1,128)S(6)} %copy.10.count_ref, s32[1,1]{1,0:T(1,128)S(6)} %copy.11.send_ref, s32[1,1]{1,0:T(1,128)} %bitcast.me_ref, s32[1,48]{1,0:T(1,128)S(1)} %copy-done, s32[1,48]{1,0:T(1,128)S(1)} %copy-done.1, ...), custom_call_target="tpu_custom_call" | custom-call | flops 754974720 | bytes 5734400 | tf_op jit(solution)/shard_map/pallas_call | solution.py:156
  11.7 0.2 collective-permute-done.borrowed_ref
  11.9 0.3 shard_map.93
  12.1 2.8 %collective-permute-start.1 = (bf16[48,1280]{1,0:T(8,128)(2,1)S(1)}, bf16[48,1280]{1,0:T(8,128)(2,1)S(1)}, u32[]{:S(2)}, u32[]{:S(2)}) collective-permute-start(bf16[48,1280]{1,0:T(8,128)(2,1)S(1)} %get-tuple-element.19), channel_id=1, source_target_pairs={{0,4},{1,5},{2,6},{3,7},{4,0},{5,1},{6,2},{7,3},{8,12},{9,13},{10,... | collective-permute-start | bytes 368648 | tf_op jit(solution)/shard_map/ppermute | solution.py:278
  15.0 0.0 collective-permute-start.3
  15.0 1.6 %collective-permute-start.4 = (bf16[24,1280]{1,0:T(8,128)(2,1)S(1)}, bf16[24,1280]{1,0:T(8,128)(2,1)S(1)}, u32[]{:S(2)}, u32[]{:S(2)}) collective-permute-start(bf16[24,1280]{1,0:T(8,128)(2,1)S(1)} %get-tuple-element.21), channel_id=1, source_target_pairs={{0,2},{1,3},{2,4},{3,5},{4,6},{5,7},{6,0},{7,1},{8,10},{9,11},{10,... | collective-permute-start | bytes 184328 | tf_op jit(solution)/shard_map/ppermute | solution.py:278
  16.5 0.1 collective-permute-start.5
  16.7 3.5 %collective-permute-start.6 = (bf16[24,1280]{1,0:T(8,128)(2,1)S(1)}, bf16[24,1280]{1,0:T(8,128)(2,1)S(1)}, u32[]{:S(2)}, u32[]{:S(2)}) collective-permute-start(bf16[24,1280]{1,0:T(8,128)(2,1)S(1)} %get-tuple-element.23), channel_id=1, source_target_pairs={{0,6},{1,7},{2,0},{3,1},{4,2},{5,3},{6,4},{7,5},{8,14},{9,15},{10,... | collective-permute-start | bytes 184328 | tf_op jit(solution)/shard_map/ppermute | solution.py:278
  20.2 3.1 %collective-permute-done.1.double_ref.refs_1_ = bf16[48,1280]{1,0:T(8,128)(2,1)S(1)} collective-permute-done((bf16[48,1280]{1,0:T(8,128)(2,1)S(1)}, bf16[48,1280]{1,0:T(8,128)(2,1)S(1)}, u32[]{:S(2)}, u32[]{:S(2)}) %collective-permute-start.1) | collective-permute-done | bytes 122912 | tf_op jit(solution)/shard_map/ppermute | solution.py:278
  23.3 0.0 collective-permute-start.7
  23.3 0.0 collective-permute-done.3.refs_3_
  23.3 1.2 %collective-permute-start.2 = (bf16[24,1280]{1,0:T(8,128)(2,1)S(1)}, bf16[24,1280]{1,0:T(8,128)(2,1)S(1)}, u32[]{:S(2)}, u32[]{:S(2)}) collective-permute-start(bf16[24,1280]{1,0:T(8,128)(2,1)S(1)} %shard_map.94), channel_id=1, source_target_pairs={{0,1},{1,0},{2,3},{3,2},{4,5},{5,4},{6,7},{7,6},{8,9},{9,8},{10,11... | collective-permute-start | bytes 184328 | tf_op jit(solution)/shard_map/ppermute | solution.py:278
  24.6 0.0 collective-permute-done.4.refs_4_
  24.6 0.0 collective-permute-done.5.refs_5_
  24.6 0.0 collective-permute-done.6.refs_6_
  24.6 2.4 %collective-permute-done.7.refs_7_ = bf16[24,1280]{1,0:T(8,128)(2,1)S(1)} collective-permute-done((bf16[24,1280]{1,0:T(8,128)(2,1)S(1)}, bf16[24,1280]{1,0:T(8,128)(2,1)S(1)}, u32[]{:S(2)}, u32[]{:S(2)}) %collective-permute-start.7) | collective-permute-done | bytes 61472 | tf_op jit(solution)/shard_map/ppermute | solution.py:278
  27.0 0.0 collective-permute-done.2.refs_2_
  27.0 1.2 %shard_map.95 = bf16[48,5120]{1,0:T(8,128)(2,1)} custom-call(bf16[192,192]{1,0:T(8,128)(2,1)S(1)} %get-tuple-element.15.place_ref, bf16[24,1280]{1,0:T(8,128)(2,1)S(1)} %get-tuple-element.18.refs_0_, bf16[48,1280]{1,0:T(8,128)(2,1)S(1)} %collective-permute-done.1.double_ref.refs_1_, bf16[24,1280]{1,0:T(8,128)(2,1)S(1)} %collective-permute-done.2.refs_2_, ...), custom_call_target="tpu_custom_call" | custom-call | tf_op jit(solution)/shard_map/pallas_call | solution.py:294
  (1 shorter events, 0.0 us)
Async XLA Ops:
  0.0 7.3 %copy-start.1 = (s32[1,48]{1,0:T(1,128)S(1)}, s32[1,48]{1,0:T(1,128)}, u32[]{:S(2)}) copy-start(s32[1,48]{1,0:T(1,128)} %row_ref.1) | copy-start | bytes 580
  0.0 7.4 %copy-start = (s32[1,48]{1,0:T(1,128)S(1)}, s32[1,48]{1,0:T(1,128)}, u32[]{:S(2)}) copy-start(s32[1,48]{1,0:T(1,128)} %slot_ref.1) | copy-start | bytes 580
  3.7 8.1 %collective-permute-start = (bf16[64,1280]{1,0:T(8,128)(2,1)S(1)}, bf16[64,1280]{1,0:T(8,128)(2,1)S(1)}, u32[]{:S(2)}, u32[]{:S(2)}) collective-permute-start(bf16[64,1280]{1,0:T(8,128)(2,1)S(1)} %shard_map.92), channel_id=1, source_target_pairs={{24,0},{0,8},{8,16},{16,24},{25,1},{1,9},{9,17},{17,25},{26,2},{2,... | collective-permute-start | bytes 491528 | tf_op jit(solution)/shard_map/ppermute | solution.py:254
  12.1 11.2 %collective-permute-start.1 = (bf16[48,1280]{1,0:T(8,128)(2,1)S(1)}, bf16[48,1280]{1,0:T(8,128)(2,1)S(1)}, u32[]{:S(2)}, u32[]{:S(2)}) collective-permute-start(bf16[48,1280]{1,0:T(8,128)(2,1)S(1)} %get-tuple-element.19), channel_id=1, source_target_pairs={{0,4},{1,5},{2,6},{3,7},{4,0},{5,1},{6,2},{7,3},{8,12},{9,13},{10,... | collective-permute-start | bytes 368648 | tf_op jit(solution)/shard_map/ppermute | solution.py:278
  15.0 8.4 %collective-permute-start.3 = (bf16[24,1280]{1,0:T(8,128)(2,1)S(1)}, bf16[24,1280]{1,0:T(8,128)(2,1)S(1)}, u32[]{:S(2)}, u32[]{:S(2)}) collective-permute-start(bf16[24,1280]{1,0:T(8,128)(2,1)S(1)} %get-tuple-element.20), channel_id=1, source_target_pairs={{0,1},{1,0},{2,3},{3,2},{4,5},{5,4},{6,7},{7,6},{8,9},{9,8},{10,11... | collective-permute-start | bytes 184328 | tf_op jit(solution)/shard_map/ppermute | solution.py:278
  15.0 9.6 %collective-permute-start.4 = (bf16[24,1280]{1,0:T(8,128)(2,1)S(1)}, bf16[24,1280]{1,0:T(8,128)(2,1)S(1)}, u32[]{:S(2)}, u32[]{:S(2)}) collective-permute-start(bf16[24,1280]{1,0:T(8,128)(2,1)S(1)} %get-tuple-element.21), channel_id=1, source_target_pairs={{0,2},{1,3},{2,4},{3,5},{4,6},{5,7},{6,0},{7,1},{8,10},{9,11},{10,... | collective-permute-start | bytes 184328 | tf_op jit(solution)/shard_map/ppermute | solution.py:278
  16.5 8.0 %collective-permute-start.5 = (bf16[24,1280]{1,0:T(8,128)(2,1)S(1)}, bf16[24,1280]{1,0:T(8,128)(2,1)S(1)}, u32[]{:S(2)}, u32[]{:S(2)}) collective-permute-start(bf16[24,1280]{1,0:T(8,128)(2,1)S(1)} %get-tuple-element.22), channel_id=1, source_target_pairs={{0,3},{1,2},{2,5},{3,4},{4,7},{5,6},{6,1},{7,0},{8,11},{9,10},{10,... | collective-permute-start | bytes 184328 | tf_op jit(solution)/shard_map/ppermute | solution.py:278
  16.7 7.9 %collective-permute-start.6 = (bf16[24,1280]{1,0:T(8,128)(2,1)S(1)}, bf16[24,1280]{1,0:T(8,128)(2,1)S(1)}, u32[]{:S(2)}, u32[]{:S(2)}) collective-permute-start(bf16[24,1280]{1,0:T(8,128)(2,1)S(1)} %get-tuple-element.23), channel_id=1, source_target_pairs={{0,6},{1,7},{2,0},{3,1},{4,2},{5,3},{6,4},{7,5},{8,14},{9,15},{10,... | collective-permute-start | bytes 184328 | tf_op jit(solution)/shard_map/ppermute | solution.py:278
  23.3 3.6 %collective-permute-start.7 = (bf16[24,1280]{1,0:T(8,128)(2,1)S(1)}, bf16[24,1280]{1,0:T(8,128)(2,1)S(1)}, u32[]{:S(2)}, u32[]{:S(2)}) collective-permute-start(bf16[24,1280]{1,0:T(8,128)(2,1)S(1)} %get-tuple-element.24), channel_id=1, source_target_pairs={{0,7},{1,6},{2,1},{3,0},{4,3},{5,2},{6,5},{7,4},{8,15},{9,14},{10,... | collective-permute-start | bytes 184328 | tf_op jit(solution)/shard_map/ppermute | solution.py:278
  23.3 3.6 %collective-permute-start.2 = (bf16[24,1280]{1,0:T(8,128)(2,1)S(1)}, bf16[24,1280]{1,0:T(8,128)(2,1)S(1)}, u32[]{:S(2)}, u32[]{:S(2)}) collective-permute-start(bf16[24,1280]{1,0:T(8,128)(2,1)S(1)} %shard_map.94), channel_id=1, source_target_pairs={{0,1},{1,0},{2,3},{3,2},{4,5},{5,4},{6,7},{7,6},{8,9},{9,8},{10,11... | collective-permute-start | bytes 184328 | tf_op jit(solution)/shard_map/ppermute | solution.py:278

commit v11 on v10

--- a/solution.py
+++ b/solution.py
@@ -197,8 +197,7 @@
     tokens = out.shape[0]
     chunks = [ref[...].astype(jnp.float32) for ref in in_refs]
     if len(chunks) > 1:
-        own, double, passed, partner, *singles = chunks
-        chunks = [own, double[: own.shape[0]], passed, *singles, partner]
+        chunks[1] = chunks[1][: chunks[0].shape[0]]
     arrived = chunks[0] if len(chunks) == 1 else jnp.concatenate(chunks, axis=0)
     arrived = arrived.astype(jnp.bfloat16)
     width = arrived.shape[1]
@@ -284,7 +283,7 @@
         onward = pl.pallas_call(
             forward_kernel, out_shape=rows_of(chunk), in_specs=[vmem], out_specs=vmem, compiler_params=small
         )(double)
-        arrived = [outgoing[0], double, exchange(onward, 0, 1), rest[-1], *rest[:-1]]
+        arrived = [outgoing[0], double, exchange(onward, 0, 1), *rest]
     else:
         arrived = [
             lax.all_to_all(

time: 28.3 us -> 26.4 us (0.933)
  waiting for transfers between devices: 5.66 us -> 4.41 us
  starting transfers between devices: 12.3 us -> 11.7 us
    ppermute x7, waiting for transfers between devices: 5.49 us -> 4.24 us  [exchange(): lax.ppermute(part, 'seq', [(i, (i // CORES + dz) % n_z * CORES + (i + dc)...]
    ppermute x7, starting transfers between devices: 9.33 us -> 8.7 us  [exchange(): lax.ppermute(part, 'seq', [(i, (i // CORES + dz) % n_z * CORES + (i + dc)...]
  transfers between devices with their start and end apart: 8 -> 8, of which waited for: 3 -> 6; matrix products, arithmetic and copies ran while one was open for 0% -> 0% of each run, Pallas kernels for 15% -> 16%
where the time goes in v11:
time: 26.4 us; the launch traced here: 26.2 us
  starting transfers between devices  11.7 us (44%)
  Pallas kernels  8.74 us (33%)
  waiting for transfers between devices  4.41 us (17%)
  between operations  1.39 us (5%)
    ppermute x7, starting transfers between devices, exchange(): lax.ppermute(part, 'seq', [(i, (i // CORES + dz) % n_z * CORES + (i + dc)...  8.7 us
    pallas_call x2, Pallas kernels, encode_call(): pl.pallas_call(kernel, out_shape=out_shape, in_specs=[smem] * len(scalars...  7.32 us
    ppermute x7, waiting for transfers between devices, exchange(): lax.ppermute(part, 'seq', [(i, (i // CORES + dz) % n_z * CORES + (i + dc)...  4.24 us
    ppermute x1, starting transfers between devices, per_device(): lax.ppermute(lent, 'enc', [((i - 1) % n_enc, i) for i in range(n_enc)])  2.99 us
    pallas_call x1, Pallas kernels, per_device(): pl.pallas_call(place_kernel, out_shape=rows_of(row_total, GROUP * width),...  1.16 us
  transfers between devices with their start and end apart: 8, of which 6 were waited for; matrix products, arithmetic and copies ran while one was open for 0% of the time, Pallas kernels for 16%

profile of v11, /device:TPU:0, one launch (start us, length us, event | category | flops | bytes accessed | tf_op | source)
XLA Modules:
  0.0 26.2 jit_solution(13747980603938195782)
XLA Ops:
  0.0 0.0 copy-start.1
  0.0 0.0 copy-start
  0.7 3.0 %shard_map.92 = bf16[64,1280]{1,0:T(8,128)(2,1)S(1)} custom-call(s32[1,1]{1,0:T(1,128)S(6)} %copy.10.count_ref, bf16[4,64,3840]{2,1,0:T(8,128)(2,1)} %qkv_hbm.3, bf16[4,64,1280]{2,1,0:T(8,128)(2,1)} %resid_hbm.3, bf16[1280,1280]{1,0:T(8,128)(2,1)} %weight_hbm.3, bf16[1280]{0:T(1024)(128)(2,1)} %bias_hbm.3, bf16[1280]{0:T(1024)(128)(2,1)} %gain_hbm.3), custom_call_target="tpu_custom_call" | custom-call | flops 251658240 | bytes 4096000 | tf_op jit(solution)/shard_map/pallas_call | solution.py:156
  3.7 3.0 %collective-permute-start = (bf16[64,1280]{1,0:T(8,128)(2,1)S(1)}, bf16[64,1280]{1,0:T(8,128)(2,1)S(1)}, u32[]{:S(2)}, u32[]{:S(2)}) collective-permute-start(bf16[64,1280]{1,0:T(8,128)(2,1)S(1)} %shard_map.92), channel_id=1, source_target_pairs={{24,0},{0,8},{8,16},{16,24},{25,1},{1,9},{9,17},{17,25},{26,2},{2,... | collective-permute-start | bytes 491528 | tf_op jit(solution)/shard_map/ppermute | solution.py:253
  7.3 0.0 copy-done.1
  7.4 0.0 copy-done
  7.4 4.3 %shard_map.91 = (bf16[192,1280]{1,0:T(8,128)(2,1)S(1)}, bf16[192,64]{1,0:T(8,128)(2,1)S(1)}, bf16[192,192]{1,0:T(8,128)(2,1)S(1)}) custom-call(s32[1,1]{1,0:T(1,128)S(6)} %copy.10.count_ref, s32[1,1]{1,0:T(1,128)S(6)} %copy.11.send_ref, s32[1,1]{1,0:T(1,128)} %bitcast.me_ref, s32[1,48]{1,0:T(1,128)S(1)} %copy-done, s32[1,48]{1,0:T(1,128)S(1)} %copy-done.1, ...), custom_call_target="tpu_custom_call" | custom-call | flops 754974720 | bytes 5734400 | tf_op jit(solution)/shard_map/pallas_call | solution.py:156
  11.7 0.2 collective-permute-done.borrowed_ref
  11.9 0.3 shard_map.93
  12.1 2.8 %collective-permute-start.1 = (bf16[48,1280]{1,0:T(8,128)(2,1)S(1)}, bf16[48,1280]{1,0:T(8,128)(2,1)S(1)}, u32[]{:S(2)}, u32[]{:S(2)}) collective-permute-start(bf16[48,1280]{1,0:T(8,128)(2,1)S(1)} %get-tuple-element.19), channel_id=1, source_target_pairs={{0,4},{1,5},{2,6},{3,7},{4,0},{5,1},{6,2},{7,3},{8,12},{9,13},{10,... | collective-permute-start | bytes 368648 | tf_op jit(solution)/shard_map/ppermute | solution.py:277
  15.0 1.6 %collective-permute-start.3 = (bf16[24,1280]{1,0:T(8,128)(2,1)S(1)}, bf16[24,1280]{1,0:T(8,128)(2,1)S(1)}, u32[]{:S(2)}, u32[]{:S(2)}) collective-permute-start(bf16[24,1280]{1,0:T(8,128)(2,1)S(1)} %get-tuple-element.20), channel_id=1, source_target_pairs={{0,2},{1,3},{2,4},{3,5},{4,6},{5,7},{6,0},{7,1},{8,10},{9,11},{10,... | collective-permute-start | bytes 184328 | tf_op jit(solution)/shard_map/ppermute | solution.py:277
  16.5 0.0 collective-permute-start.4
  16.5 2.2 %collective-permute-start.5 = (bf16[24,1280]{1,0:T(8,128)(2,1)S(1)}, bf16[24,1280]{1,0:T(8,128)(2,1)S(1)}, u32[]{:S(2)}, u32[]{:S(2)}) collective-permute-start(bf16[24,1280]{1,0:T(8,128)(2,1)S(1)} %get-tuple-element.22), channel_id=1, source_target_pairs={{0,6},{1,7},{2,0},{3,1},{4,2},{5,3},{6,4},{7,5},{8,14},{9,15},{10,... | collective-permute-start | bytes 184328 | tf_op jit(solution)/shard_map/ppermute | solution.py:277
  18.8 1.5 %collective-permute-start.6 = (bf16[24,1280]{1,0:T(8,128)(2,1)S(1)}, bf16[24,1280]{1,0:T(8,128)(2,1)S(1)}, u32[]{:S(2)}, u32[]{:S(2)}) collective-permute-start(bf16[24,1280]{1,0:T(8,128)(2,1)S(1)} %get-tuple-element.23), channel_id=1, source_target_pairs={{0,7},{1,6},{2,1},{3,0},{4,3},{5,2},{6,5},{7,4},{8,15},{9,14},{10,... | collective-permute-start | bytes 184328 | tf_op jit(solution)/shard_map/ppermute | solution.py:277
  20.3 3.3 %collective-permute-done.1.double_ref.refs_1_ = bf16[48,1280]{1,0:T(8,128)(2,1)S(1)} collective-permute-done((bf16[48,1280]{1,0:T(8,128)(2,1)S(1)}, bf16[48,1280]{1,0:T(8,128)(2,1)S(1)}, u32[]{:S(2)}, u32[]{:S(2)}) %collective-permute-start.1) | collective-permute-done | bytes 122912 | tf_op jit(solution)/shard_map/ppermute | solution.py:277
  23.6 0.0 collective-permute-start.7
  23.6 0.0 collective-permute-done.3.refs_3_
  23.6 0.6 %collective-permute-start.2 = (bf16[24,1280]{1,0:T(8,128)(2,1)S(1)}, bf16[24,1280]{1,0:T(8,128)(2,1)S(1)}, u32[]{:S(2)}, u32[]{:S(2)}) collective-permute-start(bf16[24,1280]{1,0:T(8,128)(2,1)S(1)} %shard_map.94), channel_id=1, source_target_pairs={{0,1},{1,0},{2,3},{3,2},{4,5},{5,4},{6,7},{7,6},{8,9},{9,8},{10,11... | collective-permute-start | bytes 184328 | tf_op jit(solution)/shard_map/ppermute | solution.py:277
  24.2 0.0 collective-permute-done.4.refs_4_
  24.2 0.2 collective-permute-done.5.refs_5_
  24.4 0.3 %collective-permute-done.6.refs_6_ = bf16[24,1280]{1,0:T(8,128)(2,1)S(1)} collective-permute-done((bf16[24,1280]{1,0:T(8,128)(2,1)S(1)}, bf16[24,1280]{1,0:T(8,128)(2,1)S(1)}, u32[]{:S(2)}, u32[]{:S(2)}) %collective-permute-start.6) | collective-permute-done | bytes 61472 | tf_op jit(solution)/shard_map/ppermute | solution.py:277
  24.7 0.2 collective-permute-done.7.refs_7_
  24.8 0.2 collective-permute-done.2.refs_2_
  25.1 1.2 %shard_map.95 = bf16[48,5120]{1,0:T(8,128)(2,1)} custom-call(bf16[192,192]{1,0:T(8,128)(2,1)S(1)} %get-tuple-element.15.place_ref, bf16[24,1280]{1,0:T(8,128)(2,1)S(1)} %get-tuple-element.18.refs_0_, bf16[48,1280]{1,0:T(8,128)(2,1)S(1)} %collective-permute-done.1.double_ref.refs_1_, bf16[24,1280]{1,0:T(8,128)(2,1)S(1)} %collective-permute-done.2.refs_2_, ...), custom_call_target="tpu_custom_call" | custom-call | tf_op jit(solution)/shard_map/pallas_call | solution.py:293
  (1 shorter events, 0.0 us)
Async XLA Ops:
  0.0 7.3 %copy-start.1 = (s32[1,48]{1,0:T(1,128)S(1)}, s32[1,48]{1,0:T(1,128)}, u32[]{:S(2)}) copy-start(s32[1,48]{1,0:T(1,128)} %row_ref.1) | copy-start | bytes 580
  0.0 7.4 %copy-start = (s32[1,48]{1,0:T(1,128)S(1)}, s32[1,48]{1,0:T(1,128)}, u32[]{:S(2)}) copy-start(s32[1,48]{1,0:T(1,128)} %slot_ref.1) | copy-start | bytes 580
  3.7 8.1 %collective-permute-start = (bf16[64,1280]{1,0:T(8,128)(2,1)S(1)}, bf16[64,1280]{1,0:T(8,128)(2,1)S(1)}, u32[]{:S(2)}, u32[]{:S(2)}) collective-permute-start(bf16[64,1280]{1,0:T(8,128)(2,1)S(1)} %shard_map.92), channel_id=1, source_target_pairs={{24,0},{0,8},{8,16},{16,24},{25,1},{1,9},{9,17},{17,25},{26,2},{2,... | collective-permute-start | bytes 491528 | tf_op jit(solution)/shard_map/ppermute | solution.py:253
  12.1 11.5 %collective-permute-start.1 = (bf16[48,1280]{1,0:T(8,128)(2,1)S(1)}, bf16[48,1280]{1,0:T(8,128)(2,1)S(1)}, u32[]{:S(2)}, u32[]{:S(2)}) collective-permute-start(bf16[48,1280]{1,0:T(8,128)(2,1)S(1)} %get-tuple-element.19), channel_id=1, source_target_pairs={{0,4},{1,5},{2,6},{3,7},{4,0},{5,1},{6,2},{7,3},{8,12},{9,13},{10,... | collective-permute-start | bytes 368648 | tf_op jit(solution)/shard_map/ppermute | solution.py:277
  15.0 8.6 %collective-permute-start.3 = (bf16[24,1280]{1,0:T(8,128)(2,1)S(1)}, bf16[24,1280]{1,0:T(8,128)(2,1)S(1)}, u32[]{:S(2)}, u32[]{:S(2)}) collective-permute-start(bf16[24,1280]{1,0:T(8,128)(2,1)S(1)} %get-tuple-element.20), channel_id=1, source_target_pairs={{0,2},{1,3},{2,4},{3,5},{4,6},{5,7},{6,0},{7,1},{8,10},{9,11},{10,... | collective-permute-start | bytes 184328 | tf_op jit(solution)/shard_map/ppermute | solution.py:277
  16.5 7.6 %collective-permute-start.4 = (bf16[24,1280]{1,0:T(8,128)(2,1)S(1)}, bf16[24,1280]{1,0:T(8,128)(2,1)S(1)}, u32[]{:S(2)}, u32[]{:S(2)}) collective-permute-start(bf16[24,1280]{1,0:T(8,128)(2,1)S(1)} %get-tuple-element.21), channel_id=1, source_target_pairs={{0,3},{1,2},{2,5},{3,4},{4,7},{5,6},{6,1},{7,0},{8,11},{9,10},{10,... | collective-permute-start | bytes 184328 | tf_op jit(solution)/shard_map/ppermute | solution.py:277
  16.5 7.8 %collective-permute-start.5 = (bf16[24,1280]{1,0:T(8,128)(2,1)S(1)}, bf16[24,1280]{1,0:T(8,128)(2,1)S(1)}, u32[]{:S(2)}, u32[]{:S(2)}) collective-permute-start(bf16[24,1280]{1,0:T(8,128)(2,1)S(1)} %get-tuple-element.22), channel_id=1, source_target_pairs={{0,6},{1,7},{2,0},{3,1},{4,2},{5,3},{6,4},{7,5},{8,14},{9,15},{10,... | collective-permute-start | bytes 184328 | tf_op jit(solution)/shard_map/ppermute | solution.py:277
  18.8 5.9 %collective-permute-start.6 = (bf16[24,1280]{1,0:T(8,128)(2,1)S(1)}, bf16[24,1280]{1,0:T(8,128)(2,1)S(1)}, u32[]{:S(2)}, u32[]{:S(2)}) collective-permute-start(bf16[24,1280]{1,0:T(8,128)(2,1)S(1)} %get-tuple-element.23), channel_id=1, source_target_pairs={{0,7},{1,6},{2,1},{3,0},{4,3},{5,2},{6,5},{7,4},{8,15},{9,14},{10,... | collective-permute-start | bytes 184328 | tf_op jit(solution)/shard_map/ppermute | solution.py:277
  23.6 1.2 %collective-permute-start.7 = (bf16[24,1280]{1,0:T(8,128)(2,1)S(1)}, bf16[24,1280]{1,0:T(8,128)(2,1)S(1)}, u32[]{:S(2)}, u32[]{:S(2)}) collective-permute-start(bf16[24,1280]{1,0:T(8,128)(2,1)S(1)} %get-tuple-element.24), channel_id=1, source_target_pairs={{0,1},{1,0},{2,3},{3,2},{4,5},{5,4},{6,7},{7,6},{8,9},{9,8},{10,11... | collective-permute-start | bytes 184328 | tf_op jit(solution)/shard_map/ppermute | solution.py:277
  23.6 1.5 %collective-permute-start.2 = (bf16[24,1280]{1,0:T(8,128)(2,1)S(1)}, bf16[24,1280]{1,0:T(8,128)(2,1)S(1)}, u32[]{:S(2)}, u32[]{:S(2)}) collective-permute-start(bf16[24,1280]{1,0:T(8,128)(2,1)S(1)} %shard_map.94), channel_id=1, source_target_pairs={{0,1},{1,0},{2,3},{3,2},{4,5},{5,4},{6,7},{7,6},{8,9},{9,8},{10,11... | collective-permute-start | bytes 184328 | tf_op jit(solution)/shard_map/ppermute | solution.py:277

commit v12 on v9

--- a/solution.py
+++ b/solution.py
@@ -212,8 +212,7 @@
 
 
 def exchange_steps(n_seq):
-    steps = [(dz, dc) for dz in range(1, n_seq // CORES) for dc in range(CORES)]
-    return [(0, 0)] + steps[:CORES] + [(0, 1)] + steps[CORES:]
+    return [(0, 0)] + [(dz, dc) for dz in range(1, n_seq // CORES) for dc in range(CORES)] + [(0, 1)]
 
 
 def chip_peer(n_seq, me, step, sign):

time: 26.7 us -> 25.6 us (0.959)
  starting transfers between devices: 12.6 us -> 11.2 us
    ppermute x7, starting transfers between devices: 9.58 us -> 8.24 us  [exchange(): lax.ppermute(part, 'seq', [(i, (i // CORES + dz) % n_z * CORES + (i + dc)...]
  transfers between devices with their start and end apart: 8 -> 8, of which waited for: 5 -> 4; matrix products, arithmetic and copies ran while one was open for 0% -> 0% of each run, Pallas kernels for 16% -> 17%
where the time goes in v12:
time: 25.6 us; the launch traced here: 25.3 us
  starting transfers between devices  11.2 us (44%)
  Pallas kernels  8.74 us (34%)
  waiting for transfers between devices  3.92 us (15%)
  between operations  1.38 us (5%)
    ppermute x7, starting transfers between devices, exchange(): lax.ppermute(part, 'seq', [(i, (i // CORES + dz) % n_z * CORES + (i + dc)...  8.24 us
    pallas_call x2, Pallas kernels, encode_call(): pl.pallas_call(kernel, out_shape=out_shape, in_specs=[smem] * len(scalars...  7.32 us
    ppermute x7, waiting for transfers between devices, exchange(): lax.ppermute(part, 'seq', [(i, (i // CORES + dz) % n_z * CORES + (i + dc)...  3.75 us
    ppermute x1, starting transfers between devices, per_device(): lax.ppermute(lent, 'enc', [((i - 1) % n_enc, i) for i in range(n_enc)])  2.99 us
    pallas_call x1, Pallas kernels, per_device(): pl.pallas_call(place_kernel, out_shape=rows_of(row_total, GROUP * width),...  1.16 us
  transfers between devices with their start and end apart: 8, of which 4 were waited for; matrix products, arithmetic and copies ran while one was open for 0% of the time, Pallas kernels for 17%

profile of v12, /device:TPU:0, one launch (start us, length us, event | category | flops | bytes accessed | tf_op | source)
XLA Modules:
  0.0 25.3 jit_solution(15735372864136359507)
XLA Ops:
  0.0 0.0 copy-start.1
  0.0 0.0 copy-start
  0.7 3.0 %shard_map.92 = bf16[64,1280]{1,0:T(8,128)(2,1)S(1)} custom-call(s32[1,1]{1,0:T(1,128)S(6)} %copy.10.count_ref, bf16[4,64,3840]{2,1,0:T(8,128)(2,1)} %qkv_hbm.3, bf16[4,64,1280]{2,1,0:T(8,128)(2,1)} %resid_hbm.3, bf16[1280,1280]{1,0:T(8,128)(2,1)} %weight_hbm.3, bf16[1280]{0:T(1024)(128)(2,1)} %bias_hbm.3, bf16[1280]{0:T(1024)(128)(2,1)} %gain_hbm.3), custom_call_target="tpu_custom_call" | custom-call | flops 251658240 | bytes 4096000 | tf_op jit(solution)/shard_map/pallas_call | solution.py:156
  3.7 3.0 %collective-permute-start = (bf16[64,1280]{1,0:T(8,128)(2,1)S(1)}, bf16[64,1280]{1,0:T(8,128)(2,1)S(1)}, u32[]{:S(2)}, u32[]{:S(2)}) collective-permute-start(bf16[64,1280]{1,0:T(8,128)(2,1)S(1)} %shard_map.92), channel_id=1, source_target_pairs={{24,0},{0,8},{8,16},{16,24},{25,1},{1,9},{9,17},{17,25},{26,2},{2,... | collective-permute-start | bytes 491528 | tf_op jit(solution)/shard_map/ppermute | solution.py:251
  7.3 0.0 copy-done.1
  7.4 0.0 copy-done
  7.4 4.3 %shard_map.91 = (bf16[192,1280]{1,0:T(8,128)(2,1)S(1)}, bf16[192,64]{1,0:T(8,128)(2,1)S(1)}, bf16[192,192]{1,0:T(8,128)(2,1)S(1)}) custom-call(s32[1,1]{1,0:T(1,128)S(6)} %copy.10.count_ref, s32[1,1]{1,0:T(1,128)S(6)} %copy.11.send_ref, s32[1,1]{1,0:T(1,128)} %bitcast.me_ref, s32[1,48]{1,0:T(1,128)S(1)} %copy-done, s32[1,48]{1,0:T(1,128)S(1)} %copy-done.1, ...), custom_call_target="tpu_custom_call" | custom-call | flops 754974720 | bytes 5734400 | tf_op jit(solution)/shard_map/pallas_call | solution.py:156
  11.7 0.2 collective-permute-done.borrowed_ref
  11.9 0.3 %shard_map.93 = (bf16[24,1280]{1,0:T(8,128)(2,1)S(1)}, bf16[48,1280]{1,0:T(8,128)(2,1)S(1)}, bf16[24,1280]{1,0:T(8,128)(2,1)S(1)}, bf16[24,1280]{1,0:T(8,128)(2,...) custom-call(bf16[192,1280]{1,0:T(8,128)(2,1)S(1)} %get-tuple-element.16.packed_ref,, ...), custom_call_target="tpu_custom_call" | custom-call | tf_op jit(solution)/shard_map/pallas_call | solution.py:263
  12.1 1.8 %collective-permute-start.1 = (bf16[48,1280]{1,0:T(8,128)(2,1)S(1)}, bf16[48,1280]{1,0:T(8,128)(2,1)S(1)}, u32[]{:S(2)}, u32[]{:S(2)}) collective-permute-start(bf16[48,1280]{1,0:T(8,128)(2,1)S(1)} %get-tuple-element.19), channel_id=1, source_target_pairs={{0,2},{1,3},{2,4},{3,5},{4,6},{5,7},{6,0},{7,1},{8,10},{9,11},{10,... | collective-permute-start | bytes 368648 | tf_op jit(solution)/shard_map/ppermute | solution.py:275
  13.9 2.6 %collective-permute-start.3 = (bf16[24,1280]{1,0:T(8,128)(2,1)S(1)}, bf16[24,1280]{1,0:T(8,128)(2,1)S(1)}, u32[]{:S(2)}, u32[]{:S(2)}) collective-permute-start(bf16[24,1280]{1,0:T(8,128)(2,1)S(1)} %get-tuple-element.20), channel_id=1, source_target_pairs={{0,4},{1,5},{2,6},{3,7},{4,0},{5,1},{6,2},{7,3},{8,12},{9,13},{10,... | collective-permute-start | bytes 184328 | tf_op jit(solution)/shard_map/ppermute | solution.py:275
  16.5 0.0 collective-permute-start.4
  16.5 1.3 %collective-permute-start.5 = (bf16[24,1280]{1,0:T(8,128)(2,1)S(1)}, bf16[24,1280]{1,0:T(8,128)(2,1)S(1)}, u32[]{:S(2)}, u32[]{:S(2)}) collective-permute-start(bf16[24,1280]{1,0:T(8,128)(2,1)S(1)} %get-tuple-element.22), channel_id=1, source_target_pairs={{0,6},{1,7},{2,0},{3,1},{4,2},{5,3},{6,4},{7,5},{8,14},{9,15},{10,... | collective-permute-start | bytes 184328 | tf_op jit(solution)/shard_map/ppermute | solution.py:275
  17.9 2.5 %collective-permute-start.6 = (bf16[24,1280]{1,0:T(8,128)(2,1)S(1)}, bf16[24,1280]{1,0:T(8,128)(2,1)S(1)}, u32[]{:S(2)}, u32[]{:S(2)}) collective-permute-start(bf16[24,1280]{1,0:T(8,128)(2,1)S(1)} %get-tuple-element.23), channel_id=1, source_target_pairs={{0,7},{1,6},{2,1},{3,0},{4,3},{5,2},{6,5},{7,4},{8,15},{9,14},{10,... | collective-permute-start | bytes 184328 | tf_op jit(solution)/shard_map/ppermute | solution.py:275
  20.4 0.0 collective-permute-done.1.double_ref.refs_1_
  20.4 0.0 collective-permute-start.7
  20.4 2.4 %collective-permute-done.3.refs_3_ = bf16[24,1280]{1,0:T(8,128)(2,1)S(1)} collective-permute-done((bf16[24,1280]{1,0:T(8,128)(2,1)S(1)}, bf16[24,1280]{1,0:T(8,128)(2,1)S(1)}, u32[]{:S(2)}, u32[]{:S(2)}) %collective-permute-start.3) | collective-permute-done | bytes 61472 | tf_op jit(solution)/shard_map/ppermute | solution.py:275
  22.8 0.0 collective-permute-start.2
  22.8 1.1 %collective-permute-done.4.refs_4_ = bf16[24,1280]{1,0:T(8,128)(2,1)S(1)} collective-permute-done((bf16[24,1280]{1,0:T(8,128)(2,1)S(1)}, bf16[24,1280]{1,0:T(8,128)(2,1)S(1)}, u32[]{:S(2)}, u32[]{:S(2)}) %collective-permute-start.4) | collective-permute-done | bytes 61472 | tf_op jit(solution)/shard_map/ppermute | solution.py:275
  23.9 0.0 collective-permute-done.5.refs_5_
  23.9 0.2 collective-permute-done.6.refs_6_
  24.1 0.0 collective-permute-done.7.refs_7_
  24.1 0.0 collective-permute-done.2.refs_2_
  24.1 1.2 %shard_map.95 = bf16[48,5120]{1,0:T(8,128)(2,1)} custom-call(bf16[192,192]{1,0:T(8,128)(2,1)S(1)} %get-tuple-element.15.place_ref, bf16[24,1280]{1,0:T(8,128)(2,1)S(1)} %get-tuple-element.18.refs_0_, bf16[48,1280]{1,0:T(8,128)(2,1)S(1)} %collective-permute-done.1.double_ref.refs_1_, bf16[24,1280]{1,0:T(8,128)(2,1)S(1)} %collective-permute-done.2.refs_2_, ...), custom_call_target="tpu_custom_call" | custom-call | tf_op jit(solution)/shard_map/pallas_call | solution.py:291
  (1 shorter events, 0.0 us)
Async XLA Ops:
  0.0 7.3 %copy-start.1 = (s32[1,48]{1,0:T(1,128)S(1)}, s32[1,48]{1,0:T(1,128)}, u32[]{:S(2)}) copy-start(s32[1,48]{1,0:T(1,128)} %row_ref.1) | copy-start | bytes 580
  0.0 7.4 %copy-start = (s32[1,48]{1,0:T(1,128)S(1)}, s32[1,48]{1,0:T(1,128)}, u32[]{:S(2)}) copy-start(s32[1,48]{1,0:T(1,128)} %slot_ref.1) | copy-start | bytes 580
  3.7 8.1 %collective-permute-start = (bf16[64,1280]{1,0:T(8,128)(2,1)S(1)}, bf16[64,1280]{1,0:T(8,128)(2,1)S(1)}, u32[]{:S(2)}, u32[]{:S(2)}) collective-permute-start(bf16[64,1280]{1,0:T(8,128)(2,1)S(1)} %shard_map.92), channel_id=1, source_target_pairs={{24,0},{0,8},{8,16},{16,24},{25,1},{1,9},{9,17},{17,25},{26,2},{2,... | collective-permute-start | bytes 491528 | tf_op jit(solution)/shard_map/ppermute | solution.py:251
  12.1 8.2 %collective-permute-start.1 = (bf16[48,1280]{1,0:T(8,128)(2,1)S(1)}, bf16[48,1280]{1,0:T(8,128)(2,1)S(1)}, u32[]{:S(2)}, u32[]{:S(2)}) collective-permute-start(bf16[48,1280]{1,0:T(8,128)(2,1)S(1)} %get-tuple-element.19), channel_id=1, source_target_pairs={{0,2},{1,3},{2,4},{3,5},{4,6},{5,7},{6,0},{7,1},{8,10},{9,11},{10,... | collective-permute-start | bytes 368648 | tf_op jit(solution)/shard_map/ppermute | solution.py:275
  13.9 8.9 %collective-permute-start.3 = (bf16[24,1280]{1,0:T(8,128)(2,1)S(1)}, bf16[24,1280]{1,0:T(8,128)(2,1)S(1)}, u32[]{:S(2)}, u32[]{:S(2)}) collective-permute-start(bf16[24,1280]{1,0:T(8,128)(2,1)S(1)} %get-tuple-element.20), channel_id=1, source_target_pairs={{0,4},{1,5},{2,6},{3,7},{4,0},{5,1},{6,2},{7,3},{8,12},{9,13},{10,... | collective-permute-start | bytes 184328 | tf_op jit(solution)/shard_map/ppermute | solution.py:275
  16.5 7.4 %collective-permute-start.4 = (bf16[24,1280]{1,0:T(8,128)(2,1)S(1)}, bf16[24,1280]{1,0:T(8,128)(2,1)S(1)}, u32[]{:S(2)}, u32[]{:S(2)}) collective-permute-start(bf16[24,1280]{1,0:T(8,128)(2,1)S(1)} %get-tuple-element.21), channel_id=1, source_target_pairs={{0,5},{1,4},{2,7},{3,6},{4,1},{5,0},{6,3},{7,2},{8,13},{9,12},{10,... | collective-permute-start | bytes 184328 | tf_op jit(solution)/shard_map/ppermute | solution.py:275
  16.5 7.4 %collective-permute-start.5 = (bf16[24,1280]{1,0:T(8,128)(2,1)S(1)}, bf16[24,1280]{1,0:T(8,128)(2,1)S(1)}, u32[]{:S(2)}, u32[]{:S(2)}) collective-permute-start(bf16[24,1280]{1,0:T(8,128)(2,1)S(1)} %get-tuple-element.22), channel_id=1, source_target_pairs={{0,6},{1,7},{2,0},{3,1},{4,2},{5,3},{6,4},{7,5},{8,14},{9,15},{10,... | collective-permute-start | bytes 184328 | tf_op jit(solution)/shard_map/ppermute | solution.py:275
  17.9 6.2 %collective-permute-start.6 = (bf16[24,1280]{1,0:T(8,128)(2,1)S(1)}, bf16[24,1280]{1,0:T(8,128)(2,1)S(1)}, u32[]{:S(2)}, u32[]{:S(2)}) collective-permute-start(bf16[24,1280]{1,0:T(8,128)(2,1)S(1)} %get-tuple-element.23), channel_id=1, source_target_pairs={{0,7},{1,6},{2,1},{3,0},{4,3},{5,2},{6,5},{7,4},{8,15},{9,14},{10,... | collective-permute-start | bytes 184328 | tf_op jit(solution)/shard_map/ppermute | solution.py:275
  20.4 3.8 %collective-permute-start.7 = (bf16[24,1280]{1,0:T(8,128)(2,1)S(1)}, bf16[24,1280]{1,0:T(8,128)(2,1)S(1)}, u32[]{:S(2)}, u32[]{:S(2)}) collective-permute-start(bf16[24,1280]{1,0:T(8,128)(2,1)S(1)} %get-tuple-element.24), channel_id=1, source_target_pairs={{0,1},{1,0},{2,3},{3,2},{4,5},{5,4},{6,7},{7,6},{8,9},{9,8},{10,11... | collective-permute-start | bytes 184328 | tf_op jit(solution)/shard_map/ppermute | solution.py:275
  22.8 1.3 %collective-permute-start.2 = (bf16[24,1280]{1,0:T(8,128)(2,1)S(1)}, bf16[24,1280]{1,0:T(8,128)(2,1)S(1)}, u32[]{:S(2)}, u32[]{:S(2)}) collective-permute-start(bf16[24,1280]{1,0:T(8,128)(2,1)S(1)} %shard_map.94), channel_id=1, source_target_pairs={{0,1},{1,0},{2,3},{3,2},{4,5},{5,4},{6,7},{7,6},{8,9},{9,8},{10,11... | collective-permute-start | bytes 184328 | tf_op jit(solution)/shard_map/ppermute | solution.py:275

commit v13 on v12

--- a/solution.py
+++ b/solution.py
@@ -212,7 +212,8 @@
 
 
 def exchange_steps(n_seq):
-    return [(0, 0)] + [(dz, dc) for dz in range(1, n_seq // CORES) for dc in range(CORES)] + [(0, 1)]
+    n_z = n_seq // CORES
+    return [(0, 0), (1, 0), (1, 1)] + [(dz, dc) for dc in range(CORES) for dz in range(2, n_z)] + [(0, 1)]
 
 
 def chip_peer(n_seq, me, step, sign):

time: 25.6 us -> 26.5 us (1.035)
  waiting for transfers between devices: 3.92 us -> 4.7 us
  starting transfers between devices: 11.2 us -> 11.5 us
    ppermute x7, waiting for transfers between devices: 3.75 us -> 4.53 us  [exchange(): lax.ppermute(part, 'seq', [(i, (i // CORES + dz) % n_z * CORES + (i + dc)...]
    ppermute x7, starting transfers between devices: 8.24 us -> 8.52 us  [exchange(): lax.ppermute(part, 'seq', [(i, (i // CORES + dz) % n_z * CORES + (i + dc)...]
  transfers between devices with their start and end apart: 8 -> 8, of which waited for: 4 -> 4; matrix products, arithmetic and copies ran while one was open for 0% -> 0% of each run, Pallas kernels for 17% -> 16%
where the time goes in v13:
time: 26.5 us; the launch traced here: 26.4 us
  starting transfers between devices  11.5 us (43%)
  Pallas kernels  8.74 us (33%)
  waiting for transfers between devices  4.7 us (18%)
  between operations  1.39 us (5%)
    ppermute x7, starting transfers between devices, exchange(): lax.ppermute(part, 'seq', [(i, (i // CORES + dz) % n_z * CORES + (i + dc)...  8.52 us
    pallas_call x2, Pallas kernels, encode_call(): pl.pallas_call(kernel, out_shape=out_shape, in_specs=[smem] * len(scalars...  7.32 us
    ppermute x7, waiting for transfers between devices, exchange(): lax.ppermute(part, 'seq', [(i, (i // CORES + dz) % n_z * CORES + (i + dc)...  4.53 us
    ppermute x1, starting transfers between devices, per_device(): lax.ppermute(lent, 'enc', [((i - 1) % n_enc, i) for i in range(n_enc)])  2.99 us
    pallas_call x1, Pallas kernels, per_device(): pl.pallas_call(place_kernel, out_shape=rows_of(row_total, GROUP * width),...  1.16 us
  transfers between devices with their start and end apart: 8, of which 4 were waited for; matrix products, arithmetic and copies ran while one was open for 0% of the time, Pallas kernels for 16%

profile of v13, /device:TPU:0, one launch (start us, length us, event | category | flops | bytes accessed | tf_op | source)
XLA Modules:
  0.0 26.4 jit_solution(590516453759076604)
XLA Ops:
  0.0 0.0 copy-start.1
  0.0 0.0 copy-start
  0.7 3.0 %shard_map.92 = bf16[64,1280]{1,0:T(8,128)(2,1)S(1)} custom-call(s32[1,1]{1,0:T(1,128)S(6)} %copy.10.count_ref, bf16[4,64,3840]{2,1,0:T(8,128)(2,1)} %qkv_hbm.3, bf16[4,64,1280]{2,1,0:T(8,128)(2,1)} %resid_hbm.3, bf16[1280,1280]{1,0:T(8,128)(2,1)} %weight_hbm.3, bf16[1280]{0:T(1024)(128)(2,1)} %bias_hbm.3, bf16[1280]{0:T(1024)(128)(2,1)} %gain_hbm.3), custom_call_target="tpu_custom_call" | custom-call | flops 251658240 | bytes 4096000 | tf_op jit(solution)/shard_map/pallas_call | solution.py:156
  3.7 3.0 %collective-permute-start = (bf16[64,1280]{1,0:T(8,128)(2,1)S(1)}, bf16[64,1280]{1,0:T(8,128)(2,1)S(1)}, u32[]{:S(2)}, u32[]{:S(2)}) collective-permute-start(bf16[64,1280]{1,0:T(8,128)(2,1)S(1)} %shard_map.92), channel_id=1, source_target_pairs={{24,0},{0,8},{8,16},{16,24},{25,1},{1,9},{9,17},{17,25},{26,2},{2,... | collective-permute-start | bytes 491528 | tf_op jit(solution)/shard_map/ppermute | solution.py:252
  7.3 0.0 copy-done.1
  7.4 0.0 copy-done
  7.4 4.3 %shard_map.91 = (bf16[192,1280]{1,0:T(8,128)(2,1)S(1)}, bf16[192,64]{1,0:T(8,128)(2,1)S(1)}, bf16[192,192]{1,0:T(8,128)(2,1)S(1)}) custom-call(s32[1,1]{1,0:T(1,128)S(6)} %copy.10.count_ref, s32[1,1]{1,0:T(1,128)S(6)} %copy.11.send_ref, s32[1,1]{1,0:T(1,128)} %bitcast.me_ref, s32[1,48]{1,0:T(1,128)S(1)} %copy-done, s32[1,48]{1,0:T(1,128)S(1)} %copy-done.1, ...), custom_call_target="tpu_custom_call" | custom-call | flops 754974720 | bytes 5734400 | tf_op jit(solution)/shard_map/pallas_call | solution.py:156
  11.7 0.2 collective-permute-done.borrowed_ref
  11.9 0.3 shard_map.93
  12.1 1.8 %collective-permute-start.1 = (bf16[48,1280]{1,0:T(8,128)(2,1)S(1)}, bf16[48,1280]{1,0:T(8,128)(2,1)S(1)}, u32[]{:S(2)}, u32[]{:S(2)}) collective-permute-start(bf16[48,1280]{1,0:T(8,128)(2,1)S(1)} %get-tuple-element.19), channel_id=1, source_target_pairs={{0,2},{1,3},{2,4},{3,5},{4,6},{5,7},{6,0},{7,1},{8,10},{9,11},{10,... | collective-permute-start | bytes 368648 | tf_op jit(solution)/shard_map/ppermute | solution.py:276
  13.9 2.6 %collective-permute-start.3 = (bf16[24,1280]{1,0:T(8,128)(2,1)S(1)}, bf16[24,1280]{1,0:T(8,128)(2,1)S(1)}, u32[]{:S(2)}, u32[]{:S(2)}) collective-permute-start(bf16[24,1280]{1,0:T(8,128)(2,1)S(1)} %get-tuple-element.20), channel_id=1, source_target_pairs={{0,4},{1,5},{2,6},{3,7},{4,0},{5,1},{6,2},{7,3},{8,12},{9,13},{10,... | collective-permute-start | bytes 184328 | tf_op jit(solution)/shard_map/ppermute | solution.py:276
  16.5 1.3 %collective-permute-start.4 = (bf16[24,1280]{1,0:T(8,128)(2,1)S(1)}, bf16[24,1280]{1,0:T(8,128)(2,1)S(1)}, u32[]{:S(2)}, u32[]{:S(2)}) collective-permute-start(bf16[24,1280]{1,0:T(8,128)(2,1)S(1)} %get-tuple-element.21), channel_id=1, source_target_pairs={{0,6},{1,7},{2,0},{3,1},{4,2},{5,3},{6,4},{7,5},{8,14},{9,15},{10,... | collective-permute-start | bytes 184328 | tf_op jit(solution)/shard_map/ppermute | solution.py:276
  17.9 0.0 collective-permute-start.5
  17.9 2.8 %collective-permute-start.6 = (bf16[24,1280]{1,0:T(8,128)(2,1)S(1)}, bf16[24,1280]{1,0:T(8,128)(2,1)S(1)}, u32[]{:S(2)}, u32[]{:S(2)}) collective-permute-start(bf16[24,1280]{1,0:T(8,128)(2,1)S(1)} %get-tuple-element.23), channel_id=1, source_target_pairs={{0,7},{1,6},{2,1},{3,0},{4,3},{5,2},{6,5},{7,4},{8,15},{9,14},{10,... | collective-permute-start | bytes 184328 | tf_op jit(solution)/shard_map/ppermute | solution.py:276
  20.6 0.0 collective-permute-done.1.double_ref.refs_1_
  20.6 0.0 collective-permute-start.7
  20.7 0.8 %collective-permute-done.3.refs_3_ = bf16[24,1280]{1,0:T(8,128)(2,1)S(1)} collective-permute-done((bf16[24,1280]{1,0:T(8,128)(2,1)S(1)}, bf16[24,1280]{1,0:T(8,128)(2,1)S(1)}, u32[]{:S(2)}, u32[]{:S(2)}) %collective-permute-start.3) | collective-permute-done | bytes 61472 | tf_op jit(solution)/shard_map/ppermute | solution.py:276
  21.4 0.0 collective-permute-start.2
  21.4 0.2 collective-permute-done.4.refs_4_
  21.7 3.5 %collective-permute-done.5.refs_5_ = bf16[24,1280]{1,0:T(8,128)(2,1)S(1)} collective-permute-done((bf16[24,1280]{1,0:T(8,128)(2,1)S(1)}, bf16[24,1280]{1,0:T(8,128)(2,1)S(1)}, u32[]{:S(2)}, u32[]{:S(2)}) %collective-permute-start.5) | collective-permute-done | bytes 61472 | tf_op jit(solution)/shard_map/ppermute | solution.py:276
  25.2 0.0 collective-permute-done.6.refs_6_
  25.2 0.0 collective-permute-done.7.refs_7_
  25.2 0.0 collective-permute-done.2.refs_2_
  25.2 1.2 %shard_map.95 = bf16[48,5120]{1,0:T(8,128)(2,1)} custom-call(bf16[192,192]{1,0:T(8,128)(2,1)S(1)} %get-tuple-element.15.place_ref, bf16[24,1280]{1,0:T(8,128)(2,1)S(1)} %get-tuple-element.18.refs_0_, bf16[48,1280]{1,0:T(8,128)(2,1)S(1)} %collective-permute-done.1.double_ref.refs_1_, bf16[24,1280]{1,0:T(8,128)(2,1)S(1)} %collective-permute-done.2.refs_2_, ...), custom_call_target="tpu_custom_call" | custom-call | tf_op jit(solution)/shard_map/pallas_call | solution.py:292
  (1 shorter events, 0.0 us)
Async XLA Ops:
  0.0 7.3 %copy-start.1 = (s32[1,48]{1,0:T(1,128)S(1)}, s32[1,48]{1,0:T(1,128)}, u32[]{:S(2)}) copy-start(s32[1,48]{1,0:T(1,128)} %row_ref.1) | copy-start | bytes 580
  0.0 7.4 %copy-start = (s32[1,48]{1,0:T(1,128)S(1)}, s32[1,48]{1,0:T(1,128)}, u32[]{:S(2)}) copy-start(s32[1,48]{1,0:T(1,128)} %slot_ref.1) | copy-start | bytes 580
  3.7 8.1 %collective-permute-start = (bf16[64,1280]{1,0:T(8,128)(2,1)S(1)}, bf16[64,1280]{1,0:T(8,128)(2,1)S(1)}, u32[]{:S(2)}, u32[]{:S(2)}) collective-permute-start(bf16[64,1280]{1,0:T(8,128)(2,1)S(1)} %shard_map.92), channel_id=1, source_target_pairs={{24,0},{0,8},{8,16},{16,24},{25,1},{1,9},{9,17},{17,25},{26,2},{2,... | collective-permute-start | bytes 491528 | tf_op jit(solution)/shard_map/ppermute | solution.py:252
  12.1 8.5 %collective-permute-start.1 = (bf16[48,1280]{1,0:T(8,128)(2,1)S(1)}, bf16[48,1280]{1,0:T(8,128)(2,1)S(1)}, u32[]{:S(2)}, u32[]{:S(2)}) collective-permute-start(bf16[48,1280]{1,0:T(8,128)(2,1)S(1)} %get-tuple-element.19), channel_id=1, source_target_pairs={{0,2},{1,3},{2,4},{3,5},{4,6},{5,7},{6,0},{7,1},{8,10},{9,11},{10,... | collective-permute-start | bytes 368648 | tf_op jit(solution)/shard_map/ppermute | solution.py:276
  13.9 7.5 %collective-permute-start.3 = (bf16[24,1280]{1,0:T(8,128)(2,1)S(1)}, bf16[24,1280]{1,0:T(8,128)(2,1)S(1)}, u32[]{:S(2)}, u32[]{:S(2)}) collective-permute-start(bf16[24,1280]{1,0:T(8,128)(2,1)S(1)} %get-tuple-element.20), channel_id=1, source_target_pairs={{0,4},{1,5},{2,6},{3,7},{4,0},{5,1},{6,2},{7,3},{8,12},{9,13},{10,... | collective-permute-start | bytes 184328 | tf_op jit(solution)/shard_map/ppermute | solution.py:276
  16.5 5.1 %collective-permute-start.4 = (bf16[24,1280]{1,0:T(8,128)(2,1)S(1)}, bf16[24,1280]{1,0:T(8,128)(2,1)S(1)}, u32[]{:S(2)}, u32[]{:S(2)}) collective-permute-start(bf16[24,1280]{1,0:T(8,128)(2,1)S(1)} %get-tuple-element.21), channel_id=1, source_target_pairs={{0,6},{1,7},{2,0},{3,1},{4,2},{5,3},{6,4},{7,5},{8,14},{9,15},{10,... | collective-permute-start | bytes 184328 | tf_op jit(solution)/shard_map/ppermute | solution.py:276
  17.9 7.3 %collective-permute-start.5 = (bf16[24,1280]{1,0:T(8,128)(2,1)S(1)}, bf16[24,1280]{1,0:T(8,128)(2,1)S(1)}, u32[]{:S(2)}, u32[]{:S(2)}) collective-permute-start(bf16[24,1280]{1,0:T(8,128)(2,1)S(1)} %get-tuple-element.22), channel_id=1, source_target_pairs={{0,5},{1,4},{2,7},{3,6},{4,1},{5,0},{6,3},{7,2},{8,13},{9,12},{10,... | collective-permute-start | bytes 184328 | tf_op jit(solution)/shard_map/ppermute | solution.py:276
  17.9 7.3 %collective-permute-start.6 = (bf16[24,1280]{1,0:T(8,128)(2,1)S(1)}, bf16[24,1280]{1,0:T(8,128)(2,1)S(1)}, u32[]{:S(2)}, u32[]{:S(2)}) collective-permute-start(bf16[24,1280]{1,0:T(8,128)(2,1)S(1)} %get-tuple-element.23), channel_id=1, source_target_pairs={{0,7},{1,6},{2,1},{3,0},{4,3},{5,2},{6,5},{7,4},{8,15},{9,14},{10,... | collective-permute-start | bytes 184328 | tf_op jit(solution)/shard_map/ppermute | solution.py:276
  20.6 4.5 %collective-permute-start.7 = (bf16[24,1280]{1,0:T(8,128)(2,1)S(1)}, bf16[24,1280]{1,0:T(8,128)(2,1)S(1)}, u32[]{:S(2)}, u32[]{:S(2)}) collective-permute-start(bf16[24,1280]{1,0:T(8,128)(2,1)S(1)} %get-tuple-element.24), channel_id=1, source_target_pairs={{0,1},{1,0},{2,3},{3,2},{4,5},{5,4},{6,7},{7,6},{8,9},{9,8},{10,11... | collective-permute-start | bytes 184328 | tf_op jit(solution)/shard_map/ppermute | solution.py:276
  21.4 3.8 %collective-permute-start.2 = (bf16[24,1280]{1,0:T(8,128)(2,1)S(1)}, bf16[24,1280]{1,0:T(8,128)(2,1)S(1)}, u32[]{:S(2)}, u32[]{:S(2)}) collective-permute-start(bf16[24,1280]{1,0:T(8,128)(2,1)S(1)} %shard_map.94), channel_id=1, source_target_pairs={{0,1},{1,0},{2,3},{3,2},{4,5},{5,4},{6,7},{7,6},{8,9},{9,8},{10,11... | collective-permute-start | bytes 184328 | tf_op jit(solution)/shard_map/ppermute | solution.py:276

commit v14 on v12

--- a/solution.py
+++ b/solution.py
@@ -83,7 +83,7 @@
     for copy in copies[1:]:
         copy.wait()
     rows = blocks * WIN
-    squares = jnp.zeros((rows, 1), jnp.float32)
+    squares = jnp.zeros((rows, LANES), jnp.float32)
     step = 2 * LANES
     for lo in range(0, width, step):
         cols = slice(lo, lo + step)
@@ -91,8 +91,9 @@
         h = h + bias_ref[cols].astype(jnp.float32).reshape(1, step)
         h = h + resid[:, :, cols].reshape(rows, step).astype(jnp.float32)
         hidden[:, cols] = h
-        squares = squares + jnp.sum(h * h, axis=1, keepdims=True)
-    scale = lax.rsqrt(squares * (1.0 / width) + EPS)
+        h = h * h
+        squares = squares + h[:, :LANES] + h[:, LANES:]
+    scale = lax.rsqrt(jnp.sum(squares, axis=1, keepdims=True) * (1.0 / width) + EPS)
     for lo in range(0, width, step):
         cols = slice(lo, lo + step)
         gain = gain_ref[cols].astype(jnp.float32).reshape(1, step)

time: 25.6 us -> 25.6 us (level)
  no operation moved by 1% of the time
where the time goes in v14:
time: 25.6 us; the launch traced here: 25.3 us
  starting transfers between devices  11.2 us (44%)
  Pallas kernels  8.73 us (34%)
  waiting for transfers between devices  3.92 us (15%)
  between operations  1.38 us (5%)
    ppermute x7, starting transfers between devices, exchange(): lax.ppermute(part, 'seq', [(i, (i // CORES + dz) % n_z * CORES + (i + dc)...  8.25 us
    pallas_call x2, Pallas kernels, encode_call(): pl.pallas_call(kernel, out_shape=out_shape, in_specs=[smem] * len(scalars...  7.31 us
    ppermute x7, waiting for transfers between devices, exchange(): lax.ppermute(part, 'seq', [(i, (i // CORES + dz) % n_z * CORES + (i + dc)...  3.75 us
    ppermute x1, starting transfers between devices, per_device(): lax.ppermute(lent, 'enc', [((i - 1) % n_enc, i) for i in range(n_enc)])  2.99 us
    pallas_call x1, Pallas kernels, per_device(): pl.pallas_call(place_kernel, out_shape=rows_of(row_total, GROUP * width),...  1.16 us
  transfers between devices with their start and end apart: 8, of which 4 were waited for; matrix products, arithmetic and copies ran while one was open for 0% of the time, Pallas kernels for 17%

profile of v14, /device:TPU:0, one launch (start us, length us, event | category | flops | bytes accessed | tf_op | source)
XLA Modules:
  0.0 25.3 jit_solution(2419055116627044824)
XLA Ops:
  0.0 0.0 copy-start.1
  0.0 0.0 copy-start
  0.7 3.0 %shard_map.92 = bf16[64,1280]{1,0:T(8,128)(2,1)S(1)} custom-call(s32[1,1]{1,0:T(1,128)S(6)} %copy.10.count_ref, bf16[4,64,3840]{2,1,0:T(8,128)(2,1)} %qkv_hbm.3, bf16[4,64,1280]{2,1,0:T(8,128)(2,1)} %resid_hbm.3, bf16[1280,1280]{1,0:T(8,128)(2,1)} %weight_hbm.3, bf16[1280]{0:T(1024)(128)(2,1)} %bias_hbm.3, bf16[1280]{0:T(1024)(128)(2,1)} %gain_hbm.3), custom_call_target="tpu_custom_call" | custom-call | flops 251658240 | bytes 4096000 | tf_op jit(solution)/shard_map/pallas_call | solution.py:157
  3.7 3.0 %collective-permute-start = (bf16[64,1280]{1,0:T(8,128)(2,1)S(1)}, bf16[64,1280]{1,0:T(8,128)(2,1)S(1)}, u32[]{:S(2)}, u32[]{:S(2)}) collective-permute-start(bf16[64,1280]{1,0:T(8,128)(2,1)S(1)} %shard_map.92), channel_id=1, source_target_pairs={{24,0},{0,8},{8,16},{16,24},{25,1},{1,9},{9,17},{17,25},{26,2},{2,... | collective-permute-start | bytes 491528 | tf_op jit(solution)/shard_map/ppermute | solution.py:252
  7.3 0.0 copy-done.1
  7.4 0.0 copy-done
  7.4 4.3 %shard_map.91 = (bf16[192,1280]{1,0:T(8,128)(2,1)S(1)}, bf16[192,64]{1,0:T(8,128)(2,1)S(1)}, bf16[192,192]{1,0:T(8,128)(2,1)S(1)}) custom-call(s32[1,1]{1,0:T(1,128)S(6)} %copy.10.count_ref, s32[1,1]{1,0:T(1,128)S(6)} %copy.11.send_ref, s32[1,1]{1,0:T(1,128)} %bitcast.me_ref, s32[1,48]{1,0:T(1,128)S(1)} %copy-done, s32[1,48]{1,0:T(1,128)S(1)} %copy-done.1, ...), custom_call_target="tpu_custom_call" | custom-call | flops 754974720 | bytes 5734400 | tf_op jit(solution)/shard_map/pallas_call | solution.py:157
  11.7 0.2 collective-permute-done.borrowed_ref
  11.8 0.3 %shard_map.93 = (bf16[24,1280]{1,0:T(8,128)(2,1)S(1)}, bf16[48,1280]{1,0:T(8,128)(2,1)S(1)}, bf16[24,1280]{1,0:T(8,128)(2,1)S(1)}, bf16[24,1280]{1,0:T(8,128)(2,...) custom-call(bf16[192,1280]{1,0:T(8,128)(2,1)S(1)} %get-tuple-element.16.packed_ref,, ...), custom_call_target="tpu_custom_call" | custom-call | tf_op jit(solution)/shard_map/pallas_call | solution.py:264
  12.1 1.8 %collective-permute-start.1 = (bf16[48,1280]{1,0:T(8,128)(2,1)S(1)}, bf16[48,1280]{1,0:T(8,128)(2,1)S(1)}, u32[]{:S(2)}, u32[]{:S(2)}) collective-permute-start(bf16[48,1280]{1,0:T(8,128)(2,1)S(1)} %get-tuple-element.19), channel_id=1, source_target_pairs={{0,2},{1,3},{2,4},{3,5},{4,6},{5,7},{6,0},{7,1},{8,10},{9,11},{10,... | collective-permute-start | bytes 368648 | tf_op jit(solution)/shard_map/ppermute | solution.py:276
  13.9 2.6 %collective-permute-start.3 = (bf16[24,1280]{1,0:T(8,128)(2,1)S(1)}, bf16[24,1280]{1,0:T(8,128)(2,1)S(1)}, u32[]{:S(2)}, u32[]{:S(2)}) collective-permute-start(bf16[24,1280]{1,0:T(8,128)(2,1)S(1)} %get-tuple-element.20), channel_id=1, source_target_pairs={{0,4},{1,5},{2,6},{3,7},{4,0},{5,1},{6,2},{7,3},{8,12},{9,13},{10,... | collective-permute-start | bytes 184328 | tf_op jit(solution)/shard_map/ppermute | solution.py:276
  16.5 0.0 collective-permute-start.4
  16.5 1.3 %collective-permute-start.5 = (bf16[24,1280]{1,0:T(8,128)(2,1)S(1)}, bf16[24,1280]{1,0:T(8,128)(2,1)S(1)}, u32[]{:S(2)}, u32[]{:S(2)}) collective-permute-start(bf16[24,1280]{1,0:T(8,128)(2,1)S(1)} %get-tuple-element.22), channel_id=1, source_target_pairs={{0,6},{1,7},{2,0},{3,1},{4,2},{5,3},{6,4},{7,5},{8,14},{9,15},{10,... | collective-permute-start | bytes 184328 | tf_op jit(solution)/shard_map/ppermute | solution.py:276
  17.9 2.5 %collective-permute-start.6 = (bf16[24,1280]{1,0:T(8,128)(2,1)S(1)}, bf16[24,1280]{1,0:T(8,128)(2,1)S(1)}, u32[]{:S(2)}, u32[]{:S(2)}) collective-permute-start(bf16[24,1280]{1,0:T(8,128)(2,1)S(1)} %get-tuple-element.23), channel_id=1, source_target_pairs={{0,7},{1,6},{2,1},{3,0},{4,3},{5,2},{6,5},{7,4},{8,15},{9,14},{10,... | collective-permute-start | bytes 184328 | tf_op jit(solution)/shard_map/ppermute | solution.py:276
  20.4 0.0 collective-permute-done.1.double_ref.refs_1_
  20.4 0.0 collective-permute-start.7
  20.4 2.4 %collective-permute-done.3.refs_3_ = bf16[24,1280]{1,0:T(8,128)(2,1)S(1)} collective-permute-done((bf16[24,1280]{1,0:T(8,128)(2,1)S(1)}, bf16[24,1280]{1,0:T(8,128)(2,1)S(1)}, u32[]{:S(2)}, u32[]{:S(2)}) %collective-permute-start.3) | collective-permute-done | bytes 61472 | tf_op jit(solution)/shard_map/ppermute | solution.py:276
  22.8 0.0 collective-permute-start.2
  22.8 1.1 %collective-permute-done.4.refs_4_ = bf16[24,1280]{1,0:T(8,128)(2,1)S(1)} collective-permute-done((bf16[24,1280]{1,0:T(8,128)(2,1)S(1)}, bf16[24,1280]{1,0:T(8,128)(2,1)S(1)}, u32[]{:S(2)}, u32[]{:S(2)}) %collective-permute-start.4) | collective-permute-done | bytes 61472 | tf_op jit(solution)/shard_map/ppermute | solution.py:276
  23.9 0.0 collective-permute-done.5.refs_5_
  23.9 0.2 collective-permute-done.6.refs_6_
  24.1 0.0 collective-permute-done.7.refs_7_
  24.1 0.0 collective-permute-done.2.refs_2_
  24.1 1.2 %shard_map.95 = bf16[48,5120]{1,0:T(8,128)(2,1)} custom-call(bf16[192,192]{1,0:T(8,128)(2,1)S(1)} %get-tuple-element.15.place_ref, bf16[24,1280]{1,0:T(8,128)(2,1)S(1)} %get-tuple-element.18.refs_0_, bf16[48,1280]{1,0:T(8,128)(2,1)S(1)} %collective-permute-done.1.double_ref.refs_1_, bf16[24,1280]{1,0:T(8,128)(2,1)S(1)} %collective-permute-done.2.refs_2_, ...), custom_call_target="tpu_custom_call" | custom-call | tf_op jit(solution)/shard_map/pallas_call | solution.py:292
  (1 shorter events, 0.0 us)
Async XLA Ops:
  0.0 7.3 %copy-start.1 = (s32[1,48]{1,0:T(1,128)S(1)}, s32[1,48]{1,0:T(1,128)}, u32[]{:S(2)}) copy-start(s32[1,48]{1,0:T(1,128)} %row_ref.1) | copy-start | bytes 580
  0.0 7.4 %copy-start = (s32[1,48]{1,0:T(1,128)S(1)}, s32[1,48]{1,0:T(1,128)}, u32[]{:S(2)}) copy-start(s32[1,48]{1,0:T(1,128)} %slot_ref.1) | copy-start | bytes 580
  3.7 8.1 %collective-permute-start = (bf16[64,1280]{1,0:T(8,128)(2,1)S(1)}, bf16[64,1280]{1,0:T(8,128)(2,1)S(1)}, u32[]{:S(2)}, u32[]{:S(2)}) collective-permute-start(bf16[64,1280]{1,0:T(8,128)(2,1)S(1)} %shard_map.92), channel_id=1, source_target_pairs={{24,0},{0,8},{8,16},{16,24},{25,1},{1,9},{9,17},{17,25},{26,2},{2,... | collective-permute-start | bytes 491528 | tf_op jit(solution)/shard_map/ppermute | solution.py:252
  12.1 8.2 %collective-permute-start.1 = (bf16[48,1280]{1,0:T(8,128)(2,1)S(1)}, bf16[48,1280]{1,0:T(8,128)(2,1)S(1)}, u32[]{:S(2)}, u32[]{:S(2)}) collective-permute-start(bf16[48,1280]{1,0:T(8,128)(2,1)S(1)} %get-tuple-element.19), channel_id=1, source_target_pairs={{0,2},{1,3},{2,4},{3,5},{4,6},{5,7},{6,0},{7,1},{8,10},{9,11},{10,... | collective-permute-start | bytes 368648 | tf_op jit(solution)/shard_map/ppermute | solution.py:276
  13.9 8.9 %collective-permute-start.3 = (bf16[24,1280]{1,0:T(8,128)(2,1)S(1)}, bf16[24,1280]{1,0:T(8,128)(2,1)S(1)}, u32[]{:S(2)}, u32[]{:S(2)}) collective-permute-start(bf16[24,1280]{1,0:T(8,128)(2,1)S(1)} %get-tuple-element.20), channel_id=1, source_target_pairs={{0,4},{1,5},{2,6},{3,7},{4,0},{5,1},{6,2},{7,3},{8,12},{9,13},{10,... | collective-permute-start | bytes 184328 | tf_op jit(solution)/shard_map/ppermute | solution.py:276
  16.5 7.4 %collective-permute-start.4 = (bf16[24,1280]{1,0:T(8,128)(2,1)S(1)}, bf16[24,1280]{1,0:T(8,128)(2,1)S(1)}, u32[]{:S(2)}, u32[]{:S(2)}) collective-permute-start(bf16[24,1280]{1,0:T(8,128)(2,1)S(1)} %get-tuple-element.21), channel_id=1, source_target_pairs={{0,5},{1,4},{2,7},{3,6},{4,1},{5,0},{6,3},{7,2},{8,13},{9,12},{10,... | collective-permute-start | bytes 184328 | tf_op jit(solution)/shard_map/ppermute | solution.py:276
  16.5 7.4 %collective-permute-start.5 = (bf16[24,1280]{1,0:T(8,128)(2,1)S(1)}, bf16[24,1280]{1,0:T(8,128)(2,1)S(1)}, u32[]{:S(2)}, u32[]{:S(2)}) collective-permute-start(bf16[24,1280]{1,0:T(8,128)(2,1)S(1)} %get-tuple-element.22), channel_id=1, source_target_pairs={{0,6},{1,7},{2,0},{3,1},{4,2},{5,3},{6,4},{7,5},{8,14},{9,15},{10,... | collective-permute-start | bytes 184328 | tf_op jit(solution)/shard_map/ppermute | solution.py:276
  17.9 6.2 %collective-permute-start.6 = (bf16[24,1280]{1,0:T(8,128)(2,1)S(1)}, bf16[24,1280]{1,0:T(8,128)(2,1)S(1)}, u32[]{:S(2)}, u32[]{:S(2)}) collective-permute-start(bf16[24,1280]{1,0:T(8,128)(2,1)S(1)} %get-tuple-element.23), channel_id=1, source_target_pairs={{0,7},{1,6},{2,1},{3,0},{4,3},{5,2},{6,5},{7,4},{8,15},{9,14},{10,... | collective-permute-start | bytes 184328 | tf_op jit(solution)/shard_map/ppermute | solution.py:276
  20.4 3.8 %collective-permute-start.7 = (bf16[24,1280]{1,0:T(8,128)(2,1)S(1)}, bf16[24,1280]{1,0:T(8,128)(2,1)S(1)}, u32[]{:S(2)}, u32[]{:S(2)}) collective-permute-start(bf16[24,1280]{1,0:T(8,128)(2,1)S(1)} %get-tuple-element.24), channel_id=1, source_target_pairs={{0,1},{1,0},{2,3},{3,2},{4,5},{5,4},{6,7},{7,6},{8,9},{9,8},{10,11... | collective-permute-start | bytes 184328 | tf_op jit(solution)/shard_map/ppermute | solution.py:276
  22.8 1.3 %collective-permute-start.2 = (bf16[24,1280]{1,0:T(8,128)(2,1)S(1)}, bf16[24,1280]{1,0:T(8,128)(2,1)S(1)}, u32[]{:S(2)}, u32[]{:S(2)}) collective-permute-start(bf16[24,1280]{1,0:T(8,128)(2,1)S(1)} %shard_map.94), channel_id=1, source_target_pairs={{0,1},{1,0},{2,3},{3,2},{4,5},{5,4},{6,7},{7,6},{8,9},{9,8},{10,11... | collective-permute-start | bytes 184328 | tf_op jit(solution)/shard_map/ppermute | solution.py:276

commit v15 on v14

--- a/solution.py
+++ b/solution.py
@@ -28,7 +28,7 @@
 
 def attend(q, k, v, out_ref, row0, width):
     head = width // HEADS
-    rate = 1.0 / math.sqrt(head)
+    rate = math.log2(math.e) / math.sqrt(head)
     totals = [None] * (width // LANES)
     sums = [None] * (width // LANES)
     first_half = lax.broadcasted_iota(jnp.int32, (WIN, 2 * WIN), 1) < WIN
@@ -46,7 +46,7 @@
         scores = lax.dot_general(q(lo, hi), keys, NT, preferred_element_type=jnp.float32)
         top0 = jnp.max(jnp.where(first_half, scores, -jnp.inf), axis=1, keepdims=True)
         top1 = jnp.max(jnp.where(first_half, -jnp.inf, scores), axis=1, keepdims=True)
-        raised = jnp.exp((scores - jnp.where(first_half, top0, top1)) * rate).astype(jnp.bfloat16)
+        raised = jnp.exp2((scores - jnp.where(first_half, top0, top1)) * rate).astype(jnp.bfloat16)
         part = dot32(raised, values)
         norm = dot32(raised, mask)
         for tile in range(lo // LANES, hi // LANES):

time: 25.6 us -> 25.6 us (level)
  no operation moved by 1% of the time
where the time goes in v15:
time: 25.6 us; the launch traced here: 25.3 us
  starting transfers between devices  11.2 us (44%)
  Pallas kernels  8.73 us (34%)
  waiting for transfers between devices  3.91 us (15%)
  between operations  1.38 us (5%)
    ppermute x7, starting transfers between devices, exchange(): lax.ppermute(part, 'seq', [(i, (i // CORES + dz) % n_z * CORES + (i + dc)...  8.25 us
    pallas_call x2, Pallas kernels, encode_call(): pl.pallas_call(kernel, out_shape=out_shape, in_specs=[smem] * len(scalars...  7.31 us
    ppermute x7, waiting for transfers between devices, exchange(): lax.ppermute(part, 'seq', [(i, (i // CORES + dz) % n_z * CORES + (i + dc)...  3.75 us
    ppermute x1, starting transfers between devices, per_device(): lax.ppermute(lent, 'enc', [((i - 1) % n_enc, i) for i in range(n_enc)])  2.99 us
    pallas_call x1, Pallas kernels, per_device(): pl.pallas_call(place_kernel, out_shape=rows_of(row_total, GROUP * width),...  1.16 us
  transfers between devices with their start and end apart: 8, of which 4 were waited for; matrix products, arithmetic and copies ran while one was open for 0% of the time, Pallas kernels for 17%

profile of v15, /device:TPU:0, one launch (start us, length us, event | category | flops | bytes accessed | tf_op | source)
XLA Modules:
  0.0 25.3 jit_solution(5295757981376435830)
XLA Ops:
  0.0 0.0 copy-start.1
  0.0 0.0 copy-start
  0.7 3.0 %shard_map.92 = bf16[64,1280]{1,0:T(8,128)(2,1)S(1)} custom-call(s32[1,1]{1,0:T(1,128)S(6)} %copy.10.count_ref, bf16[4,64,3840]{2,1,0:T(8,128)(2,1)} %qkv_hbm.3, bf16[4,64,1280]{2,1,0:T(8,128)(2,1)} %resid_hbm.3, bf16[1280,1280]{1,0:T(8,128)(2,1)} %weight_hbm.3, bf16[1280]{0:T(1024)(128)(2,1)} %bias_hbm.3, bf16[1280]{0:T(1024)(128)(2,1)} %gain_hbm.3), custom_call_target="tpu_custom_call" | custom-call | flops 251658240 | bytes 4096000 | tf_op jit(solution)/shard_map/pallas_call | solution.py:157
  3.7 3.0 %collective-permute-start = (bf16[64,1280]{1,0:T(8,128)(2,1)S(1)}, bf16[64,1280]{1,0:T(8,128)(2,1)S(1)}, u32[]{:S(2)}, u32[]{:S(2)}) collective-permute-start(bf16[64,1280]{1,0:T(8,128)(2,1)S(1)} %shard_map.92), channel_id=1, source_target_pairs={{24,0},{0,8},{8,16},{16,24},{25,1},{1,9},{9,17},{17,25},{26,2},{2,... | collective-permute-start | bytes 491528 | tf_op jit(solution)/shard_map/ppermute | solution.py:252
  7.3 0.0 copy-done.1
  7.4 0.0 copy-done
  7.4 4.3 %shard_map.91 = (bf16[192,1280]{1,0:T(8,128)(2,1)S(1)}, bf16[192,64]{1,0:T(8,128)(2,1)S(1)}, bf16[192,192]{1,0:T(8,128)(2,1)S(1)}) custom-call(s32[1,1]{1,0:T(1,128)S(6)} %copy.10.count_ref, s32[1,1]{1,0:T(1,128)S(6)} %copy.11.send_ref, s32[1,1]{1,0:T(1,128)} %bitcast.me_ref, s32[1,48]{1,0:T(1,128)S(1)} %copy-done, s32[1,48]{1,0:T(1,128)S(1)} %copy-done.1, ...), custom_call_target="tpu_custom_call" | custom-call | flops 754974720 | bytes 5734400 | tf_op jit(solution)/shard_map/pallas_call | solution.py:157
  11.7 0.2 collective-permute-done.borrowed_ref
  11.8 0.3 %shard_map.93 = (bf16[24,1280]{1,0:T(8,128)(2,1)S(1)}, bf16[48,1280]{1,0:T(8,128)(2,1)S(1)}, bf16[24,1280]{1,0:T(8,128)(2,1)S(1)}, bf16[24,1280]{1,0:T(8,128)(2,...) custom-call(bf16[192,1280]{1,0:T(8,128)(2,1)S(1)} %get-tuple-element.16.packed_ref,, ...), custom_call_target="tpu_custom_call" | custom-call | tf_op jit(solution)/shard_map/pallas_call | solution.py:264
  12.1 1.8 %collective-permute-start.1 = (bf16[48,1280]{1,0:T(8,128)(2,1)S(1)}, bf16[48,1280]{1,0:T(8,128)(2,1)S(1)}, u32[]{:S(2)}, u32[]{:S(2)}) collective-permute-start(bf16[48,1280]{1,0:T(8,128)(2,1)S(1)} %get-tuple-element.19), channel_id=1, source_target_pairs={{0,2},{1,3},{2,4},{3,5},{4,6},{5,7},{6,0},{7,1},{8,10},{9,11},{10,... | collective-permute-start | bytes 368648 | tf_op jit(solution)/shard_map/ppermute | solution.py:276
  13.9 2.6 %collective-permute-start.3 = (bf16[24,1280]{1,0:T(8,128)(2,1)S(1)}, bf16[24,1280]{1,0:T(8,128)(2,1)S(1)}, u32[]{:S(2)}, u32[]{:S(2)}) collective-permute-start(bf16[24,1280]{1,0:T(8,128)(2,1)S(1)} %get-tuple-element.20), channel_id=1, source_target_pairs={{0,4},{1,5},{2,6},{3,7},{4,0},{5,1},{6,2},{7,3},{8,12},{9,13},{10,... | collective-permute-start | bytes 184328 | tf_op jit(solution)/shard_map/ppermute | solution.py:276
  16.5 0.0 collective-permute-start.4
  16.5 1.3 %collective-permute-start.5 = (bf16[24,1280]{1,0:T(8,128)(2,1)S(1)}, bf16[24,1280]{1,0:T(8,128)(2,1)S(1)}, u32[]{:S(2)}, u32[]{:S(2)}) collective-permute-start(bf16[24,1280]{1,0:T(8,128)(2,1)S(1)} %get-tuple-element.22), channel_id=1, source_target_pairs={{0,6},{1,7},{2,0},{3,1},{4,2},{5,3},{6,4},{7,5},{8,14},{9,15},{10,... | collective-permute-start | bytes 184328 | tf_op jit(solution)/shard_map/ppermute | solution.py:276
  17.9 2.5 %collective-permute-start.6 = (bf16[24,1280]{1,0:T(8,128)(2,1)S(1)}, bf16[24,1280]{1,0:T(8,128)(2,1)S(1)}, u32[]{:S(2)}, u32[]{:S(2)}) collective-permute-start(bf16[24,1280]{1,0:T(8,128)(2,1)S(1)} %get-tuple-element.23), channel_id=1, source_target_pairs={{0,7},{1,6},{2,1},{3,0},{4,3},{5,2},{6,5},{7,4},{8,15},{9,14},{10,... | collective-permute-start | bytes 184328 | tf_op jit(solution)/shard_map/ppermute | solution.py:276
  20.4 0.0 collective-permute-done.1.double_ref.refs_1_
  20.4 0.0 collective-permute-start.7
  20.4 2.4 %collective-permute-done.3.refs_3_ = bf16[24,1280]{1,0:T(8,128)(2,1)S(1)} collective-permute-done((bf16[24,1280]{1,0:T(8,128)(2,1)S(1)}, bf16[24,1280]{1,0:T(8,128)(2,1)S(1)}, u32[]{:S(2)}, u32[]{:S(2)}) %collective-permute-start.3) | collective-permute-done | bytes 61472 | tf_op jit(solution)/shard_map/ppermute | solution.py:276
  22.8 0.0 collective-permute-start.2
  22.8 1.1 %collective-permute-done.4.refs_4_ = bf16[24,1280]{1,0:T(8,128)(2,1)S(1)} collective-permute-done((bf16[24,1280]{1,0:T(8,128)(2,1)S(1)}, bf16[24,1280]{1,0:T(8,128)(2,1)S(1)}, u32[]{:S(2)}, u32[]{:S(2)}) %collective-permute-start.4) | collective-permute-done | bytes 61472 | tf_op jit(solution)/shard_map/ppermute | solution.py:276
  23.9 0.0 collective-permute-done.5.refs_5_
  23.9 0.2 collective-permute-done.6.refs_6_
  24.1 0.0 collective-permute-done.7.refs_7_
  24.1 0.0 collective-permute-done.2.refs_2_
  24.1 1.2 %shard_map.95 = bf16[48,5120]{1,0:T(8,128)(2,1)} custom-call(bf16[192,192]{1,0:T(8,128)(2,1)S(1)} %get-tuple-element.15.place_ref, bf16[24,1280]{1,0:T(8,128)(2,1)S(1)} %get-tuple-element.18.refs_0_, bf16[48,1280]{1,0:T(8,128)(2,1)S(1)} %collective-permute-done.1.double_ref.refs_1_, bf16[24,1280]{1,0:T(8,128)(2,1)S(1)} %collective-permute-done.2.refs_2_, ...), custom_call_target="tpu_custom_call" | custom-call | tf_op jit(solution)/shard_map/pallas_call | solution.py:292
  (1 shorter events, 0.0 us)
Async XLA Ops:
  0.0 7.3 %copy-start.1 = (s32[1,48]{1,0:T(1,128)S(1)}, s32[1,48]{1,0:T(1,128)}, u32[]{:S(2)}) copy-start(s32[1,48]{1,0:T(1,128)} %row_ref.1) | copy-start | bytes 580
  0.0 7.4 %copy-start = (s32[1,48]{1,0:T(1,128)S(1)}, s32[1,48]{1,0:T(1,128)}, u32[]{:S(2)}) copy-start(s32[1,48]{1,0:T(1,128)} %slot_ref.1) | copy-start | bytes 580
  3.7 8.1 %collective-permute-start = (bf16[64,1280]{1,0:T(8,128)(2,1)S(1)}, bf16[64,1280]{1,0:T(8,128)(2,1)S(1)}, u32[]{:S(2)}, u32[]{:S(2)}) collective-permute-start(bf16[64,1280]{1,0:T(8,128)(2,1)S(1)} %shard_map.92), channel_id=1, source_target_pairs={{24,0},{0,8},{8,16},{16,24},{25,1},{1,9},{9,17},{17,25},{26,2},{2,... | collective-permute-start | bytes 491528 | tf_op jit(solution)/shard_map/ppermute | solution.py:252
  12.1 8.2 %collective-permute-start.1 = (bf16[48,1280]{1,0:T(8,128)(2,1)S(1)}, bf16[48,1280]{1,0:T(8,128)(2,1)S(1)}, u32[]{:S(2)}, u32[]{:S(2)}) collective-permute-start(bf16[48,1280]{1,0:T(8,128)(2,1)S(1)} %get-tuple-element.19), channel_id=1, source_target_pairs={{0,2},{1,3},{2,4},{3,5},{4,6},{5,7},{6,0},{7,1},{8,10},{9,11},{10,... | collective-permute-start | bytes 368648 | tf_op jit(solution)/shard_map/ppermute | solution.py:276
  13.9 8.9 %collective-permute-start.3 = (bf16[24,1280]{1,0:T(8,128)(2,1)S(1)}, bf16[24,1280]{1,0:T(8,128)(2,1)S(1)}, u32[]{:S(2)}, u32[]{:S(2)}) collective-permute-start(bf16[24,1280]{1,0:T(8,128)(2,1)S(1)} %get-tuple-element.20), channel_id=1, source_target_pairs={{0,4},{1,5},{2,6},{3,7},{4,0},{5,1},{6,2},{7,3},{8,12},{9,13},{10,... | collective-permute-start | bytes 184328 | tf_op jit(solution)/shard_map/ppermute | solution.py:276
  16.5 7.4 %collective-permute-start.4 = (bf16[24,1280]{1,0:T(8,128)(2,1)S(1)}, bf16[24,1280]{1,0:T(8,128)(2,1)S(1)}, u32[]{:S(2)}, u32[]{:S(2)}) collective-permute-start(bf16[24,1280]{1,0:T(8,128)(2,1)S(1)} %get-tuple-element.21), channel_id=1, source_target_pairs={{0,5},{1,4},{2,7},{3,6},{4,1},{5,0},{6,3},{7,2},{8,13},{9,12},{10,... | collective-permute-start | bytes 184328 | tf_op jit(solution)/shard_map/ppermute | solution.py:276
  16.5 7.4 %collective-permute-start.5 = (bf16[24,1280]{1,0:T(8,128)(2,1)S(1)}, bf16[24,1280]{1,0:T(8,128)(2,1)S(1)}, u32[]{:S(2)}, u32[]{:S(2)}) collective-permute-start(bf16[24,1280]{1,0:T(8,128)(2,1)S(1)} %get-tuple-element.22), channel_id=1, source_target_pairs={{0,6},{1,7},{2,0},{3,1},{4,2},{5,3},{6,4},{7,5},{8,14},{9,15},{10,... | collective-permute-start | bytes 184328 | tf_op jit(solution)/shard_map/ppermute | solution.py:276
  17.9 6.2 %collective-permute-start.6 = (bf16[24,1280]{1,0:T(8,128)(2,1)S(1)}, bf16[24,1280]{1,0:T(8,128)(2,1)S(1)}, u32[]{:S(2)}, u32[]{:S(2)}) collective-permute-start(bf16[24,1280]{1,0:T(8,128)(2,1)S(1)} %get-tuple-element.23), channel_id=1, source_target_pairs={{0,7},{1,6},{2,1},{3,0},{4,3},{5,2},{6,5},{7,4},{8,15},{9,14},{10,... | collective-permute-start | bytes 184328 | tf_op jit(solution)/shard_map/ppermute | solution.py:276
  20.4 3.8 %collective-permute-start.7 = (bf16[24,1280]{1,0:T(8,128)(2,1)S(1)}, bf16[24,1280]{1,0:T(8,128)(2,1)S(1)}, u32[]{:S(2)}, u32[]{:S(2)}) collective-permute-start(bf16[24,1280]{1,0:T(8,128)(2,1)S(1)} %get-tuple-element.24), channel_id=1, source_target_pairs={{0,1},{1,0},{2,3},{3,2},{4,5},{5,4},{6,7},{7,6},{8,9},{9,8},{10,11... | collective-permute-start | bytes 184328 | tf_op jit(solution)/shard_map/ppermute | solution.py:276
  22.8 1.3 %collective-permute-start.2 = (bf16[24,1280]{1,0:T(8,128)(2,1)S(1)}, bf16[24,1280]{1,0:T(8,128)(2,1)S(1)}, u32[]{:S(2)}, u32[]{:S(2)}) collective-permute-start(bf16[24,1280]{1,0:T(8,128)(2,1)S(1)} %shard_map.94), channel_id=1, source_target_pairs={{0,1},{1,0},{2,3},{3,2},{4,5},{5,4},{6,7},{7,6},{8,9},{9,8},{10,11... | collective-permute-start | bytes 184328 | tf_op jit(solution)/shard_map/ppermute | solution.py:276
